TPU v7x, 32 devices: a whole 2x2x4 slice. The times are simulated.
32 devices in a mesh: dp: 4 (over y, x), row: 2 (over core), col: 4 (over z).
Axes of the slice: x: 2, y: 2, z: 4, core: 2. Of those that a mesh axis runs over, the one named last changes fastest.
Arguments:
- layer_input: bfloat16 [4096, 2048], P(('dp', 'row'), 'col'), may hold values from -6 to 6
- doc_ids: int32 [4096], P('dp'), may hold values from 0 to 3, as said below
- positions: int32 [4096], P('dp'), may hold values from 0 to 1023, as said below
- w_query: bfloat16 [2048, 2048], P('col', 'row'), may hold values from -0.125 to 0.125
- w_key: bfloat16 [2048, 2048], P('col', 'row'), may hold values from -0.125 to 0.125
- w_value: bfloat16 [2048, 2048], P('col', 'row'), may hold values from -0.125 to 0.125
- w_out: bfloat16 [2048, 2048], P('row', 'col'), may hold values from -0.125 to 0.125
- w_gate: bfloat16 [2048, 8192], P('col', 'row'), may hold values from -0.125 to 0.125
- w_up: bfloat16 [2048, 8192], P('col', 'row'), may hold values from -0.125 to 0.125
- w_down: bfloat16 [8192, 2048], P('row', 'col'), may hold values from -0.0625 to 0.0625
- gain_query: float32 [2048], P(('row', 'col')), may hold values from 0.1 to 1.9
- gain_key: float32 [2048], P(('row', 'col')), may hold values from 0.1 to 1.9
- gain_attn: float32 [2048], P('col'), may hold values from 0.1 to 1.9
- gain_ffn: float32 [2048], P('col'), may hold values from 0.1 to 1.9
- grad_output: bfloat16 [4096, 2048], P(('dp', 'row'), 'col'), may hold values from -6 to 6
Outputs:
- layer_output: bfloat16 [4096, 2048], P(('dp', 'row'), 'col')
- grad_input: float32 [4096, 2048], P(('dp', 'row'), 'col')
- grad_w_query: float32 [2048, 2048], P('col', 'row')
- grad_w_key: float32 [2048, 2048], P('col', 'row')
- grad_w_value: float32 [2048, 2048], P('col', 'row')
- grad_w_out: float32 [2048, 2048], P('row', 'col')
- grad_w_gate: float32 [2048, 8192], P('col', 'row')
- grad_w_up: float32 [2048, 8192], P('col', 'row')
- grad_w_down: float32 [8192, 2048], P('row', 'col')
- grad_gain_query: float32 [2048], P(('row', 'col'))
- grad_gain_key: float32 [2048], P(('row', 'col'))
- grad_gain_attn: float32 [2048], P('col')
- grad_gain_ffn: float32 [2048], P('col')
Inputs may be any that keep to these rules, and one draw needn't show every extreme that they name: `doc_ids`: within each group of 1024 consecutive slots the number never falls from slot to slot; a group holds 1 to 4 sequences, and in some group a single sequence fills all 1024 slots. `positions`: each sequence starts at position 0 and the position rises by one from slot to slot within it.
All inputs are finite; a program needn't handle non-finite values.
Results may differ from a plain program's by a relative error of at most 0.019.
Values may be sent and summed in bfloat16 or wider, within the bound.
No kernel may reach another device: no remote copies, remote signals or barrier semaphores. Data moves between devices by JAX's collectives and lax.ppermute only.
A program may use at most 192 MiB of HBM per device.

v0:
```python
import jax
import jax.numpy as jnp
from jax import lax
from jax.sharding import PartitionSpec as P

D = 2048
HEAD = 128


EPSILON = 1e-06
ROPE_BASE = 500000.0
MASKED = -1e30


def rope_tables(positions):
    frequency = ROPE_BASE ** (-(jnp.arange(HEAD // 2, dtype=jnp.float32) * (2.0 / HEAD)))
    angles = positions.astype(jnp.float32)[:, None] * frequency[None, :]
    return (jnp.cos(angles)[:, None, :], jnp.sin(angles)[:, None, :])


def rotate(values, cosine_table, sine_table):
    middle = values.shape[-1] // 2
    first_half = values[..., :middle]
    second_half = values[..., middle:]
    return jnp.concatenate(
        [
            first_half * cosine_table - second_half * sine_table,
            second_half * cosine_table + first_half * sine_table,
        ],
        axis=-1,
    )


def unrotate(values, cosine_table, sine_table):
    middle = values.shape[-1] // 2
    first_half = values[..., :middle]
    second_half = values[..., middle:]
    return jnp.concatenate(
        [
            first_half * cosine_table + second_half * sine_table,
            second_half * cosine_table - first_half * sine_table,
        ],
        axis=-1,
    )


def rows_gather(values):
    return lax.all_gather(values, "row", axis=0, tiled=True)


def rows_sum(values):
    return lax.psum_scatter(values, "row", scatter_dimension=0, tiled=True)


def columns_gather(values):
    return lax.all_gather(values, "col", axis=1, tiled=True)


def columns_sum(values):
    return lax.psum_scatter(values, "col", scatter_dimension=1, tiled=True)


def feature_norm(values):
    return lax.psum(values, "col")


def head_norms(first_terms, second_terms):
    return lax.psum((first_terms, second_terms), ("row", "col"))


def post_norm(branch, gains):
    square_sum = feature_norm(jnp.sum(branch * branch, axis=1))
    scales = lax.rsqrt(square_sum / D + EPSILON)[:, None]
    return (branch * scales * gains, scales)


def post_norm_back(grad_normed, branch, scales, gains):
    weighted = grad_normed * gains
    inner_sum = feature_norm(jnp.sum(weighted * branch, axis=1))[:, None]
    grad_branch = scales * weighted - branch * (scales * scales * scales) * inner_sum / D
    grad_gains = jnp.sum(grad_normed * branch * scales, axis=0)
    return (grad_branch, grad_gains)


def allowed_block(doc_ids, first_row, block_rows):
    length_all = doc_ids.shape[0]
    rows_here = first_row + jnp.arange(block_rows)
    docs_here = lax.dynamic_slice_in_dim(doc_ids, first_row, block_rows)
    return (docs_here[:, None] == doc_ids[None, :]) & (
        jnp.arange(length_all)[None, :] <= rows_here[:, None]
    )


def attend_forward(queries, keys_rot, values_low, doc_ids, block_rows):
    starts = jnp.arange(queries.shape[0] // block_rows) * block_rows
    factor = HEAD ** (-0.5)

    def one_block(first_row):
        query_block = lax.dynamic_slice_in_dim(queries, first_row, block_rows, 0)
        scores = (
            jnp.einsum("qhd,khd->hqk", query_block, keys_rot, preferred_element_type=jnp.float32)
            * factor
        )
        scores = jnp.where(allowed_block(doc_ids, first_row, block_rows)[None], scores, MASKED)
        largest = jnp.max(scores, axis=-1, keepdims=True)
        weights = jnp.exp(scores - largest)
        totals = jnp.sum(weights, axis=-1, keepdims=True)
        chances = (weights / totals).astype(jnp.bfloat16)
        mixture = jnp.einsum(
            "hqk,khd->qhd", chances, values_low, preferred_element_type=jnp.float32
        )
        return (mixture, largest[..., 0] + jnp.log(totals[..., 0]))

    return lax.map(one_block, starts)


def attend_backward(queries, keys_rot, values_low, grad_mixture, log_totals, doc_ids, block_rows):
    starts = jnp.arange(queries.shape[0] // block_rows) * block_rows
    factor = HEAD ** (-0.5)

    def one_block(carry, inputs):
        grad_keys, grad_values = carry
        first_row, log_block = inputs
        query_block = lax.dynamic_slice_in_dim(queries, first_row, block_rows, 0)
        grad_block = lax.dynamic_slice_in_dim(grad_mixture, first_row, block_rows, 0)
        scores = (
            jnp.einsum("qhd,khd->hqk", query_block, keys_rot, preferred_element_type=jnp.float32)
            * factor
        )
        scores = jnp.where(allowed_block(doc_ids, first_row, block_rows)[None], scores, MASKED)
        chances = jnp.exp(scores - log_block[..., None])
        chances_low = chances.astype(jnp.bfloat16)
        grad_values = grad_values + jnp.einsum(
            "hqk,qhd->khd", chances_low, grad_block, preferred_element_type=jnp.float32
        )
        grad_chances = jnp.einsum(
            "qhd,khd->hqk", grad_block, values_low, preferred_element_type=jnp.float32
        )
        inner_sum = jnp.sum(chances * grad_chances, axis=-1, keepdims=True)
        grad_scores = (chances * (grad_chances - inner_sum)).astype(jnp.bfloat16)
        grad_query = (
            jnp.einsum("hqk,khd->qhd", grad_scores, keys_rot, preferred_element_type=jnp.float32)
            * factor
        )
        grad_keys = (
            grad_keys
            + jnp.einsum(
                "hqk,qhd->khd", grad_scores, query_block, preferred_element_type=jnp.float32
            )
            * factor
        )
        return ((grad_keys, grad_values), grad_query)

    zeros_start = jnp.zeros(keys_rot.shape, jnp.float32)
    carried, grad_queries = lax.scan(one_block, (zeros_start, zeros_start), (starts, log_totals))
    return (grad_queries.reshape(queries.shape), carried[0], carried[1])


def per_device(
    layer_input,
    doc_ids,
    positions,
    w_query,
    w_key,
    w_value,
    w_out,
    w_gate,
    w_up,
    w_down,
    gain_query,
    gain_key,
    gain_attn,
    gain_ffn,
    grad_output,
):
    input_rows = rows_gather(layer_input)
    query_part = jnp.dot(input_rows, w_query, preferred_element_type=jnp.float32)
    key_part = jnp.dot(input_rows, w_key, preferred_element_type=jnp.float32)
    value_part = jnp.dot(input_rows, w_value, preferred_element_type=jnp.float32)
    query_raw, key_raw, value_raw = (
        lax.psum_scatter(query_part, "col", scatter_dimension=1, tiled=True),
        lax.psum_scatter(key_part, "col", scatter_dimension=1, tiled=True),
        lax.psum_scatter(value_part, "col", scatter_dimension=1, tiled=True),
    )
    length_all = query_raw.shape[0]
    local_width = query_raw.shape[1]
    local_heads = local_width // HEAD
    block_rows = min(512, length_all)
    heads_shape = (length_all, local_heads, HEAD)
    query_square, key_square = head_norms(
        jnp.sum(query_raw * query_raw, axis=1), jnp.sum(key_raw * key_raw, axis=1)
    )
    query_scale = lax.rsqrt(query_square / D + EPSILON)[:, None]
    key_scale = lax.rsqrt(key_square / D + EPSILON)[:, None]
    cosine_table, sine_table = rope_tables(positions)
    query_rot = rotate(
        (query_raw * query_scale * gain_query).reshape(heads_shape), cosine_table, sine_table
    ).astype(jnp.bfloat16)
    key_rot = rotate(
        (key_raw * key_scale * gain_key).reshape(heads_shape), cosine_table, sine_table
    ).astype(jnp.bfloat16)
    value_low = value_raw.astype(jnp.bfloat16).reshape(heads_shape)
    mixture_blocks, log_totals = attend_forward(query_rot, key_rot, value_low, doc_ids, block_rows)
    mixture = mixture_blocks.reshape(length_all, local_width).astype(jnp.bfloat16)
    mixture_cols = columns_gather(mixture)
    attended = rows_sum(jnp.dot(mixture_cols, w_out, preferred_element_type=jnp.float32))
    attn_normed, attn_scale = post_norm(attended, gain_attn)
    hidden_state = layer_input.astype(jnp.float32) + attn_normed
    state_rows = rows_gather(hidden_state.astype(jnp.bfloat16))
    gate_values, up_values = (
        lax.psum_scatter(
            jnp.dot(state_rows, w_gate, preferred_element_type=jnp.float32),
            "col",
            scatter_dimension=1,
            tiled=True,
        ),
        lax.psum_scatter(
            jnp.dot(state_rows, w_up, preferred_element_type=jnp.float32),
            "col",
            scatter_dimension=1,
            tiled=True,
        ),
    )
    sigmoid_gate = jax.nn.sigmoid(gate_values)
    silu_gate = gate_values * sigmoid_gate
    activated = (silu_gate * up_values).astype(jnp.bfloat16)
    activated_cols = columns_gather(activated)
    lowered = rows_sum(jnp.dot(activated_cols, w_down, preferred_element_type=jnp.float32))
    ffn_normed, ffn_scale = post_norm(lowered, gain_ffn)
    layer_output = (hidden_state + ffn_normed).astype(jnp.bfloat16)
    cotangent = grad_output.astype(jnp.float32)
    grad_lowered, grad_gain_ffn = post_norm_back(cotangent, lowered, ffn_scale, gain_ffn)
    lowered_rows = rows_gather(grad_lowered.astype(jnp.bfloat16))
    grad_w_down = jnp.einsum(
        "tf,tc->fc", activated_cols, lowered_rows, preferred_element_type=jnp.float32
    )
    grad_activated = columns_sum(
        jnp.einsum("tc,fc->tf", lowered_rows, w_down, preferred_element_type=jnp.float32)
    )
    grad_gate = (
        grad_activated * up_values * (sigmoid_gate * (1.0 + gate_values * (1.0 - sigmoid_gate)))
    )
    grad_up = grad_activated * silu_gate
    gate_grad_cols, up_grad_cols = (
        lax.all_gather(grad_gate.astype(jnp.bfloat16), "col", axis=1, tiled=True),
        lax.all_gather(grad_up.astype(jnp.bfloat16), "col", axis=1, tiled=True),
    )
    grad_w_gate = jnp.einsum(
        "tc,tf->cf", state_rows, gate_grad_cols, preferred_element_type=jnp.float32
    )
    grad_w_up = jnp.einsum(
        "tc,tf->cf", state_rows, up_grad_cols, preferred_element_type=jnp.float32
    )
    state_part = jnp.einsum(
        "tf,cf->tc", gate_grad_cols, w_gate, preferred_element_type=jnp.float32
    ) + jnp.einsum("tf,cf->tc", up_grad_cols, w_up, preferred_element_type=jnp.float32)
    grad_state = cotangent + rows_sum(state_part)
    grad_attended, grad_gain_attn = post_norm_back(grad_state, attended, attn_scale, gain_attn)
    attended_rows = rows_gather(grad_attended.astype(jnp.bfloat16))
    grad_w_out = jnp.einsum(
        "tk,tc->kc", mixture_cols, attended_rows, preferred_element_type=jnp.float32
    )
    grad_mixture = columns_sum(
        jnp.einsum("tc,kc->tk", attended_rows, w_out, preferred_element_type=jnp.float32)
    )
    grad_mixture = grad_mixture.astype(jnp.bfloat16).reshape(heads_shape)
    grad_qrot, grad_krot, grad_value = attend_backward(
        query_rot, key_rot, value_low, grad_mixture, log_totals, doc_ids, block_rows
    )
    grad_qnormed = unrotate(grad_qrot, cosine_table, sine_table).reshape(length_all, local_width)
    grad_knormed = unrotate(grad_krot, cosine_table, sine_table).reshape(length_all, local_width)
    grad_gain_query = jnp.sum(grad_qnormed * query_raw * query_scale, axis=0)
    grad_gain_key = jnp.sum(grad_knormed * key_raw * key_scale, axis=0)
    query_weighted = grad_qnormed * gain_query
    key_weighted = grad_knormed * gain_key
    query_inner, key_inner = head_norms(
        jnp.sum(query_weighted * query_raw, axis=1), jnp.sum(key_weighted * key_raw, axis=1)
    )
    grad_query = (
        query_scale * query_weighted
        - query_raw * (query_scale * query_scale * query_scale) * query_inner[:, None] / D
    )
    grad_key = (
        key_scale * key_weighted
        - key_raw * (key_scale * key_scale * key_scale) * key_inner[:, None] / D
    )
    query_grad_cols, key_grad_cols, value_grad_cols = (
        lax.all_gather(grad_query.astype(jnp.bfloat16), "col", axis=1, tiled=True),
        lax.all_gather(grad_key.astype(jnp.bfloat16), "col", axis=1, tiled=True),
        lax.all_gather(
            grad_value.reshape(length_all, local_width).astype(jnp.bfloat16),
            "col",
            axis=1,
            tiled=True,
        ),
    )
    grad_w_query = jnp.einsum(
        "tc,tk->ck", input_rows, query_grad_cols, preferred_element_type=jnp.float32
    )
    grad_w_key = jnp.einsum(
        "tc,tk->ck", input_rows, key_grad_cols, preferred_element_type=jnp.float32
    )
    grad_w_value = jnp.einsum(
        "tc,tk->ck", input_rows, value_grad_cols, preferred_element_type=jnp.float32
    )
    input_part = (
        jnp.einsum("tk,ck->tc", query_grad_cols, w_query, preferred_element_type=jnp.float32)
        + jnp.einsum("tk,ck->tc", key_grad_cols, w_key, preferred_element_type=jnp.float32)
        + jnp.einsum("tk,ck->tc", value_grad_cols, w_value, preferred_element_type=jnp.float32)
    )
    grad_input = grad_state + rows_sum(input_part)
    summed = (
        lax.psum(grad_w_query.astype(jnp.bfloat16), "dp").astype(jnp.float32),
        lax.psum(grad_w_key.astype(jnp.bfloat16), "dp").astype(jnp.float32),
        lax.psum(grad_w_value.astype(jnp.bfloat16), "dp").astype(jnp.float32),
        lax.psum(grad_w_out.astype(jnp.bfloat16), "dp").astype(jnp.float32),
        lax.psum(grad_w_gate.astype(jnp.bfloat16), "dp").astype(jnp.float32),
        lax.psum(grad_w_up.astype(jnp.bfloat16), "dp").astype(jnp.float32),
        lax.psum(grad_w_down.astype(jnp.bfloat16), "dp").astype(jnp.float32),
        lax.psum(grad_gain_query.astype(jnp.bfloat16), "dp").astype(jnp.float32),
        lax.psum(grad_gain_key.astype(jnp.bfloat16), "dp").astype(jnp.float32),
    )
    gain_totals = lax.psum((grad_gain_attn, grad_gain_ffn), ("dp", "row"))
    return (
        layer_output,
        grad_input,
        summed[0],
        summed[1],
        summed[2],
        summed[3],
        summed[4],
        summed[5],
        summed[6],
        summed[7],
        summed[8],
        gain_totals[0],
        gain_totals[1],
    )


def solution(mesh):
    in_specs = (
        P(("dp", "row"), "col"),
        P("dp"),
        P("dp"),
        P("col", "row"),
        P("col", "row"),
        P("col", "row"),
        P("row", "col"),
        P("col", "row"),
        P("col", "row"),
        P("row", "col"),
        P(("row", "col")),
        P(("row", "col")),
        P("col"),
        P("col"),
        P(("dp", "row"), "col"),
    )
    out_specs = (
        P(("dp", "row"), "col"),
        P(("dp", "row"), "col"),
        P("col", "row"),
        P("col", "row"),
        P("col", "row"),
        P("row", "col"),
        P("col", "row"),
        P("col", "row"),
        P("row", "col"),
        P(("row", "col")),
        P(("row", "col")),
        P("col"),
        P("col"),
    )
    return jax.shard_map(
        per_device, mesh=mesh, in_specs=in_specs, out_specs=out_specs, check_vma=False
    )
```

profile of v0, /device:TPU:0, one launch (start us, length us, event | category | flops | bytes accessed | tf_op | source)
XLA Modules:
  0.0 2465.4 jit_solution(7940710772283181161)
XLA Ops:
  8.0 13.4 all-gather.12.cloned.1.call-done
  21.3 4.8 fusion.59
  33.1 4.8 fusion.60
  40.5 63.8 %reduce-scatter.14.cloned.1.call-done = f32[1024,256]{1,0:T(8,128)} async-done(((f32[1024,1024]{1,0:T(8,128)}), f32[1024,256]{1,0:T(8,128)}) %reduce-scatter.14.cloned.1.call-update) | async-done | bytes 1048592 | tf_op jit(solution)/shard_map/reduce_scatter | solution.py:182
  105.7 78.9 %reduce-scatter.12.cloned.1.call-done = f32[1024,256]{1,0:T(8,128)} async-done(((f32[1024,1024]{1,0:T(8,128)}), f32[1024,256]{1,0:T(8,128)}) %reduce-scatter.12.cloned.1.call-update) | async-done | bytes 1048592 | tf_op jit(solution)/shard_map/reduce_scatter | solution.py:181
  186.1 17.6 all-reduce.1
  219.0 46.2 %reduce-scatter.16.cloned.1.call-done = f32[1024,256]{1,0:T(8,128)} async-done(((f32[1024,1024]{1,0:T(8,128)}), f32[1024,256]{1,0:T(8,128)}) %reduce-scatter.16.cloned.1.call-update) | async-done | bytes 1048592 | tf_op jit(solution)/shard_map/reduce_scatter | solution.py:183
  266.6 16.0 while.27
  284.1 46.6 %all-gather.14.cloned.1.call-done = bf16[1024,1024]{1,0:T(8,128)(2,1)} async-done(((bf16[1024,256]{1,0:T(8,128)(2,1)}), bf16[1024,1024]{1,0:T(8,128)(2,1)}) %all-gather.14.cloned.1.call-update) | async-done | bytes 2097168 | tf_op jit(solution)/shard_map/all_gather | solution.py:56
  334.9 8.0 reduce-scatter.18.cloned.1.call-done
  344.2 12.0 psum.135
  358.9 6.9 all-gather.16.cloned.1.call-done
  365.8 12.8 fusion.63
  378.7 12.9 fusion.62
  391.7 268.6 %reduce-scatter.22.cloned.1.call-done = f32[1024,1024]{1,0:T(8,128)} async-done(((f32[1024,4096]{1,0:T(8,128)}), f32[1024,1024]{1,0:T(8,128)}) %reduce-scatter.22.cloned.1.call-update) | async-done | bytes 4194320 | tf_op jit(solution)/shard_map/reduce_scatter | solution.py:217
  660.3 283.5 %reduce-scatter.20.cloned.1.call-done = f32[1024,1024]{1,0:T(8,128)} async-done(((f32[1024,4096]{1,0:T(8,128)}), f32[1024,1024]{1,0:T(8,128)}) %reduce-scatter.20.cloned.1.call-update) | async-done | bytes 4194320 | tf_op jit(solution)/shard_map/reduce_scatter | solution.py:211
  943.8 6.1 multiply_convert_fusion.3
  950.1 150.4 %all-gather.18.cloned.1.call-done = bf16[1024,4096]{1,0:T(8,128)(2,1)} async-done(((bf16[1024,1024]{1,0:T(8,128)(2,1)}), bf16[1024,4096]{1,0:T(8,128)(2,1)}) %all-gather.18.cloned.1.call-update) | async-done | bytes 8388624 | tf_op jit(solution)/shard_map/all_gather | solution.py:56
  1100.5 10.4 fusion.64
  1110.9 7.9 reduce-scatter.24.cloned.1.call-done
  1120.2 12.0 psum.136
  1134.4 8.5 psum.137
  1145.3 8.8 all-gather.20.cloned.1.call-done
  1154.1 12.8 fusion.65
  1167.0 281.6 %reduce-scatter.26.cloned.1.call-done = f32[1024,1024]{1,0:T(8,128)} async-done(((f32[1024,4096]{1,0:T(8,128)}), f32[1024,1024]{1,0:T(8,128)}) %reduce-scatter.26.cloned.1.call-update) | async-done | bytes 4194320 | tf_op jit(solution)/shard_map/reduce_scatter | solution.py:60
  1448.5 7.2 multiply_convert_fusion.1
  1456.4 149.9 %all-gather.22.cloned.1.call-done = bf16[1024,4096]{1,0:T(8,128)(2,1)} async-done(((bf16[1024,1024]{1,0:T(8,128)(2,1)}), bf16[1024,4096]{1,0:T(8,128)(2,1)}) %all-gather.22.cloned.1.call-update) | async-done | bytes 8388624 | tf_op jit(solution)/shard_map/all_gather | solution.py:245
  1606.3 10.4 fusion.66
  1616.7 139.4 %all-gather.24.cloned.1.call-done = bf16[1024,4096]{1,0:T(8,128)(2,1)} async-done(((bf16[1024,1024]{1,0:T(8,128)(2,1)}), bf16[1024,4096]{1,0:T(8,128)(2,1)}) %all-gather.24.cloned.1.call-update) | async-done | bytes 8388624 | tf_op jit(solution)/shard_map/all_gather | solution.py:246
  1756.2 11.1 convolution_add_fusion
  1767.3 7.9 reduce-scatter.28.cloned.1.call-done
  1777.2 12.0 psum.138
  1792.7 7.3 all-gather.26.cloned.1.call-done
  1804.9 77.8 %reduce-scatter.30.cloned.1.call-done = f32[1024,256]{1,0:T(8,128)} async-done(((f32[1024,1024]{1,0:T(8,128)}), f32[1024,256]{1,0:T(8,128)}) %reduce-scatter.30.cloned.1.call-update) | async-done | bytes 1048592 | tf_op jit(solution)/shard_map/reduce_scatter | solution.py:60
  1886.7 26.9 %while.28 = (s32[]{:T(128)}, f32[1024,2,128]{0,2,1:T(8,128)S(1)}, f32[1024,2,128]{0,2,1:T(8,128)}, f32[2,512,2,128]{3,1,0,2:T(8,128)}, s32[2]{0:T(128)S(1)}, /*i...) while((s32[]{:T(128)}, f32[1024,2,128]{0,2,1:T(8,128)S(1)}, ...), condition=%wide.region_28.29_spmd.clone, body=%wide.region_26.28_spmd.clone.sunk | while | flops 1360920064 | bytes 58239312 | solution.py:155
  1920.7 16.3 all-reduce
  1944.9 40.6 %all-gather.28.cloned.1.call-done = bf16[1024,1024]{1,0:T(8,128)(2,1)} async-done(((bf16[1024,256]{1,0:T(8,128)(2,1)}), bf16[1024,1024]{1,0:T(8,128)(2,1)}) %all-gather.28.cloned.1.call-update) | async-done | bytes 2097168 | tf_op jit(solution)/shard_map/all_gather | solution.py:288
  1988.6 43.3 %all-gather.30.cloned.1.call-done = bf16[1024,1024]{1,0:T(8,128)(2,1)} async-done(((bf16[1024,256]{1,0:T(8,128)(2,1)}), bf16[1024,1024]{1,0:T(8,128)(2,1)}) %all-gather.30.cloned.1.call-update) | async-done | bytes 2097168 | tf_op jit(solution)/shard_map/all_gather | solution.py:289
  2036.4 41.9 %all-gather.32.cloned.1.call-done = bf16[1024,1024]{0,1:T(8,128)(2,1)} async-done(((bf16[1024,256]{0,1:T(8,128)(2,1)}), bf16[1024,1024]{0,1:T(8,128)(2,1)}) %all-gather.32.cloned.1.call-update) | async-done | bytes 2097168 | tf_op jit(solution)/shard_map/all_gather | solution.py:290
  2078.3 5.2 add_add_fusion
  2083.6 10.3 convolution_convert_fusion.2
  2093.8 9.7 convolution_convert_fusion.1
  2103.5 9.6 convolution_convert_fusion
  2122.9 14.6 all-reduce.2
  2137.4 7.7 all-reduce.3
  2148.7 285.5 %all-reduce.7.cloned.1.call-done = (bf16[512,1024]{0,1:T(8,128)(2,1)}, bf16[512,1024]{0,1:T(8,128)(2,1)}, bf16[512,1024]{0,1:T(8,128)(2,1)}, bf16[1024,512]{1,0:...) async-done(((bf16[512,1024]{0,1:T(8,128)(2,1)}, bf16[512,1024]{0,1:T(8,128)(2,1)}, bf16[512,1024]{0,1:T(8,128)(2,1)}, ...) | async-done | bytes 16777232 | tf_op jit(solution)/shard_map/psum | solution.py:313
  2442.8 6.8 convert_element_type.158
  2454.1 4.6 convert_element_type.162
  (252 shorter events, 144.4 us)
Async XLA Ops:
  7.2 323.5 %copy-start = (bf16[1024,512]{1,0:T(8,128)(2,1)S(1)}, bf16[1024,512]{1,0:T(8,128)(2,1)}, u32[]{:S(2)}) copy-start(bf16[1024,512]{1,0:T(8,128)(2,1)} %param.25) | copy-start | bytes 3145732
  7.2 14.1 all-gather.12.cloned.1.call-start
  7.9 96.3 %reduce-scatter.14.cloned.1.call-start = ((), (), s32[]{:S(2)}) async-start(), calls=%async_computation.13 | async-start | bytes 5242880 | tf_op jit(solution)/shard_map/reduce_scatter | solution.py:182
  26.2 158.4 %reduce-scatter.12.cloned.1.call-start = ((), (), s32[]{:S(2)}) async-start(), calls=%async_computation.12 | async-start | bytes 5242880 | tf_op jit(solution)/shard_map/reduce_scatter | solution.py:181
  31.9 233.4 %reduce-scatter.16.cloned.1.call-start = ((), (), s32[]{:S(2)}) async-start(), calls=%async_computation.14 | async-start | bytes 5242880 | tf_op jit(solution)/shard_map/reduce_scatter | solution.py:183
  37.9 167.0 %copy-start.38 = (f32[256]{0:T(256)S(1)}, f32[256]{0:T(256)}, u32[]{:S(2)}) copy-start(f32[256]{0:T(256)} %param.30) | copy-start | bytes 3076
  37.9 172.1 %copy-start.36 = (f32[256]{0:T(256)S(1)}, f32[256]{0:T(256)}, u32[]{:S(2)}) copy-start(f32[256]{0:T(256)} %param.29) | copy-start | bytes 3076
  37.9 292.8 %all-gather.14.cloned.1.call-start = ((), (), s32[]{:S(2)}) async-start(), calls=%async_computation.15 | async-start | bytes 2621440 | tf_op jit(solution)/shard_map/all_gather | solution.py:56
  40.5 177.4 %copy-start.13 = (f32[1024,64]{1,0:T(8,128)}, f32[1024,64]{1,0:T(8,128)S(1)}, u32[]{:S(2)}) copy-start(f32[1024,64]{1,0:T(8,128)S(1)} %get-tuple-element.305) | copy-start | bytes 786436
  40.5 177.4 %copy-start.14 = (f32[1024,64]{1,0:T(8,128)}, f32[1024,64]{1,0:T(8,128)S(1)}, u32[]{:S(2)}) copy-start(f32[1024,64]{1,0:T(8,128)S(1)} %get-tuple-element.306) | copy-start | bytes 786436
  184.5 25.4 %copy-start.3 = (f32[1024,256]{1,0:T(8,128)S(1)}, f32[1024,256]{1,0:T(8,128)}, u32[]{:S(2)}) copy-start(f32[1024,256]{1,0:T(8,128)} %reduce-scatter.12.cloned.1.call-done) | copy-start | bytes 3145732
  204.3 9.7 copy-start.30
  211.1 5.6 copy-start.11
  218.4 48.1 %copy-start.26 = (s32[1024]{0:T(1024)S(1)}, s32[1024]{0:T(1024)}, u32[]{:S(2)}) copy-start(s32[1024]{0:T(1024)} %param.20) | copy-start | bytes 12292
  218.4 48.1 %copy-start.27 = (bf16[2,512,2,128]{3,1,2,0:T(8,128)(2,1)S(1)}, bf16[2,512,2,128]{3,1,2,0:T(8,128)(2,1)}, u32[]{:S(2)}) copy-start(bf16[2,512,2,128]{3,1,2,0:T(8,128)(2,1)} %custom-call.2) | copy-start | bytes 1572868
  284.0 72.2 %copy-start.15 = (bf16[512,512]{1,0:T(8,128)(2,1)S(1)}, bf16[512,512]{1,0:T(8,128)(2,1)}, u32[]{:S(2)}) copy-start(bf16[512,512]{1,0:T(8,128)(2,1)} %param.19) | copy-start | bytes 1572868
  284.0 72.2 %copy-start.32 = (f32[512]{0:T(512)S(1)}, f32[512]{0:T(512)}, u32[]{:S(2)}) copy-start(f32[512]{0:T(512)} %param.31) | copy-start | bytes 6148
  284.0 58.9 %reduce-scatter.18.cloned.1.call-start = ((), (), s32[]{:S(2)}) async-start(), calls=%async_computation.16 | async-start | bytes 3145728 | tf_op jit(solution)/shard_map/reduce_scatter | solution.py:52
  334.9 31.0 %all-gather.16.cloned.1.call-start = ((), (), s32[]{:S(2)}) async-start(), calls=%async_computation.17 | async-start | bytes 1572864 | tf_op jit(solution)/shard_map/all_gather | solution.py:48
  358.5 301.8 %reduce-scatter.22.cloned.1.call-start = ((), (), s32[]{:S(2)}) async-start(), calls=%async_computation.19 | async-start | bytes 20971520 | tf_op jit(solution)/shard_map/reduce_scatter | solution.py:217
  378.6 565.2 %reduce-scatter.20.cloned.1.call-start = ((), (), s32[]{:S(2)}) async-start(), calls=%async_computation.18 | async-start | bytes 20971520 | tf_op jit(solution)/shard_map/reduce_scatter | solution.py:211
  391.7 708.8 %all-gather.18.cloned.1.call-start = ((), (), s32[]{:S(2)}) async-start(), calls=%async_computation.20 | async-start | bytes 10485760 | tf_op jit(solution)/shard_map/all_gather | solution.py:56
  950.0 182.2 %copy-start.5 = (bf16[512,512]{1,0:T(8,128)(2,1)S(1)}, bf16[512,512]{1,0:T(8,128)(2,1)}, u32[]{:S(2)}) copy-start(bf16[512,512]{1,0:T(8,128)(2,1)} %param.33) | copy-start | bytes 1572868
  950.0 182.2 %copy-start.33 = (f32[512]{0:T(512)S(1)}, f32[512]{0:T(512)}, u32[]{:S(2)}) copy-start(f32[512]{0:T(512)} %param.32) | copy-start | bytes 6148
  950.0 168.8 %reduce-scatter.24.cloned.1.call-start = ((), (), s32[]{:S(2)}) async-start(), calls=%async_computation.21 | async-start | bytes 3145728 | tf_op jit(solution)/shard_map/reduce_scatter | solution.py:52
  1110.9 43.2 %all-gather.20.cloned.1.call-start = ((), (), s32[]{:S(2)}) async-start(), calls=%async_computation.22 | async-start | bytes 1572864 | tf_op jit(solution)/shard_map/all_gather | solution.py:48
  1145.3 303.3 %reduce-scatter.26.cloned.1.call-start = ((), (), s32[]{:S(2)}) async-start(), calls=%async_computation.23 | async-start | bytes 20971520 | tf_op jit(solution)/shard_map/reduce_scatter | solution.py:60
  1166.9 439.4 %all-gather.22.cloned.1.call-start = ((), (), s32[]{:S(2)}) async-start(), calls=%async_computation.24 | async-start | bytes 10485760 | tf_op jit(solution)/shard_map/all_gather | solution.py:245
  1455.8 300.4 %all-gather.24.cloned.1.call-start = ((), (), s32[]{:S(2)}) async-start(), calls=%async_computation.25 | async-start | bytes 10485760 | tf_op jit(solution)/shard_map/all_gather | solution.py:246
  1456.4 318.8 %reduce-scatter.28.cloned.1.call-start = ((), (), s32[]{:S(2)}) async-start(), calls=%async_computation.26 | async-start | bytes 3145728 | tf_op jit(solution)/shard_map/reduce_scatter | solution.py:52
  1767.3 32.8 %all-gather.26.cloned.1.call-start = ((), (), s32[]{:S(2)}) async-start(), calls=%async_computation.27 | async-start | bytes 1572864 | tf_op jit(solution)/shard_map/all_gather | solution.py:48
  1792.7 90.0 %reduce-scatter.30.cloned.1.call-start = ((), (), s32[]{:S(2)}) async-start(), calls=%async_computation.28 | async-start | bytes 5242880 | tf_op jit(solution)/shard_map/reduce_scatter | solution.py:60
  1804.6 180.9 %all-gather.28.cloned.1.call-start = ((), (), s32[]{:S(2)}) async-start(), calls=%async_computation.29 | async-start | bytes 2621440 | tf_op jit(solution)/shard_map/all_gather | solution.py:288
  1914.9 5.0 copy-start.31
  1915.0 5.0 copy-start.37
  1918.3 18.8 copy-start.35
  1920.0 20.3 copy-start.34
  1940.2 91.7 %all-gather.30.cloned.1.call-start = ((), (), s32[]{:S(2)}) async-start(), calls=%async_computation.30 | async-start | bytes 2621440 | tf_op jit(solution)/shard_map/all_gather | solution.py:289
  1943.5 134.8 %all-gather.32.cloned.1.call-start = ((), (), s32[]{:S(2)}) async-start(), calls=%async_computation.31 | async-start | bytes 2621440 | tf_op jit(solution)/shard_map/all_gather | solution.py:290
  1944.4 201.8 %reduce-scatter.32.cloned.1.call-start = ((), (), s32[]{:S(2)}) async-start(), calls=%async_computation.32 | async-start | bytes 3145728 | tf_op jit(solution)/shard_map/reduce_scatter | solution.py:52
  2083.5 10.3 copy-start.47
  2083.5 350.8 %all-reduce.7.cloned.1.call-start = ((), (), s32[]{:S(2)}) async-start(), calls=%async_computation.33 | async-start | bytes 33554432 | tf_op jit(solution)/shard_map/psum | solution.py:313
  2103.5 9.6 copy-start.42
  2103.5 9.6 copy-start.48
  2122.2 24.1 copy-start.10
  2434.3 5.3 copy-start.21
  2434.3 6.9 copy-start.20
  2442.8 6.8 copy-start.17
  (28 other events, 65.3 us)
Sparse Core Ops, SparseCore 0:
  9.6 11.7 all-gather.11
  26.3 77.9 reduce-scatter.13
  107.2 77.2 reduce-scatter.11
  187.3 77.9 reduce-scatter.15
  284.1 46.5 all-gather.13
  335.0 7.8 reduce-scatter.17
  358.6 7.1 all-gather.15
  378.8 281.4 reduce-scatter.21
  662.7 281.0 reduce-scatter.19
  950.1 150.3 all-gather.17
  1111.0 7.7 reduce-scatter.23
  1145.4 8.6 all-gather.19
  1167.0 281.4 reduce-scatter.25
  1455.9 150.3 all-gather.21
  1608.3 147.8 all-gather.23
  1767.4 7.7 reduce-scatter.27
  1792.8 7.1 all-gather.25
  1804.7 77.9 reduce-scatter.29
  1940.3 45.0 all-gather.27
  1987.4 44.4 all-gather.29
  2034.1 44.1 all-gather.31
  2083.6 8.3 reduce-scatter.31
  2122.4 311.8 all-reduce.6
where the time goes:
time: 2470 us
  waiting for transfers between devices  2060 us (83%)
  matrix products  161 us (7%)
  blocking collectives  101 us (4%)
  other arithmetic  85.1 us (3%)
  local copies, waits for them, and re-layouts  34.1 us (1%)
    reduce_scatter x2, waiting for transfers between devices, columns_sum(): return lax.psum_scatter(values, 'col', scatter_dimension=1, tiled=True)  359 us
    psum x1, waiting for transfers between devices, per_device(): lax.psum(grad_w_query.astype(jnp.bfloat16), 'dp').astype(jnp.float32)  286 us
    reduce_scatter x1, waiting for transfers between devices, per_device(): lax.psum_scatter(jnp.dot(state_rows, w_gate, preferred_element_type=jnp.f...  284 us
    reduce_scatter x1, waiting for transfers between devices, per_device(): lax.psum_scatter(jnp.dot(state_rows, w_up, preferred_element_type=jnp.flo...  269 us
    all_gather x2, waiting for transfers between devices, columns_gather(): return lax.all_gather(values, 'col', axis=1, tiled=True)  197 us
    all_gather x1, waiting for transfers between devices, per_device(): lax.all_gather(grad_gate.astype(jnp.bfloat16), 'col', axis=1, tiled=True)  150 us
    all_gather x1, waiting for transfers between devices, per_device(): lax.all_gather(grad_up.astype(jnp.bfloat16), 'col', axis=1, tiled=True)  139 us
    reduce_scatter x1, waiting for transfers between devices, per_device(): lax.psum_scatter(query_part, 'col', scatter_dimension=1, tiled=True)  78.9 us
  transfers between devices with their start and end apart: 23, of which 22 were waited for; matrix products, arithmetic and copies ran while one was open for 4% of the time, Pallas kernels for 0%

commit v1 on v0

v1 whole, which is shorter than its diff:
```python
import functools

import jax
import jax.numpy as jnp
from jax import lax
from jax.experimental import pallas as pl
from jax.experimental.pallas import tpu as pltpu
from jax.sharding import PartitionSpec as P

HEAD = 128
EPSILON = 1e-06
ROPE_BASE = 500000.0
MASKED = -1e30
BF = jnp.bfloat16
F32 = jnp.float32


def rope_tables(positions):
    digit = 32
    frequency = ROPE_BASE ** (-(jnp.arange(HEAD // 2, dtype=F32) * (2.0 / HEAD)))
    frequency = jnp.concatenate([frequency, frequency])

    def looked_up(index, count, unit):
        angles = (jnp.arange(count) * unit).astype(F32)[:, None] * frequency[None, :]
        table = jnp.concatenate([jnp.cos(angles), jnp.sin(angles)], axis=1)
        chosen = (index[:, None] == jnp.arange(count)[None, :]).astype(F32)
        both = jnp.dot(chosen, table, precision=lax.Precision.HIGHEST)
        return both[:, :HEAD], both[:, HEAD:]

    high_cosine, high_sine = looked_up(
        positions // digit, -(-positions.shape[0] // digit), digit
    )
    low_cosine, low_sine = looked_up(positions % digit, digit, 1)
    signs = jnp.where(jnp.arange(HEAD) < HEAD // 2, -1.0, 1.0).astype(F32)[None, :]
    return (
        high_cosine * low_cosine - high_sine * low_sine,
        (high_sine * low_cosine + high_cosine * low_sine) * signs,
    )


def dot(a, b):
    return jnp.dot(a, b, preferred_element_type=F32)


def dot_nt(a, b):
    return lax.dot_general(a, b, (((1,), (1,)), ((), ())), preferred_element_type=F32)


def dot_tn(a, b):
    return lax.dot_general(a, b, (((0,), (0,)), ((), ())), preferred_element_type=F32)


class Ring:
    def __init__(self, name, size):
        self.name, self.size = name, size
        self.here = lax.axis_index(name)

    def fetch(self, values, step):
        if step % self.size == 0:
            return values
        pairs = [(i, (i - step) % self.size) for i in range(self.size)]
        return lax.ppermute(values, self.name, pairs)

    def send(self, values, pairs):
        return lax.ppermute(values, self.name, pairs)

    def give(self, values, step):
        return self.fetch(values, -step)

    def at(self, step):
        return lax.rem(self.here + (step % self.size), self.size)


def gather_col(col, values):
    if col.size != 4:
        return [col.fetch(values, k) for k in range(col.size)]
    two = col.send(values, [(0, 2), (1, 3), (2, 0), (3, 1)])
    below = col.send(values, [(0, 1), (1, 2), (2, 3)])
    above = col.send(values, [(1, 0), (2, 1), (3, 2)])
    relayed = col.send(two, [(2, 3), (1, 0)])
    return [
        values,
        jnp.where(col.here == 3, relayed, above),
        two,
        jnp.where(col.here == 0, relayed, below),
    ]


def reduce_col(col, blocks):
    low = [block.astype(BF) for block in blocks]
    result = blocks[0]
    if col.size != 4:
        for k in range(1, col.size):
            result = result + col.give(low[k], k).astype(F32)
        return result
    relayed = col.send(jnp.where(col.here == 3, low[1], low[3]), [(3, 2), (0, 1)])
    above = col.send(low[3], [(1, 0), (2, 1), (3, 2)])
    below = col.send(low[1], [(0, 1), (1, 2), (2, 3)])
    two = (blocks[2] + relayed.astype(F32)).astype(BF)
    two = col.send(two, [(0, 2), (1, 3), (2, 0), (3, 1)])
    return result + above.astype(F32) + below.astype(F32) + two.astype(F32)


def after(values, *earlier):
    return lax.optimization_barrier((values, earlier))[0]


def block_at(values, index, size, axis):
    return lax.dynamic_slice_in_dim(values, index * size, size, axis)


def assemble(ring, blocks, axis):
    size = blocks[0].shape[axis]
    shape = list(blocks[0].shape)
    shape[axis] = size * ring.size
    whole = jnp.zeros(shape, blocks[0].dtype)
    for step, block in enumerate(blocks):
        whole = lax.dynamic_update_slice_in_dim(whole, block, ring.at(step) * size, axis)
    return whole


def from_here(ring, values, size, axis):
    twice = jnp.concatenate([values, values], axis=axis)
    return lax.dynamic_slice_in_dim(twice, ring.here * size, size * ring.size, axis)


def to_order(ring, values, size, axis):
    twice = jnp.concatenate([values, values], axis=axis)
    start = lax.rem(ring.size - ring.here, ring.size) * size
    return lax.dynamic_slice_in_dim(twice, start, size * ring.size, axis)


def exchange(ring, block_for):
    return [ring.fetch(block_for(ring.at(-step)), step) for step in range(ring.size)]


def gather_tokens(row, col, values):
    return [
        jnp.concatenate([row.fetch(block, j) for j in range(row.size)], axis=0)
        for block in gather_col(col, values)
    ]


def sum_rows(row, partial):
    parts = jnp.split(partial, row.size, axis=0)
    total = parts[0]
    for j in range(1, row.size):
        total = total + row.give(parts[j].astype(BF), j).astype(F32)
    return total


def sum_tokens(row, col, partials):
    return reduce_col(col, [sum_rows(row, partial) for partial in partials])


def sum_all(row, col, values):
    size = values.shape[1] // row.size
    total = values
    for j in range(1, row.size):
        total = total + jnp.roll(row.fetch(values, j), j * size, axis=1)
    result = total
    for k in range(1, col.size):
        result = result + col.fetch(total, k)
    return result


def rms_scale(values):
    return lax.rsqrt(jnp.mean(values * values, axis=1, keepdims=True) + EPSILON)


def rms_back(grad_normed, branch, scales, gains):
    weighted = grad_normed * gains
    inner = jnp.mean(weighted * branch, axis=1, keepdims=True)
    grad_branch = scales * weighted - branch * (scales * scales * scales) * inner
    grad_gains = jnp.sum(grad_normed * branch * scales, axis=0)
    return grad_branch, grad_gains


def turn(values, cosine, sine):
    return values * cosine + pltpu.roll(values, values.shape[-1] // 2, 1) * sine


def kernel_dot(a, b, dims):
    return lax.dot_general(a, b, (dims, ((), ())), preferred_element_type=F32)


def block_scores(queries, keys, doc_rows, doc_cols, slot_rows, slot_cols):
    scores = kernel_dot(queries, keys, ((1,), (1,))) * (HEAD**-0.5)
    allowed = (doc_rows == doc_cols) & (slot_cols <= slot_rows)
    return jnp.where(allowed, scores, MASKED)


def forward_kernel(
    block_rows,
    query_ref,
    key_ref,
    value_ref,
    query_scale_ref,
    key_scale_ref,
    query_gain_ref,
    key_gain_ref,
    cosine_ref,
    sine_ref,
    doc_rows_ref,
    doc_cols_ref,
    slot_rows_ref,
    slot_cols_ref,
    query_rot_ref,
    key_rot_ref,
    value_low_ref,
    mixture_ref,
    log_ref,
):
    cosine, sine = cosine_ref[...], sine_ref[...]
    normed = query_ref[...] * query_scale_ref[...] * query_gain_ref[...]
    query_rot_ref[...] = turn(normed, cosine, sine).astype(BF)
    normed = key_ref[...] * key_scale_ref[...] * key_gain_ref[...]
    key_rot_ref[...] = turn(normed, cosine, sine).astype(BF)
    value_low_ref[...] = value_ref[...].astype(BF)
    keys, values = key_rot_ref[...], value_low_ref[...]
    for start in range(0, query_ref.shape[0], block_rows):
        rows = pl.ds(start, block_rows)
        scores = block_scores(
            query_rot_ref[rows, :],
            keys,
            doc_rows_ref[rows, :],
            doc_cols_ref[...],
            slot_rows_ref[rows, :],
            slot_cols_ref[...],
        )
        largest = jnp.max(scores, axis=1, keepdims=True)
        weights = jnp.exp(scores - largest)
        totals = jnp.sum(weights, axis=1, keepdims=True)
        chances = (weights * (1.0 / totals)).astype(BF)
        mixture_ref[rows, :] = kernel_dot(chances, values, ((1,), (0,))).astype(BF)
        log_ref[0, rows, :] = largest + jnp.log(totals)


def backward_kernel(
    block_rows,
    query_ref,
    key_ref,
    query_scale_ref,
    key_scale_ref,
    query_gain_ref,
    key_gain_ref,
    cosine_ref,
    sine_ref,
    doc_rows_ref,
    doc_cols_ref,
    slot_rows_ref,
    slot_cols_ref,
    query_rot_ref,
    key_rot_ref,
    value_low_ref,
    grad_ref,
    log_ref,
    query_weighted_ref,
    key_weighted_ref,
    grad_value_ref,
    query_inner_ref,
    key_inner_ref,
    query_gain_grad_ref,
    key_gain_grad_ref,
    key_total,
    value_total,
):
    cosine, sine = cosine_ref[...], sine_ref[...]
    keys, values = key_rot_ref[...], value_low_ref[...]
    factor = HEAD**-0.5
    for start in range(0, query_ref.shape[0], block_rows):
        rows = pl.ds(start, block_rows)
        queries, grads = query_rot_ref[rows, :], grad_ref[rows, :]
        scores = block_scores(
            queries,
            keys,
            doc_rows_ref[rows, :],
            doc_cols_ref[...],
            slot_rows_ref[rows, :],
            slot_cols_ref[...],
        )
        chances = jnp.exp(scores - log_ref[0, rows, :])
        value_part = kernel_dot(chances.astype(BF), grads, ((0,), (0,)))
        grad_chances = kernel_dot(grads, values, ((1,), (1,)))
        inner = jnp.sum(chances * grad_chances, axis=1, keepdims=True)
        grad_scores = (chances * (grad_chances - inner)).astype(BF)
        query_weighted_ref[rows, :] = kernel_dot(grad_scores, keys, ((1,), (0,))) * factor
        key_part = kernel_dot(grad_scores, queries, ((0,), (0,))) * factor
        if start == 0:
            value_total[...] = value_part
            key_total[...] = key_part
        else:
            value_total[...] += value_part
            key_total[...] += key_part
    grad_value_ref[...] = value_total[...].astype(BF)
    for grad, raw_ref, scale_ref, gain_ref, weighted_ref, inner_ref, gain_grad_ref in (
        (
            query_weighted_ref[...],
            query_ref,
            query_scale_ref,
            query_gain_ref,
            query_weighted_ref,
            query_inner_ref,
            query_gain_grad_ref,
        ),
        (
            key_total[...],
            key_ref,
            key_scale_ref,
            key_gain_ref,
            key_weighted_ref,
            key_inner_ref,
            key_gain_grad_ref,
        ),
    ):
        unturned = turn(grad, cosine, -sine)
        raw = raw_ref[...]
        gain_grad_ref[0] = jnp.sum(unturned * raw * scale_ref[...], axis=0, keepdims=True)
        weighted = unturned * gain_ref[...]
        weighted_ref[...] = weighted
        inner_ref[0] = jnp.sum(weighted * raw, axis=1, keepdims=True)


def head_specs(length, heads):
    return {
        "head": lambda first: pl.BlockSpec((length, HEAD), lambda h, first=first: (0, first + h)),
        "gain": pl.BlockSpec((1, HEAD), lambda h: (0, h)),
        "column": pl.BlockSpec((length, 1), lambda h: (0, 0)),
        "line": pl.BlockSpec((1, length), lambda h: (0, 0)),
        "table": pl.BlockSpec((length, HEAD), lambda h: (0, 0)),
        "head_column": pl.BlockSpec((1, length, 1), lambda h: (h, 0, 0)),
        "head_line": pl.BlockSpec((1, 1, HEAD), lambda h: (h, 0, 0)),
    }


def attend_forward(raw, query_scale, key_scale, gains, tables, marks):
    length = raw.shape[0]
    heads = raw.shape[1] // (3 * HEAD)
    spec = head_specs(length, heads)
    wide = jax.ShapeDtypeStruct((length, heads * HEAD), BF)
    return pl.pallas_call(
        functools.partial(forward_kernel, min(256, length)),
        grid=(heads,),
        in_specs=[spec["head"](0), spec["head"](heads), spec["head"](2 * heads)]
        + [spec["column"]] * 2
        + [spec["gain"]] * 2
        + [spec["table"]] * 2
        + [spec["column"], spec["line"], spec["column"], spec["line"]],
        out_specs=[spec["head"](0)] * 4 + [spec["head_column"]],
        out_shape=[wide] * 4 + [jax.ShapeDtypeStruct((heads, length, 1), F32)],
        compiler_params=pltpu.CompilerParams(vmem_limit_bytes=40 << 20),
        cost_estimate=pl.CostEstimate(
            flops=heads * 4 * length * length * HEAD,
            bytes_accessed=heads * length * HEAD * 20,
            transcendentals=heads * length * length,
        ),
        name="attend_forward",
    )(raw, raw, raw, query_scale, key_scale, *gains, *tables, *marks)


def attend_backward(raw, query_scale, key_scale, gains, tables, marks, saved, grad, logs):
    length = raw.shape[0]
    heads = raw.shape[1] // (3 * HEAD)
    spec = head_specs(length, heads)
    wide = jax.ShapeDtypeStruct((length, heads * HEAD), F32)
    low = jax.ShapeDtypeStruct((length, heads * HEAD), BF)
    tall = jax.ShapeDtypeStruct((heads, length, 1), F32)
    flat = jax.ShapeDtypeStruct((heads, 1, HEAD), F32)
    return pl.pallas_call(
        functools.partial(backward_kernel, min(256, length)),
        grid=(heads,),
        in_specs=[spec["head"](0), spec["head"](heads)]
        + [spec["column"]] * 2
        + [spec["gain"]] * 2
        + [spec["table"]] * 2
        + [spec["column"], spec["line"], spec["column"], spec["line"]]
        + [spec["head"](0)] * 4
        + [spec["head_column"]],
        out_specs=[spec["head"](0)] * 3 + [spec["head_column"]] * 2 + [spec["head_line"]] * 2,
        out_shape=[wide, wide, low, tall, tall, flat, flat],
        scratch_shapes=[pltpu.VMEM((length, HEAD), F32)] * 2,
        compiler_params=pltpu.CompilerParams(vmem_limit_bytes=40 << 20),
        cost_estimate=pl.CostEstimate(
            flops=heads * 10 * length * length * HEAD,
            bytes_accessed=heads * length * HEAD * 30,
            transcendentals=heads * length * length,
        ),
        name="attend_backward",
    )(raw, raw, query_scale, key_scale, *gains, *tables, *marks, *saved, grad, logs)


def device_program(sizes):
    n_dp, n_row, n_col = sizes["dp"], sizes["row"], sizes["col"]

    def per_device(
        layer_input,
        doc_ids,
        positions,
        w_query,
        w_key,
        w_value,
        w_out,
        w_gate,
        w_up,
        w_down,
        gain_query,
        gain_key,
        gain_attn,
        gain_ffn,
        grad_output,
    ):
        row, col = Ring("row", n_row), Ring("col", n_col)
        dp = lax.axis_index("dp")
        length = doc_ids.shape[0]
        row_tokens = layer_input.shape[0]
        own_tokens = row_tokens // n_col
        features = layer_input.shape[1]
        width = features * n_col
        head_cols = w_query.shape[1] // n_col
        hidden_cols = w_gate.shape[1] // n_col
        in_rows = features // n_dp
        out_rows = head_cols // n_dp
        down_rows = hidden_cols // n_dp

        def gather_dp(values):
            return lax.all_gather(values, "dp", axis=0, tiled=True)

        steps = [1 << bit for bit in range(n_dp.bit_length() - 1)]

        def partner(values, step):
            return lax.ppermute(values, "dp", [(i, i ^ step) for i in range(n_dp)])

        class GroupSum:
            def __init__(self, block_for):
                blocks = [block_for(dp ^ d) for d in range(n_dp)]
                half = blocks[0].shape[-1] // 2
                self.halves = [
                    (dict(enumerate(b[..., :half] for b in blocks)), list(steps)),
                    (dict(enumerate(b[..., half:] for b in blocks)), list(steps[::-1])),
                ]
                self.came = None
                self.send()

            def send(self):
                self.came = []
                for blocks, order in self.halves:
                    given = [blocks[d] for d in sorted(blocks) if d & order[0]]
                    self.came.append(partner(jnp.stack(given), order[0]))

            def land(self, chain, more=True):
                self.came, chain = lax.optimization_barrier((self.came, chain))
                for (blocks, order), came in zip(self.halves, self.came):
                    step = order.pop(0)
                    for place, d in enumerate([d for d in sorted(blocks) if d & step]):
                        kept = blocks[d ^ step].astype(F32) + came[place].astype(F32)
                        blocks[d ^ step] = kept.astype(BF)
                        del blocks[d]
                if self.halves[0][1]:
                    self.send()
                return chain

            def finish(self, chain):
                while self.halves[0][1]:
                    chain = self.land(chain)
                whole = jnp.concatenate([blocks[0] for blocks, _ in self.halves], axis=-1)
                return whole, chain

        def qkv_block(index):
            return jnp.concatenate(
                [
                    lax.dynamic_slice(
                        w, (dp * in_rows, index * head_cols), (in_rows, head_cols)
                    )
                    for w in (w_query, w_key, w_value)
                ],
                axis=1,
            )

        def gate_up_block(index):
            return jnp.concatenate(
                [
                    lax.dynamic_slice(
                        w, (dp * in_rows, index * hidden_cols), (in_rows, hidden_cols)
                    )
                    for w in (w_gate, w_up)
                ],
                axis=1,
            )

        def out_block(index):
            return lax.dynamic_slice_in_dim(
                w_out, index * head_cols + dp * out_rows, out_rows, 0
            )

        def down_block(index):
            return lax.dynamic_slice_in_dim(
                w_down, index * hidden_cols + dp * down_rows, down_rows, 0
            )

        qkv_parts = jnp.stack(exchange(col, qkv_block))
        w_qkv = gather_dp(qkv_parts[None])
        w_qkv = [w_qkv[:, k].reshape(features, 3 * head_cols) for k in range(n_col)]
        out_parts = assemble(col, exchange(col, out_block), 1)
        w_out_all = gather_dp(out_parts)

        turned_docs = from_here(row, doc_ids, row_tokens, 0)
        turned_positions = from_here(row, positions, row_tokens, 0)
        slots = lax.rem(jnp.arange(length) + row.here * row_tokens, length)
        tables = rope_tables(turned_positions)
        near, tables = lax.optimization_barrier((gather_col(col, layer_input), tables))
        input_rows = [
            jnp.concatenate([row.fetch(block, j) for j in range(n_row)], axis=0)
            for block in near
        ]
        own_input = jnp.concatenate(
            [block_at(block, col.here, own_tokens, 0) for block in near], axis=1
        )
        own_input = to_order(col, own_input, features, 1).astype(F32)

        w_down, grad_output = after((w_down, grad_output), near)
        down_parts = exchange(col, down_block)
        cotangent = exchange(
            col, lambda index: block_at(grad_output, index, own_tokens, 0)
        )

        raw = sum(dot(rows, w) for rows, w in zip(input_rows, w_qkv))
        query_raw = raw[:, :head_cols]
        key_raw = raw[:, head_cols : 2 * head_cols]
        squares = jnp.stack(
            [jnp.sum(query_raw * query_raw, axis=1), jnp.sum(key_raw * key_raw, axis=1)]
        )
        squares = sum_all(row, col, squares)
        gains = jnp.stack([gain_attn, gain_ffn])
        gains = assemble(col, [col.fetch(gains, k) for k in range(n_col)], 1)
        gain_attn_all, gain_ffn_all = gains[0:1], gains[1:2]

        squares, down_parts, cotangent = lax.optimization_barrier(
            (squares, down_parts, cotangent)
        )
        w_down_all = gather_dp(assemble(col, down_parts, 1))
        cotangent = assemble(col, cotangent, 1).astype(F32)
        w_gate, w_up = after((w_gate, w_up), down_parts)
        gate_up_parts = exchange(col, gate_up_block)

        scales = lax.rsqrt(squares / width + EPSILON)
        query_scale, key_scale = scales[0][:, None], scales[1][:, None]
        head_gains = (gain_query[None, :], gain_key[None, :])
        marks = (turned_docs[:, None], turned_docs[None, :], slots[:, None], slots[None, :])
        *saved, mixture, logs = attend_forward(
            raw, query_scale, key_scale, head_gains, tables, marks
        )
        mixture = from_here(
            col, mixture.reshape(n_row, row_tokens, head_cols), own_tokens, 1
        ).reshape(n_row, n_col, own_tokens, head_cols)
        mixture = [mixture[:, k].reshape(-1, head_cols) for k in range(n_col)]
        attended = [dot(block, w_out_all) for block in mixture]
        gate_up_parts, attended = lax.optimization_barrier((gate_up_parts, attended))
        gate_up_parts = assemble(col, [part[None] for part in gate_up_parts], 0)
        w_gate_up = gather_dp(gate_up_parts[None])
        w_gate_up = w_gate_up.transpose(1, 0, 2, 3).reshape(width, 2 * hidden_cols)
        attended = sum_tokens(row, col, attended)
        attn_scale = rms_scale(attended)
        hidden_state = own_input + attended * attn_scale * gain_attn_all

        state_rows = gather_tokens(row, col, hidden_state.astype(BF))
        kept, activated = [], []
        for block in state_rows:
            gate_up = dot(block, w_gate_up)
            gate_values, up_values = gate_up[:, :hidden_cols], gate_up[:, hidden_cols:]
            sigmoid_gate = jax.nn.sigmoid(gate_values)
            silu_gate = gate_values * sigmoid_gate
            kept.append((gate_values, up_values, sigmoid_gate, silu_gate))
            activated.append((silu_gate * up_values).astype(BF))
        lowered = sum_tokens(row, col, [dot(block, w_down_all) for block in activated])
        ffn_scale = rms_scale(lowered)
        own_output = (hidden_state + lowered * ffn_scale * gain_ffn_all).astype(BF)
        layer_output = assemble(
            col,
            exchange(col, lambda index: block_at(own_output, index, features, 1)),
            0,
        )

        grad_lowered, grad_gain_ffn = rms_back(cotangent, lowered, ffn_scale, gain_ffn_all)
        lowered_rows = gather_tokens(row, col, grad_lowered.astype(BF))
        grad_gate_up, state_part = [], []
        for block, (gate_values, up_values, sigmoid_gate, silu_gate) in zip(lowered_rows, kept):
            grad_activated = dot_nt(block, w_down_all)
            grad_gate = (
                grad_activated
                * up_values
                * (sigmoid_gate * (1.0 + gate_values * (1.0 - sigmoid_gate)))
            )
            grad_up = grad_activated * silu_gate
            grad_gate_up.append(
                jnp.concatenate([grad_gate.astype(BF), grad_up.astype(BF)], axis=1)
            )
            state_part.append(dot_nt(grad_gate_up[-1], w_gate_up))
        grad_w_down = dot_tn(jnp.concatenate(activated), jnp.concatenate(lowered_rows))
        grad_w_down = grad_w_down.astype(BF)
        down_sum = GroupSum(lambda index: block_at(grad_w_down, index, down_rows, 0))
        grad_w_gate_up = dot_tn(jnp.concatenate(state_rows), jnp.concatenate(grad_gate_up))
        grad_w_gate_up = grad_w_gate_up.astype(BF)
        gate_up_grads = grad_w_gate_up.reshape(n_col, n_dp, in_rows, 2 * hidden_cols)
        gate_up_sum = GroupSum(
            lambda index: lax.dynamic_index_in_dim(gate_up_grads, index, 1, False)
        )
        state_part = sum_tokens(row, col, state_part)
        state_part = down_sum.land(state_part)
        state_part = gate_up_sum.land(state_part)
        down_sum, state_part = down_sum.finish(state_part)
        grad_state = cotangent + state_part
        grad_attended, grad_gain_attn = rms_back(
            grad_state, attended, attn_scale, gain_attn_all
        )
        attended_rows = gather_tokens(row, col, grad_attended.astype(BF))
        gate_up_sum, attended_rows = gate_up_sum.finish(attended_rows)
        mixture, attended_rows = jnp.concatenate(mixture), jnp.concatenate(attended_rows)
        gate_up_sum = gate_up_sum.reshape(-1, 2 * hidden_cols)

        def give_back(parts_for):
            return gather_dp(
                assemble(col, [part[None] for part in exchange(col, parts_for)], 0)[None]
            )

        down_sum, gate_up_sum = after((down_sum, gate_up_sum), attended_rows)
        down_all = give_back(lambda index: block_at(down_sum, index, features, 1))
        gate_up_all = give_back(lambda index: block_at(gate_up_sum, index, in_rows, 0))
        grad_w_out = dot_tn(mixture, attended_rows).astype(BF)
        out_sum = GroupSum(lambda index: block_at(grad_w_out, index, out_rows, 0))
        grad_mixture = dot_nt(attended_rows, w_out_all).astype(BF)
        grad_mixture = grad_mixture.reshape(n_col, n_row, own_tokens, head_cols)
        grad_mixture = grad_mixture.swapaxes(0, 1).reshape(n_row, row_tokens, head_cols)
        grad_mixture = to_order(col, grad_mixture, own_tokens, 1).reshape(length, head_cols)
        (
            query_weighted,
            key_weighted,
            grad_value,
            query_inner,
            key_inner,
            grad_gain_query,
            grad_gain_key,
        ) = attend_backward(
            raw, query_scale, key_scale, head_gains, tables, marks, saved, grad_mixture, logs
        )
        inner = jnp.stack([jnp.sum(query_inner, axis=0)[:, 0], jnp.sum(key_inner, axis=0)[:, 0]])
        inner = sum_all(row, col, inner) / width
        grad_query = (
            query_scale * query_weighted
            - query_raw * (query_scale * query_scale * query_scale) * inner[0][:, None]
        )
        grad_key = (
            key_scale * key_weighted
            - key_raw * (key_scale * key_scale * key_scale) * inner[1][:, None]
        )
        grad_qkv = jnp.concatenate(
            [grad_query.astype(BF), grad_key.astype(BF), grad_value], axis=1
        )
        grad_w_qkv = jnp.stack([dot_tn(rows, grad_qkv).astype(BF) for rows in input_rows])
        qkv_grads = grad_w_qkv.reshape(n_col, n_dp, in_rows, 3 * head_cols)
        qkv_sum = GroupSum(lambda index: lax.dynamic_index_in_dim(qkv_grads, index, 1, False))
        ordered_qkv = after(grad_qkv, grad_w_qkv)
        out_sum, ordered_qkv = out_sum.finish(ordered_qkv)
        out_all = give_back(lambda index: block_at(out_sum, index, features, 1))
        input_part = [sum_rows(row, dot_nt(ordered_qkv, w)) for w in w_qkv]
        qkv_sum, input_part = qkv_sum.finish(input_part)
        qkv_back = [col.fetch(qkv_sum[-k % n_col], k)[None] for k in range(n_col)]
        qkv_back, input_part = lax.optimization_barrier((qkv_back, input_part))
        qkv_all = gather_dp(assemble(col, qkv_back, 0)[None])
        own_state = grad_state.astype(BF)
        grad_input = reduce_col(col, input_part) + assemble(
            col,
            exchange(col, lambda index: block_at(own_state, index, features, 1)),
            0,
        ).astype(F32)

        def columns_of(whole, start, size):
            return jnp.concatenate(
                [
                    whole[:, k, :, start : start + size].reshape(features, size)
                    for k in range(n_col)
                ],
                axis=1,
            ).astype(F32)

        grad_w_down = down_all.swapaxes(0, 1).reshape(w_down.shape).astype(F32)
        grad_w_gate = columns_of(gate_up_all, 0, hidden_cols)
        grad_w_up = columns_of(gate_up_all, hidden_cols, hidden_cols)
        grad_w_out = out_all.swapaxes(0, 1).reshape(w_out.shape).astype(F32)
        grad_w_query = columns_of(qkv_all, 0, head_cols)
        grad_w_key = columns_of(qkv_all, head_cols, head_cols)
        grad_w_value = columns_of(qkv_all, 2 * head_cols, head_cols)

        small = jnp.stack([grad_gain_attn, grad_gain_ffn])
        pieces = exchange(col, lambda index: block_at(small, index, features, 1))
        small = sum(pieces[1:], pieces[0])
        total_small = small
        for j in range(1, n_row):
            total_small = total_small + row.fetch(small, j)
        gain_sums = lax.psum(
            (total_small, jnp.stack([grad_gain_query.reshape(-1), grad_gain_key.reshape(-1)])), "dp"
        )
        return (
            layer_output,
            grad_input,
            grad_w_query,
            grad_w_key,
            grad_w_value,
            grad_w_out,
            grad_w_gate,
            grad_w_up,
            grad_w_down,
            gain_sums[1][0],
            gain_sums[1][1],
            gain_sums[0][0],
            gain_sums[0][1],
        )

    return per_device


def solution(mesh):
    in_specs = (
        P(("dp", "row"), "col"),
        P("dp"),
        P("dp"),
        P("col", "row"),
        P("col", "row"),
        P("col", "row"),
        P("row", "col"),
        P("col", "row"),
        P("col", "row"),
        P("row", "col"),
        P(("row", "col")),
        P(("row", "col")),
        P("col"),
        P("col"),
        P(("dp", "row"), "col"),
    )
    out_specs = (
        P(("dp", "row"), "col"),
        P(("dp", "row"), "col"),
        P("col", "row"),
        P("col", "row"),
        P("col", "row"),
        P("row", "col"),
        P("col", "row"),
        P("col", "row"),
        P("row", "col"),
        P(("row", "col")),
        P(("row", "col")),
        P("col"),
        P("col"),
    )
    return jax.shard_map(
        device_program(dict(mesh.shape)),
        mesh=mesh,
        in_specs=in_specs,
        out_specs=out_specs,
        check_vma=False,
    )
```

time: 2470 us -> 993 us (0.40)
  waiting for transfers between devices: 2060 us -> 423 us
  starting transfers between devices: 1.97 us -> 193 us
  blocking collectives: 101 us -> 9.93 us
  local copies, waits for them, and re-layouts: 34.1 us -> 125 us
  matrix products: 161 us -> 107 us
    reduce_scatter x11 -> x0, waiting for transfers between devices: 1120 us -> none  [the longest x2 359 us: columns_sum(): return lax.psum_scatter(values, 'col', scatter_dimension=1, tiled=True)]
    all_gather x11 -> x8, waiting for transfers between devices: 649 us -> 22.6 us  [gather_dp(): return lax.all_gather(values, 'dp', axis=0, tiled=True)]
    ppermute x0 -> x128, waiting for transfers between devices: none -> 400 us  [the longest x32 190 us: send(): return lax.ppermute(values, self.name, pairs)]
    psum x1 -> x0, waiting for transfers between devices: 286 us -> none  [per_device(): lax.psum(grad_w_query.astype(jnp.bfloat16), 'dp').astype(jnp.float32)]
    ppermute x0 -> x128, starting transfers between devices: none -> 192 us  [the longest x80 88.8 us: fetch(): return lax.ppermute(values, self.name, pairs)]
    psum x8 -> x1, blocking collectives: 101 us -> 9.93 us  [per_device(): lax.psum((total_small, jnp.stack([grad_gain_query.reshape(-1), grad_gain_...]
    dot_general x35 -> x38, matrix products: 161 us -> 107 us  [the longest x7 39.9 us: dot_tn(): lax.dot_general(a, b, (((0,), (0,)), ((), ())), preferred_element_type=F32)]
    dynamic_update_slice x0 -> x39, local copies, waits for them, and re-layouts: none -> 28.5 us  [assemble(): lax.dynamic_update_slice_in_dim(whole, block, ring.at(step) * size, axis)]
  transfers between devices with their start and end apart: 23 -> 136, of which waited for: 22 -> 53; matrix products, arithmetic and copies ran while one was open for 4% -> 26% of each run, Pallas kernels for 0% -> 1%
where the time goes in v1:
time: 993 us; the launch traced here: 983 us
  waiting for transfers between devices  423 us (43%)
  starting transfers between devices  193 us (19%)
  local copies, waits for them, and re-layouts  125 us (13%)
  matrix products  107 us (11%)
  other arithmetic  86.6 us (9%)
  Pallas kernels  21.3 us (2%)
  between operations  17.6 us (2%)
  blocking collectives  9.93 us (1%)
    ppermute x32, waiting for transfers between devices, send(): return lax.ppermute(values, self.name, pairs)  190 us
    ppermute x80, waiting for transfers between devices, fetch(): return lax.ppermute(values, self.name, pairs)  145 us
    ppermute x80, starting transfers between devices, fetch(): return lax.ppermute(values, self.name, pairs)  88.8 us
    ppermute x32, starting transfers between devices, send(): return lax.ppermute(values, self.name, pairs)  85.2 us
    ppermute x16, waiting for transfers between devices, partner(): return lax.ppermute(values, 'dp', [(i, i ^ step) for i in range(n_dp)])  64.4 us
    unnamed x324, local copies, waits for them, and re-layouts  41.4 us
    dot_general x7, matrix products, dot_tn(): lax.dot_general(a, b, (((0,), (0,)), ((), ())), preferred_element_type=F32)  39.9 us
    dot_general x16, matrix products, dot(): return jnp.dot(a, b, preferred_element_type=F32)  38.2 us
  transfers between devices with their start and end apart: 136, of which 53 were waited for; matrix products, arithmetic and copies ran while one was open for 26% of the time, Pallas kernels for 1%

profile of v1, /device:TPU:0, one launch (start us, length us, event | category | flops | bytes accessed | tf_op | source)
XLA Modules:
  0.0 982.8 jit_solution(5242447951251252629)
XLA Ops:
  9.4 5.1 collective-permute-start.5
  19.8 11.3 %collective-permute-done.6 = bf16[128,768]{1,0:T(8,128)(2,1)S(1)} collective-permute-done((bf16[128,768]{1,0:T(8,128)(2,1)S(1)}, bf16[128,768]{1,0:T(8,128)(2,1)S(1)}, u32[]{:S(2)}, u32[]{:S(2)}) %collective-permute-start.6) | collective-permute-done | bytes 196640 | tf_op jit(solution)/shard_map/ppermute | solution.py:62
  36.5 5.4 collective-permute-start.3
  47.7 11.0 %collective-permute-done = bf16[512,512]{1,0:T(8,128)(2,1)S(1)} collective-permute-done((bf16[512,512]{1,0:T(8,128)(2,1)}, bf16[512,512]{1,0:T(8,128)(2,1)S(1)}, u32[]{:S(2)}, u32[]{:S(2)}) %collective-permute-start) | collective-permute-done | bytes 524320 | tf_op jit(solution)/shard_map/ppermute | solution.py:65
  62.6 11.8 %collective-permute-start.26 = (bf16[64,512]{1,0:T(8,128)(2,1)}, bf16[64,512]{1,0:T(8,128)(2,1)}, u32[]{:S(2)}, u32[]{:S(2)}) collective-permute-start(bf16[64,512]{1,0:T(8,128)(2,1)} %get-tuple-element.295), channel_id=1, source_target_pairs={{0,1},{1,2},{2,3},{3,0},{4,5},{5,6},{6,7},{7,4},{8,9},{9,10},{10,1... | collective-permute-start | bytes 196616 | tf_op jit(solution)/shard_map/ppermute | solution.py:62
  105.0 17.7 %collective-permute-done.13 = f32[2,1024]{1,0:T(2,128)} collective-permute-done((f32[2,1024]{1,0:T(2,128)}, f32[2,1024]{1,0:T(2,128)}, u32[]{:S(2)}, u32[]{:S(2)}) %collective-permute-start.13) | collective-permute-done | bytes 8224 | tf_op jit(solution)/shard_map/ppermute | solution.py:62
  126.6 7.2 collective-permute-done.19
  147.1 7.9 attend_forward.1
  168.4 10.8 %collective-permute-done.22 = bf16[128,2048]{1,0:T(8,128)(2,1)} collective-permute-done((bf16[128,2048]{1,0:T(8,128)(2,1)}, bf16[128,2048]{1,0:T(8,128)(2,1)}, u32[]{:S(2)}, u32[]{:S(2)}) %collective-permute-start.22) | collective-permute-done | bytes 524320 | tf_op jit(solution)/shard_map/ppermute | solution.py:62
  189.2 11.5 %collective-permute-start.35 = (f32[2,512]{1,0:T(2,128)}, f32[2,512]{1,0:T(2,128)}, u32[]{:S(2)}, u32[]{:S(2)}) collective-permute-start(f32[2,512]{1,0:T(2,128)} %get-tuple-element.359), channel_id=1, source_target_pairs={{0,3},{1,0},{2,1},{3,2},{4,7},{5,4},{6,5},{7,6},{8,11},{9,8},{10,9... | collective-permute-start | bytes 12296 | tf_op jit(solution)/shard_map/ppermute | solution.py:62
  253.1 18.3 %collective-permute-done.34 = bf16[128,2048]{1,0:T(8,128)(2,1)S(1)} collective-permute-done((bf16[128,2048]{1,0:T(8,128)(2,1)S(1)}, bf16[128,2048]{1,0:T(8,128)(2,1)S(1)}, u32[]{:S(2)}, u32[]{:S(2)}) %collective-permute-start.34) | collective-permute-done | bytes 524320 | tf_op jit(solution)/shard_map/ppermute | solution.py:65
  275.1 19.7 %collective-permute-done.40 = bf16[128,2048]{1,0:T(8,128)(2,1)S(1)} collective-permute-done((bf16[128,2048]{1,0:T(8,128)(2,1)S(1)}, bf16[128,2048]{1,0:T(8,128)(2,1)S(1)}, u32[]{:S(2)}, u32[]{:S(2)}) %collective-permute-start.40) | collective-permute-done | bytes 524320 | tf_op jit(solution)/shard_map/ppermute | solution.py:65
  296.2 10.2 %collective-permute-done.46 = bf16[128,2048]{1,0:T(8,128)(2,1)S(1)} collective-permute-done((bf16[128,2048]{1,0:T(8,128)(2,1)S(1)}, bf16[128,2048]{1,0:T(8,128)(2,1)S(1)}, u32[]{:S(2)}, u32[]{:S(2)}) %collective-permute-start.46) | collective-permute-done | bytes 524320 | tf_op jit(solution)/shard_map/ppermute | solution.py:65
  306.4 11.1 %collective-permute-done.41 = bf16[128,2048]{1,0:T(8,128)(2,1)S(1)} collective-permute-done((bf16[128,2048]{1,0:T(8,128)(2,1)S(1)}, bf16[128,2048]{1,0:T(8,128)(2,1)S(1)}, u32[]{:S(2)}, u32[]{:S(2)}) %collective-permute-start.41) | collective-permute-done | bytes 524320 | tf_op jit(solution)/shard_map/ppermute | solution.py:65
  321.2 10.0 %collective-permute-done.42 = bf16[128,2048]{1,0:T(8,128)(2,1)S(1)} collective-permute-done((bf16[128,2048]{1,0:T(8,128)(2,1)S(1)}, bf16[128,2048]{1,0:T(8,128)(2,1)S(1)}, u32[]{:S(2)}, u32[]{:S(2)}) %collective-permute-start.42) | collective-permute-done | bytes 524320 | tf_op jit(solution)/shard_map/ppermute | solution.py:65
  334.1 6.1 fusion.59
  346.9 6.3 fusion.55
  370.4 4.6 collective-permute-start.49
  384.8 8.0 collective-permute-done.45
  392.8 13.8 %collective-permute-done.53 = bf16[128,2048]{1,0:T(8,128)(2,1)S(1)} collective-permute-done((bf16[128,2048]{1,0:T(8,128)(2,1)S(1)}, bf16[128,2048]{1,0:T(8,128)(2,1)S(1)}, u32[]{:S(2)}, u32[]{:S(2)}) %collective-permute-start.53) | collective-permute-done | bytes 524320 | tf_op jit(solution)/shard_map/ppermute | solution.py:65
  413.1 8.5 collective-permute-start.63
  421.6 15.2 %collective-permute-done.58 = bf16[128,2048]{1,0:T(8,128)(2,1)} collective-permute-done((bf16[128,2048]{1,0:T(8,128)(2,1)}, bf16[128,2048]{1,0:T(8,128)(2,1)}, u32[]{:S(2)}, u32[]{:S(2)}) %collective-permute-start.58) | collective-permute-done | bytes 524320 | tf_op jit(solution)/shard_map/ppermute | solution.py:65
  438.1 4.6 multiply_convert_fusion.7
  475.8 25.2 %convolution_convert_fusion = bf16[2048,2048]{1,0:T(8,128)(2,1)} fusion(bf16[1024,2048]{1,0:T(8,128)(2,1)} %constant_dynamic-update-slice_fusion.8, bf16[256,1024]{1,0:T(8,128)(2,1)S(1)} %copy-done.146, bf16[256,1024]{1,0:T(8,128)(2,1)S(1)} %get-tuple-element.262, bf16[256,1024]{1,0:T(8,128)(2,1)S(1)} %get-tuple-element.265, ...), kind=kOutput, calls=%fused_computation | convolution fusion | flops 8627683328 | bytes 16777216 | tf_op jit(solution)/shard_map/dot_general | solution.py:50
  501.0 5.8 dynamic-slice_bitcast_fusion
  516.0 7.0 convolution_convert_fusion.1
  533.4 6.2 collective-permute-start.76
  545.9 19.5 %collective-permute-done.76 = bf16[128,2048]{1,0:T(8,128)(2,1)S(1)} collective-permute-done((bf16[128,2048]{1,0:T(8,128)(2,1)S(1)}, bf16[128,2048]{1,0:T(8,128)(2,1)S(1)}, u32[]{:S(2)}, u32[]{:S(2)}) %collective-permute-start.76) | collective-permute-done | bytes 524320 | tf_op jit(solution)/shard_map/ppermute | solution.py:65
  566.8 11.8 %collective-permute-done.68 = bf16[2,256,1024]{2,1,0:T(8,128)(2,1)S(1)} collective-permute-done((bf16[2,256,1024]{2,1,0:T(8,128)(2,1)S(1)}, bf16[2,256,1024]{2,1,0:T(8,128)(2,1)S(1)}, u32[]{:S(2)}, u32[]{:S(2)}) %collective-permute-start.68) | collective-permute-done | bytes 1048608 | tf_op jit(solution)/shard_map/ppermute | solution.py:431
  584.5 11.5 %collective-permute-done.79 = bf16[1,256,1024]{2,1,0:T(8,128)(2,1)S(1)} collective-permute-done((bf16[1,256,1024]{2,1,0:T(8,128)(2,1)S(1)}, bf16[1,256,1024]{2,1,0:T(8,128)(2,1)S(1)}, u32[]{:S(2)}, u32[]{:S(2)}) %collective-permute-start.79) | collective-permute-done | bytes 524320 | tf_op jit(solution)/shard_map/ppermute | solution.py:431
  604.5 7.7 collective-permute-start.87
  612.2 15.2 %collective-permute-done.82 = bf16[128,2048]{1,0:T(8,128)(2,1)} collective-permute-done((bf16[128,2048]{1,0:T(8,128)(2,1)}, bf16[128,2048]{1,0:T(8,128)(2,1)}, u32[]{:S(2)}, u32[]{:S(2)}) %collective-permute-start.82) | collective-permute-done | bytes 524320 | tf_op jit(solution)/shard_map/ppermute | solution.py:65
  642.8 8.5 collective-permute-done.78
  661.4 13.3 %attend_backward.1 = (f32[1024,256]{1,0:T(8,128)S(1)}, f32[1024,256]{1,0:T(8,128)S(1)}, bf16[1024,256]{1,0:T(8,128)(2,1)S(1)}, f32[2,1024,1]{2,1,0:T(8,128)S(1)}...) custom-call(f32[1024,768]{1,0:T(8,128)S(1)} %add_add_fusion.query_ref.key_ref.value_ref, ...), custom_call_target="tpu_custom_call" | custom-call | flops 2684354560 | bytes 7864320 | tf_op jit(solution)/shard_map/attend_backward/pallas_call | solution.py:369
  709.4 16.4 %collective-permute-done.97 = bf16[1,64,1024]{2,1,0:T(8,128)(2,1)S(1)} collective-permute-done((bf16[1,64,1024]{2,1,0:T(8,128)(2,1)S(1)}, bf16[1,64,1024]{2,1,0:T(8,128)(2,1)S(1)}, u32[]{:S(2)}, u32[]{:S(2)}) %collective-permute-start.97) | collective-permute-done | bytes 131104 | tf_op jit(solution)/shard_map/ppermute | solution.py:431
  744.3 7.7 collective-permute-done.104
  760.4 5.9 collective-permute-done.107
  766.8 8.6 collective-permute-done.106
  788.4 5.3 collective-permute-done.121
  794.4 12.4 %collective-permute-done.122 = bf16[256,512]{1,0:T(8,128)(2,1)S(1)} collective-permute-done((bf16[256,512]{1,0:T(8,128)(2,1)S(1)}, bf16[256,512]{1,0:T(8,128)(2,1)S(1)}, u32[]{:S(2)}, u32[]{:S(2)}) %collective-permute-start.122) | collective-permute-done | bytes 262176 | tf_op jit(solution)/shard_map/ppermute | solution.py:62
  815.8 5.8 collective-permute-done.118
  822.4 34.9 %collective-permute-done.119 = bf16[128,2048]{1,0:T(8,128)(2,1)S(1)} collective-permute-done((bf16[128,2048]{1,0:T(8,128)(2,1)S(1)}, bf16[128,2048]{1,0:T(8,128)(2,1)S(1)}, u32[]{:S(2)}, u32[]{:S(2)}) %collective-permute-start.119) | collective-permute-done | bytes 524320 | tf_op jit(solution)/shard_map/ppermute | solution.py:62
  873.4 7.8 collective-permute-done.113
  888.4 5.3 collective-permute-start.109
  896.5 9.9 %all-reduce = (f32[2,256]{1,0:T(2,128)S(1)}, f32[2,512]{1,0:T(2,128)S(1)}) all-reduce(f32[2,256]{1,0:T(2,128)S(1)} %pad_maximum_fusion.28, f32[2,512]{1,0:T(2,128)S(1)} %add.799), channel_id=1, replica_groups=mesh['dp'=4,'row'=2,'col'=4] {'dp'}, use_global_device_ids=true, to_apply=%region_8.9 | all-reduce | flops 1536 | bytes 12288 | tf_op jit(solution)/shard_map/psum | solution.py:699
  910.5 14.9 %collective-permute-done.111 = bf16[512,512]{1,0:T(8,128)(2,1)S(1)} collective-permute-done((bf16[512,512]{1,0:T(8,128)(2,1)}, bf16[512,512]{1,0:T(8,128)(2,1)S(1)}, u32[]{:S(2)}, u32[]{:S(2)}) %collective-permute-start.111) | collective-permute-done | bytes 524320 | tf_op jit(solution)/shard_map/ppermute | solution.py:65
  934.7 6.7 convert_element_type.785
  941.4 22.5 %all-gather.20.cloned.1.call-done = bf16[4,4,128,2048]{3,2,0,1:T(8,128)(2,1)} async-done(((bf16[1,4,128,2048]{3,2,0,1:T(8,128)(2,1)}), bf16[4,4,128,2048]{3,2,0,1:T(8,128)(2,1)}) %all-gather.20.cloned.1.call-update) | async-done | bytes 8388624 | tf_op jit(solution)/shard_map/all_gather | solution.py:426
  (819 shorter events, 432.9 us)
Async XLA Ops:
  7.2 76.5 %all-gather.24.cloned.1.call-start = ((), (), s32[]{:S(2)}) async-start(), calls=%async_computation.7 | async-start | bytes 3932160 | tf_op jit(solution)/shard_map/all_gather | solution.py:426
  32.2 127.7 %all-gather.10.cloned.1.call-start = ((), (), s32[]{:S(2)}) async-start(), calls=%async_computation | async-start | bytes 1310720 | tf_op jit(solution)/shard_map/all_gather | solution.py:426
  32.2 26.5 %collective-permute-start = (bf16[512,512]{1,0:T(8,128)(2,1)}, bf16[512,512]{1,0:T(8,128)(2,1)S(1)}, u32[]{:S(2)}, u32[]{:S(2)}) collective-permute-start(bf16[512,512]{1,0:T(8,128)(2,1)} %param.15), channel_id=1, source_target_pairs={{0,2},{1,3},{2,0},{3,1},{4,6},{5,7},{6,4},{7,5},{8,10},{9,11},{10,... | collective-permute-start | bytes 1572872 | tf_op jit(solution)/shard_map/ppermute | solution.py:65
  35.2 39.8 %collective-permute-start.2 = (bf16[512,512]{1,0:T(8,128)(2,1)}, bf16[512,512]{1,0:T(8,128)(2,1)S(1)}, u32[]{:S(2)}, u32[]{:S(2)}) collective-permute-start(bf16[512,512]{1,0:T(8,128)(2,1)} %param.15), channel_id=1, source_target_pairs={{1,0},{2,1},{3,2},{5,4},{6,5},{7,6},{9,8},{10,9},{11,10},{13,12},{... | collective-permute-start | bytes 1572872 | tf_op jit(solution)/shard_map/ppermute | solution.py:65
  36.5 38.5 %collective-permute-start.3 = (bf16[512,512]{1,0:T(8,128)(2,1)}, bf16[512,512]{1,0:T(8,128)(2,1)}, u32[]{:S(2)}, u32[]{:S(2)}) collective-permute-start(bf16[512,512]{1,0:T(8,128)(2,1)} %param.15), channel_id=1, source_target_pairs={{0,1},{1,2},{2,3},{4,5},{5,6},{6,7},{8,9},{9,10},{10,11},{12,13},{... | collective-permute-start | bytes 1572872 | tf_op jit(solution)/shard_map/ppermute | solution.py:65
  44.2 33.8 %collective-permute-start.25 = (bf16[64,512]{1,0:T(8,128)(2,1)S(1)}, bf16[64,512]{1,0:T(8,128)(2,1)S(1)}, u32[]{:S(2)}, u32[]{:S(2)}) collective-permute-start(bf16[64,512]{1,0:T(8,128)(2,1)S(1)} %get-tuple-element.298), channel_id=1, source_target_pairs={{0,2},{1,3},{2,0},{3,1},{4,6},{5,7},{6,4},{7,5},{8,10},{9,11},{10,... | collective-permute-start | bytes 196616 | tf_op jit(solution)/shard_map/ppermute | solution.py:62
  62.6 36.5 %collective-permute-start.26 = (bf16[64,512]{1,0:T(8,128)(2,1)}, bf16[64,512]{1,0:T(8,128)(2,1)}, u32[]{:S(2)}, u32[]{:S(2)}) collective-permute-start(bf16[64,512]{1,0:T(8,128)(2,1)} %get-tuple-element.295), channel_id=1, source_target_pairs={{0,1},{1,2},{2,3},{3,0},{4,5},{5,6},{6,7},{7,4},{8,9},{9,10},{10,1... | collective-permute-start | bytes 196616 | tf_op jit(solution)/shard_map/ppermute | solution.py:62
  95.6 38.2 %collective-permute-start.15 = (bf16[256,512]{1,0:T(8,128)(2,1)}, bf16[256,512]{1,0:T(8,128)(2,1)}, u32[]{:S(2)}, u32[]{:S(2)}) collective-permute-start(bf16[256,512]{1,0:T(8,128)(2,1)} %get-tuple-element.240), channel_id=1, source_target_pairs={{0,3},{1,0},{2,1},{3,2},{4,7},{5,4},{6,5},{7,6},{8,11},{9,8},{10,9... | collective-permute-start | bytes 786440 | tf_op jit(solution)/shard_map/ppermute | solution.py:62
  98.1 35.7 %collective-permute-start.16 = (bf16[256,512]{1,0:T(8,128)(2,1)}, bf16[256,512]{1,0:T(8,128)(2,1)}, u32[]{:S(2)}, u32[]{:S(2)}) collective-permute-start(bf16[256,512]{1,0:T(8,128)(2,1)} %get-tuple-element.239), channel_id=1, source_target_pairs={{0,2},{1,3},{2,0},{3,1},{4,6},{5,7},{6,4},{7,5},{8,10},{9,11},{10,... | collective-permute-start | bytes 786440 | tf_op jit(solution)/shard_map/ppermute | solution.py:62
  99.1 34.7 %collective-permute-start.17 = (bf16[256,512]{1,0:T(8,128)(2,1)}, bf16[256,512]{1,0:T(8,128)(2,1)}, u32[]{:S(2)}, u32[]{:S(2)}) collective-permute-start(bf16[256,512]{1,0:T(8,128)(2,1)} %get-tuple-element.238), channel_id=1, source_target_pairs={{0,1},{1,2},{2,3},{3,0},{4,5},{5,6},{6,7},{7,4},{8,9},{9,10},{10,1... | collective-permute-start | bytes 786440 | tf_op jit(solution)/shard_map/ppermute | solution.py:62
  105.0 229.1 %all-gather.12.cloned.1.call-start = ((), (), s32[]{:S(2)}) async-start(), calls=%async_computation.1 | async-start | bytes 10485760 | tf_op jit(solution)/shard_map/all_gather | solution.py:426
  141.4 27.0 %collective-permute-start.23 = (bf16[128,2048]{1,0:T(8,128)(2,1)}, bf16[128,2048]{1,0:T(8,128)(2,1)}, u32[]{:S(2)}, u32[]{:S(2)}) collective-permute-start(bf16[128,2048]{1,0:T(8,128)(2,1)} %pad_maximum_fusion.18), channel_id=1, source_target_pairs={{0,1},{1,2},{2,3},{3,0},{4,5},{5,6},{6,7},{7,4},{8,9},{9,10},{10,1... | collective-permute-start | bytes 1572872 | tf_op jit(solution)/shard_map/ppermute | solution.py:62
  142.2 37.0 %collective-permute-start.22 = (bf16[128,2048]{1,0:T(8,128)(2,1)}, bf16[128,2048]{1,0:T(8,128)(2,1)}, u32[]{:S(2)}, u32[]{:S(2)}) collective-permute-start(bf16[128,2048]{1,0:T(8,128)(2,1)} %pad_maximum_fusion.17), channel_id=1, source_target_pairs={{0,2},{1,3},{2,0},{3,1},{4,6},{5,7},{6,4},{7,5},{8,10},{9,11},{10,... | collective-permute-start | bytes 1572872 | tf_op jit(solution)/shard_map/ppermute | solution.py:62
  143.8 35.4 %collective-permute-start.21 = (bf16[128,2048]{1,0:T(8,128)(2,1)}, bf16[128,2048]{1,0:T(8,128)(2,1)}, u32[]{:S(2)}, u32[]{:S(2)}) collective-permute-start(bf16[128,2048]{1,0:T(8,128)(2,1)} %pad_maximum_fusion.16), channel_id=1, source_target_pairs={{0,3},{1,0},{2,1},{3,2},{4,7},{5,4},{6,5},{7,6},{8,11},{9,8},{10,9... | collective-permute-start | bytes 1572872 | tf_op jit(solution)/shard_map/ppermute | solution.py:62
  187.2 155.4 %all-gather.14.cloned.1.call-start = ((), (), s32[]{:S(2)}) async-start(), calls=%async_computation.2 | async-start | bytes 5242880 | tf_op jit(solution)/shard_map/all_gather | solution.py:426
  232.9 674.8 %all-gather.18.cloned.1.call-start = ((), (), s32[]{:S(2)}) async-start(), calls=%async_computation.4 | async-start | bytes 1310720 | tf_op jit(solution)/shard_map/all_gather | solution.py:426
  242.3 29.1 %collective-permute-start.34 = (bf16[128,2048]{1,0:T(8,128)(2,1)S(1)}, bf16[128,2048]{1,0:T(8,128)(2,1)S(1)}, u32[]{:S(2)}, u32[]{:S(2)}) collective-permute-start(bf16[128,2048]{1,0:T(8,128)(2,1)S(1)} %add_convert_fusion.2), channel_id=1, source_target_pairs={{0,2},{1,3},{2,0},{3,1},{4,6},{5,7},{6,4},{7,5},{8,10},{9,11},{10,... | collective-permute-start | bytes 1572872 | tf_op jit(solution)/shard_map/ppermute | solution.py:65
  273.7 22.4 %collective-permute-start.38 = (bf16[128,2048]{1,0:T(8,128)(2,1)S(1)}, bf16[128,2048]{1,0:T(8,128)(2,1)S(1)}, u32[]{:S(2)}, u32[]{:S(2)}) collective-permute-start(bf16[128,2048]{1,0:T(8,128)(2,1)S(1)} %get-tuple-element.190), channel_id=1, source_target_pairs={{0,4},{4,0},{1,5},{5,1},{2,6},{6,2},{3,7},{7,3},{8,12},{12,8},{9,1... | collective-permute-start | bytes 1572872 | tf_op jit(solution)/shard_map/ppermute | solution.py:62
  273.8 32.6 %collective-permute-start.46 = (bf16[128,2048]{1,0:T(8,128)(2,1)S(1)}, bf16[128,2048]{1,0:T(8,128)(2,1)S(1)}, u32[]{:S(2)}, u32[]{:S(2)}) collective-permute-start(bf16[128,2048]{1,0:T(8,128)(2,1)S(1)} %get-tuple-element.190), channel_id=1, source_target_pairs={{1,0},{2,1},{3,2},{5,4},{6,5},{7,6},{9,8},{10,9},{11,10},{13,12},{... | collective-permute-start | bytes 1572872 | tf_op jit(solution)/shard_map/ppermute | solution.py:65
  294.8 22.7 %collective-permute-start.41 = (bf16[128,2048]{1,0:T(8,128)(2,1)S(1)}, bf16[128,2048]{1,0:T(8,128)(2,1)S(1)}, u32[]{:S(2)}, u32[]{:S(2)}) collective-permute-start(bf16[128,2048]{1,0:T(8,128)(2,1)S(1)} %collective-permute-done.40), channel_id=1, source_target_pairs={{2,3},{1,0},{6,7},{5,4},{10,11},{9,8},{14,15},{13,12},{18,19},{17,... | collective-permute-start | bytes 1572872 | tf_op jit(solution)/shard_map/ppermute | solution.py:65
  369.1 23.7 %collective-permute-start.45 = (bf16[128,2048]{1,0:T(8,128)(2,1)S(1)}, bf16[128,2048]{1,0:T(8,128)(2,1)S(1)}, u32[]{:S(2)}, u32[]{:S(2)}) collective-permute-start(bf16[128,2048]{1,0:T(8,128)(2,1)S(1)} %get-tuple-element.203), channel_id=1, source_target_pairs={{1,0},{2,1},{3,2},{5,4},{6,5},{7,6},{9,8},{10,9},{11,10},{13,12},{... | collective-permute-start | bytes 1572872 | tf_op jit(solution)/shard_map/ppermute | solution.py:65
  370.4 22.4 %collective-permute-start.49 = (bf16[128,2048]{1,0:T(8,128)(2,1)S(1)}, bf16[128,2048]{1,0:T(8,128)(2,1)S(1)}, u32[]{:S(2)}, u32[]{:S(2)}) collective-permute-start(bf16[128,2048]{1,0:T(8,128)(2,1)S(1)} %get-tuple-element.204), channel_id=1, source_target_pairs={{0,1},{1,2},{2,3},{4,5},{5,6},{6,7},{8,9},{9,10},{10,11},{12,13},{... | collective-permute-start | bytes 1572872 | tf_op jit(solution)/shard_map/ppermute | solution.py:65
  379.7 26.9 %collective-permute-start.53 = (bf16[128,2048]{1,0:T(8,128)(2,1)S(1)}, bf16[128,2048]{1,0:T(8,128)(2,1)S(1)}, u32[]{:S(2)}, u32[]{:S(2)}) collective-permute-start(bf16[128,2048]{1,0:T(8,128)(2,1)S(1)} %fusion.45), channel_id=1, source_target_pairs={{0,2},{1,3},{2,0},{3,1},{4,6},{5,7},{6,4},{7,5},{8,10},{9,11},{10,... | collective-permute-start | bytes 1572872 | tf_op jit(solution)/shard_map/ppermute | solution.py:65
  409.4 27.4 %collective-permute-start.58 = (bf16[128,2048]{1,0:T(8,128)(2,1)}, bf16[128,2048]{1,0:T(8,128)(2,1)}, u32[]{:S(2)}, u32[]{:S(2)}) collective-permute-start(bf16[128,2048]{1,0:T(8,128)(2,1)} %get-tuple-element.199), channel_id=1, source_target_pairs={{0,2},{1,3},{2,0},{3,1},{4,6},{5,7},{6,4},{7,5},{8,10},{9,11},{10,... | collective-permute-start | bytes 1572872 | tf_op jit(solution)/shard_map/ppermute | solution.py:65
  409.4 28.6 %collective-permute-start.57 = (bf16[128,2048]{1,0:T(8,128)(2,1)}, bf16[128,2048]{1,0:T(8,128)(2,1)}, u32[]{:S(2)}, u32[]{:S(2)}) collective-permute-start(bf16[128,2048]{1,0:T(8,128)(2,1)} %get-tuple-element.199), channel_id=1, source_target_pairs={{0,4},{4,0},{1,5},{5,1},{2,6},{6,2},{3,7},{7,3},{8,12},{12,8},{9,1... | collective-permute-start | bytes 1572872 | tf_op jit(solution)/shard_map/ppermute | solution.py:62
  411.5 37.1 %collective-permute-start.60 = (bf16[128,2048]{1,0:T(8,128)(2,1)}, bf16[128,2048]{1,0:T(8,128)(2,1)S(1)}, u32[]{:S(2)}, u32[]{:S(2)}) collective-permute-start(bf16[128,2048]{1,0:T(8,128)(2,1)} %get-tuple-element.199), channel_id=1, source_target_pairs={{1,0},{2,1},{3,2},{5,4},{6,5},{7,6},{9,8},{10,9},{11,10},{13,12},{... | collective-permute-start | bytes 1572872 | tf_op jit(solution)/shard_map/ppermute | solution.py:65
  413.1 49.9 %collective-permute-start.63 = (bf16[128,2048]{1,0:T(8,128)(2,1)}, bf16[128,2048]{1,0:T(8,128)(2,1)S(1)}, u32[]{:S(2)}, u32[]{:S(2)}) collective-permute-start(bf16[128,2048]{1,0:T(8,128)(2,1)} %get-tuple-element.199), channel_id=1, source_target_pairs={{0,1},{1,2},{2,3},{4,5},{5,6},{6,7},{8,9},{9,10},{10,11},{12,13},{... | collective-permute-start | bytes 1572872 | tf_op jit(solution)/shard_map/ppermute | solution.py:65
  446.0 87.4 %collective-permute-start.69 = (bf16[128,2048]{1,0:T(8,128)(2,1)}, bf16[128,2048]{1,0:T(8,128)(2,1)}, u32[]{:S(2)}, u32[]{:S(2)}) collective-permute-start(bf16[128,2048]{1,0:T(8,128)(2,1)} %split.239), channel_id=1, source_target_pairs={{0,4},{4,0},{1,5},{5,1},{2,6},{6,2},{3,7},{7,3},{8,12},{12,8},{9,1... | collective-permute-start | bytes 1572872 | tf_op jit(solution)/shard_map/ppermute | solution.py:62
  458.8 64.7 %collective-permute-start.74 = (bf16[128,2048]{1,0:T(8,128)(2,1)}, bf16[128,2048]{1,0:T(8,128)(2,1)}, u32[]{:S(2)}, u32[]{:S(2)}) collective-permute-start(bf16[128,2048]{1,0:T(8,128)(2,1)} %split.236), channel_id=1, source_target_pairs={{0,4},{4,0},{1,5},{5,1},{2,6},{6,2},{3,7},{7,3},{8,12},{12,8},{9,1... | collective-permute-start | bytes 1572872 | tf_op jit(solution)/shard_map/ppermute | solution.py:62
  468.9 42.5 %collective-permute-start.72 = (bf16[128,2048]{1,0:T(8,128)(2,1)}, bf16[128,2048]{1,0:T(8,128)(2,1)}, u32[]{:S(2)}, u32[]{:S(2)}) collective-permute-start(bf16[128,2048]{1,0:T(8,128)(2,1)} %split.237), channel_id=1, source_target_pairs={{0,4},{4,0},{1,5},{5,1},{2,6},{6,2},{3,7},{7,3},{8,12},{12,8},{9,1... | collective-permute-start | bytes 1572872 | tf_op jit(solution)/shard_map/ppermute | solution.py:62
  508.5 76.0 %collective-permute-start.66 = (bf16[2,4,128,1024]{3,2,1,0:T(8,128)(2,1)S(1)}, bf16[2,4,128,1024]{3,2,1,0:T(8,128)(2,1)S(1)}, u32[]{:S(2)}, u32[]{:S(2)}) collective-permute-start(bf16[2,4,128,1024]{3,2,1,0:T(8,128)(2,1)S(1)} %pad_maximum_fusion.2), channel_id=1, source_target_pairs={{0,16},{8,24},{16,0},{24,8},{1,17},{9,25},{17,1},{25,9},{2,18},{10... | collective-permute-start | bytes 6291464 | tf_op jit(solution)/shard_map/ppermute | solution.py:431
  511.4 73.1 %collective-permute-start.65 = (bf16[2,4,128,1024]{3,2,1,0:T(8,128)(2,1)S(1)}, bf16[2,4,128,1024]{3,2,1,0:T(8,128)(2,1)S(1)}, u32[]{:S(2)}, u32[]{:S(2)}) collective-permute-start(bf16[2,4,128,1024]{3,2,1,0:T(8,128)(2,1)S(1)} %pad_maximum_fusion.1), channel_id=1, source_target_pairs={{0,8},{8,0},{16,24},{24,16},{1,9},{9,1},{17,25},{25,17},{2,10},{10... | collective-permute-start | bytes 6291464 | tf_op jit(solution)/shard_map/ppermute | solution.py:431
  533.4 32.1 %collective-permute-start.76 = (bf16[128,2048]{1,0:T(8,128)(2,1)S(1)}, bf16[128,2048]{1,0:T(8,128)(2,1)S(1)}, u32[]{:S(2)}, u32[]{:S(2)}) collective-permute-start(bf16[128,2048]{1,0:T(8,128)(2,1)S(1)} %fusion.38), channel_id=1, source_target_pairs={{0,2},{1,3},{2,0},{3,1},{4,6},{5,7},{6,4},{7,5},{8,10},{9,11},{10,... | collective-permute-start | bytes 1572872 | tf_op jit(solution)/shard_map/ppermute | solution.py:65
  539.7 38.9 %collective-permute-start.68 = (bf16[2,256,1024]{2,1,0:T(8,128)(2,1)S(1)}, bf16[2,256,1024]{2,1,0:T(8,128)(2,1)S(1)}, u32[]{:S(2)}, u32[]{:S(2)}) collective-permute-start(bf16[2,256,1024]{2,1,0:T(8,128)(2,1)S(1)} %pad_maximum_fusion.6), channel_id=1, source_target_pairs={{0,16},{8,24},{16,0},{24,8},{1,17},{9,25},{17,1},{25,9},{2,18},{10... | collective-permute-start | bytes 3145736 | tf_op jit(solution)/shard_map/ppermute | solution.py:431
  544.5 37.5 %collective-permute-start.67 = (bf16[2,256,1024]{2,1,0:T(8,128)(2,1)S(1)}, bf16[2,256,1024]{2,1,0:T(8,128)(2,1)S(1)}, u32[]{:S(2)}, u32[]{:S(2)}) collective-permute-start(bf16[2,256,1024]{2,1,0:T(8,128)(2,1)S(1)} %pad_maximum_fusion.5), channel_id=1, source_target_pairs={{0,8},{8,0},{16,24},{24,16},{1,9},{9,1},{17,25},{25,17},{2,10},{10... | collective-permute-start | bytes 3145736 | tf_op jit(solution)/shard_map/ppermute | solution.py:431
  600.1 27.4 %collective-permute-start.82 = (bf16[128,2048]{1,0:T(8,128)(2,1)}, bf16[128,2048]{1,0:T(8,128)(2,1)}, u32[]{:S(2)}, u32[]{:S(2)}) collective-permute-start(bf16[128,2048]{1,0:T(8,128)(2,1)} %get-tuple-element.281), channel_id=1, source_target_pairs={{0,2},{1,3},{2,0},{3,1},{4,6},{5,7},{6,4},{7,5},{8,10},{9,11},{10,... | collective-permute-start | bytes 1572872 | tf_op jit(solution)/shard_map/ppermute | solution.py:65
  603.0 32.5 %collective-permute-start.84 = (bf16[128,2048]{1,0:T(8,128)(2,1)}, bf16[128,2048]{1,0:T(8,128)(2,1)S(1)}, u32[]{:S(2)}, u32[]{:S(2)}) collective-permute-start(bf16[128,2048]{1,0:T(8,128)(2,1)} %get-tuple-element.281), channel_id=1, source_target_pairs={{1,0},{2,1},{3,2},{5,4},{6,5},{7,6},{9,8},{10,9},{11,10},{13,12},{... | collective-permute-start | bytes 1572872 | tf_op jit(solution)/shard_map/ppermute | solution.py:65
  604.5 31.1 %collective-permute-start.87 = (bf16[128,2048]{1,0:T(8,128)(2,1)}, bf16[128,2048]{1,0:T(8,128)(2,1)S(1)}, u32[]{:S(2)}, u32[]{:S(2)}) collective-permute-start(bf16[128,2048]{1,0:T(8,128)(2,1)} %get-tuple-element.281), channel_id=1, source_target_pairs={{0,1},{1,2},{2,3},{4,5},{5,6},{6,7},{8,9},{9,10},{10,11},{12,13},{... | collective-permute-start | bytes 1572872 | tf_op jit(solution)/shard_map/ppermute | solution.py:65
  704.9 35.0 %collective-permute-start.94 = (bf16[2,4,128,384]{3,2,1,0:T(8,128)(2,1)S(1)}, bf16[2,4,128,384]{3,2,1,0:T(8,128)(2,1)S(1)}, u32[]{:S(2)}, u32[]{:S(2)}) collective-permute-start(bf16[2,4,128,384]{3,2,1,0:T(8,128)(2,1)S(1)} %pad_maximum_fusion.14), channel_id=1, source_target_pairs={{0,16},{8,24},{16,0},{24,8},{1,17},{9,25},{17,1},{25,9},{2,18},{10... | collective-permute-start | bytes 2359304 | tf_op jit(solution)/shard_map/ppermute | solution.py:431
  707.9 32.1 %collective-permute-start.93 = (bf16[2,4,128,384]{3,2,1,0:T(8,128)(2,1)S(1)}, bf16[2,4,128,384]{3,2,1,0:T(8,128)(2,1)S(1)}, u32[]{:S(2)}, u32[]{:S(2)}) collective-permute-start(bf16[2,4,128,384]{3,2,1,0:T(8,128)(2,1)S(1)} %pad_maximum_fusion.13), channel_id=1, source_target_pairs={{0,8},{8,0},{16,24},{24,16},{1,9},{9,1},{17,25},{25,17},{2,10},{10... | collective-permute-start | bytes 2359304 | tf_op jit(solution)/shard_map/ppermute | solution.py:431
  744.2 183.6 %all-gather.16.cloned.1.call-start = ((), (), s32[]{:S(2)}) async-start(), calls=%async_computation.3 | async-start | bytes 3932160 | tf_op jit(solution)/shard_map/all_gather | solution.py:426
  776.5 158.2 %all-gather.22.cloned.1.call-start = ((), (), s32[]{:S(2)}) async-start(), calls=%async_computation.6 | async-start | bytes 5242880 | tf_op jit(solution)/shard_map/all_gather | solution.py:426
  808.3 155.7 %all-gather.20.cloned.1.call-start = ((), (), s32[]{:S(2)}) async-start(), calls=%async_computation.5 | async-start | bytes 10485760 | tf_op jit(solution)/shard_map/all_gather | solution.py:426
  808.6 48.7 %collective-permute-start.119 = (bf16[128,2048]{1,0:T(8,128)(2,1)S(1)}, bf16[128,2048]{1,0:T(8,128)(2,1)S(1)}, u32[]{:S(2)}, u32[]{:S(2)}) collective-permute-start(bf16[128,2048]{1,0:T(8,128)(2,1)S(1)} %get-tuple-element.273), channel_id=1, source_target_pairs={{0,2},{1,3},{2,0},{3,1},{4,6},{5,7},{6,4},{7,5},{8,10},{9,11},{10,... | collective-permute-start | bytes 1572872 | tf_op jit(solution)/shard_map/ppermute | solution.py:62
  813.9 44.3 %collective-permute-start.120 = (bf16[128,2048]{1,0:T(8,128)(2,1)S(1)}, bf16[128,2048]{1,0:T(8,128)(2,1)S(1)}, u32[]{:S(2)}, u32[]{:S(2)}) collective-permute-start(bf16[128,2048]{1,0:T(8,128)(2,1)S(1)} %get-tuple-element.272), channel_id=1, source_target_pairs={{0,1},{1,2},{2,3},{3,0},{4,5},{5,6},{6,7},{7,4},{8,9},{9,10},{10,1... | collective-permute-start | bytes 1572872 | tf_op jit(solution)/shard_map/ppermute | solution.py:62
  887.1 23.4 %collective-permute-start.108 = (bf16[512,512]{1,0:T(8,128)(2,1)S(1)}, bf16[512,512]{1,0:T(8,128)(2,1)}, u32[]{:S(2)}, u32[]{:S(2)}) collective-permute-start(bf16[512,512]{1,0:T(8,128)(2,1)S(1)} %copy-done.71), channel_id=1, source_target_pairs={{1,0},{2,1},{3,2},{5,4},{6,5},{7,6},{9,8},{10,9},{11,10},{13,12},{... | collective-permute-start | bytes 1572872 | tf_op jit(solution)/shard_map/ppermute | solution.py:65
  888.4 22.1 %collective-permute-start.109 = (bf16[512,512]{1,0:T(8,128)(2,1)S(1)}, bf16[512,512]{1,0:T(8,128)(2,1)}, u32[]{:S(2)}, u32[]{:S(2)}) collective-permute-start(bf16[512,512]{1,0:T(8,128)(2,1)S(1)} %copy-done.72), channel_id=1, source_target_pairs={{0,1},{1,2},{2,3},{4,5},{5,6},{6,7},{8,9},{9,10},{10,11},{12,13},{... | collective-permute-start | bytes 1572872 | tf_op jit(solution)/shard_map/ppermute | solution.py:65
  894.7 30.6 %collective-permute-start.111 = (bf16[512,512]{1,0:T(8,128)(2,1)}, bf16[512,512]{1,0:T(8,128)(2,1)S(1)}, u32[]{:S(2)}, u32[]{:S(2)}) collective-permute-start(bf16[512,512]{1,0:T(8,128)(2,1)} %add_convert_fusion), channel_id=1, source_target_pairs={{0,2},{1,3},{2,0},{3,1},{4,6},{5,7},{6,4},{7,5},{8,10},{9,11},{10,... | collective-permute-start | bytes 1572872 | tf_op jit(solution)/shard_map/ppermute | solution.py:65
  (239 other events, 2402.4 us)
Sparse Core Ops, SparseCore 0:
  32.3 44.5 all-gather.23
  105.1 25.7 all-gather.9
  187.4 96.8 all-gather.11
  286.5 52.6 all-gather.13
  744.4 25.1 all-gather.17
  776.6 41.9 all-gather.15
  821.0 52.6 all-gather.21
  876.2 87.7 all-gather.19

commit v2 on v1

v2 whole, which is shorter than its diff:
```python
import functools
import math

import jax
import jax.numpy as jnp
from jax import lax
from jax.experimental import pallas as pl
from jax.experimental.pallas import tpu as pltpu
from jax.sharding import PartitionSpec as P

HEAD = 128
EPSILON = 1e-06
ROPE_BASE = 500000.0
MASKED = -1e30
BF = jnp.bfloat16
F32 = jnp.float32


def rope_tables(positions):
    digit = 32
    frequency = ROPE_BASE ** (-(jnp.arange(HEAD // 2, dtype=F32) * (2.0 / HEAD)))
    frequency = jnp.concatenate([frequency, frequency])

    def looked_up(index, count, unit):
        angles = (jnp.arange(count) * unit).astype(F32)[:, None] * frequency[None, :]
        table = jnp.concatenate([jnp.cos(angles), jnp.sin(angles)], axis=1)
        chosen = (index[:, None] == jnp.arange(count)[None, :]).astype(F32)
        both = jnp.dot(chosen, table, precision=lax.Precision.HIGHEST)
        return both[:, :HEAD], both[:, HEAD:]

    high_cosine, high_sine = looked_up(
        positions // digit, -(-positions.shape[0] // digit), digit
    )
    low_cosine, low_sine = looked_up(positions % digit, digit, 1)
    signs = jnp.where(jnp.arange(HEAD) < HEAD // 2, -1.0, 1.0).astype(F32)[None, :]
    return (
        high_cosine * low_cosine - high_sine * low_sine,
        (high_sine * low_cosine + high_cosine * low_sine) * signs,
    )


def dot(a, b):
    return jnp.dot(a, b, preferred_element_type=F32)


def dot_nt(a, b):
    return lax.dot_general(a, b, (((1,), (1,)), ((), ())), preferred_element_type=F32)


def dot_tn(a, b):
    return lax.dot_general(a, b, (((0,), (0,)), ((), ())), preferred_element_type=F32)


class Ring:
    def __init__(self, name, size):
        self.name, self.size = name, size
        self.here = lax.axis_index(name)

    def fetch(self, values, step):
        if step % self.size == 0:
            return values
        pairs = [(i, (i - step) % self.size) for i in range(self.size)]
        return lax.ppermute(values, self.name, pairs)

    def send(self, values, pairs):
        return lax.ppermute(values, self.name, pairs)

    def give(self, values, step):
        return self.fetch(values, -step)

    def at(self, step):
        return lax.rem(self.here + (step % self.size), self.size)


def after(values, *earlier):
    return lax.optimization_barrier((values, earlier))[0]


def gather_steps(col, values, early=(), beside=()):
    two = col.send(values, [(0, 2), (1, 3), (2, 0), (3, 1)])
    below = col.send(values, [(0, 1), (1, 2), (2, 3)])
    above = col.send(values, [(1, 0), (2, 1), (3, 2)])
    two, early = lax.optimization_barrier((two, early))
    beside = beside(early) if callable(beside) else beside
    two, below, above, beside = lax.optimization_barrier((two, below, above, beside))
    relayed = col.send(two, [(2, 3), (1, 0)])
    return two, below, above, relayed, early, beside


def gather_col(col, values, early, beside):
    if col.size != 4:
        return [col.fetch(values, k) for k in range(col.size)], early, beside
    two, below, above, relayed, early, beside = gather_steps(col, values, early, beside)
    near = [
        values,
        jnp.where(col.here == 3, relayed, above),
        two,
        jnp.where(col.here == 0, relayed, below),
    ]
    return near, early, beside


def by_arrival(col, blocks):
    if col.size != 4:
        return blocks
    last = col.here == 3
    return [
        blocks[0],
        jnp.where(last, blocks[3], blocks[1]),
        blocks[2],
        jnp.where(last, blocks[1], blocks[3]),
    ]


def gather_near(col, values, early=(), beside=()):
    if col.size != 4:
        beside = beside(early) if callable(beside) else beside
        return [col.fetch(values, k) for k in range(col.size)], early, beside
    two, below, above, relayed, early, beside = gather_steps(col, values, early, beside)
    inside = (col.here == 1) | (col.here == 2)
    near = [
        values,
        jnp.where(col.here == 3, below, above),
        two,
        jnp.where(inside, below, relayed),
    ]
    return near, early, beside


def reduce_near(col, blocks, between=()):
    low = [block.astype(BF) for block in blocks]
    result = blocks[0]
    if col.size != 4:
        for k in range(1, col.size):
            result = result + col.give(low[k], k).astype(F32)
        return result, between
    relayed = col.send(low[3], [(3, 2), (0, 1)])
    below = col.send(low[1], [(0, 1), (1, 2), (2, 3)])
    above = col.send(
        jnp.where(col.here == 3, low[1], low[3]), [(1, 0), (2, 1), (3, 2)]
    )
    two = (blocks[2] + relayed.astype(F32)).astype(BF)
    two, between = lax.optimization_barrier((two, between))
    two = col.send(two, [(0, 2), (1, 3), (2, 0), (3, 1)])
    return result + above.astype(F32) + below.astype(F32) + two.astype(F32), between


def block_at(values, index, size, axis):
    return lax.dynamic_slice_in_dim(values, index * size, size, axis)


def assemble_kernel(here_ref, *refs):
    blocks, whole = refs[:-1], refs[-1]
    for step, block in enumerate(blocks):

        @pl.when(pl.program_id(0) == step)
        def _():
            whole[...] = block[...]


def assemble(ring, blocks, axis):
    shape = list(blocks[0].shape)
    size = len(blocks)
    zeros = (0,) * len(shape)

    def place(step, here):
        return zeros[:axis] + (lax.rem(here[0] + step, size),) + zeros[axis + 1 :]

    block_shape = tuple(shape)
    shape[axis] *= size
    return pl.pallas_call(
        assemble_kernel,
        grid_spec=pltpu.PrefetchScalarGridSpec(
            num_scalar_prefetch=1,
            grid=(size,),
            in_specs=[pl.BlockSpec(block_shape, lambda step, here: zeros)] * size,
            out_specs=pl.BlockSpec(block_shape, place),
        ),
        out_shape=jax.ShapeDtypeStruct(tuple(shape), blocks[0].dtype),
        compiler_params=pltpu.CompilerParams(vmem_limit_bytes=32 << 20),
        cost_estimate=pl.CostEstimate(
            flops=0,
            bytes_accessed=2 * math.prod(shape) * blocks[0].dtype.itemsize,
            transcendentals=0,
        ),
        name="assemble",
    )(ring.here.astype(jnp.int32)[None], *blocks)


def first_weights_kernel(sizes, places_ref, *refs):
    pieces, (in_ref, out_ref) = refs[:-2], refs[-2:]
    n_col, n_out, out_rows, wide = sizes
    features = out_ref.shape[1] // n_col
    narrow = features // n_out

    def store(piece, first):
        for k in range(piece.shape[0]):
            in_ref[first + k] = piece[k, :, :wide]
            start = lax.rem(places_ref[1] + first + k, n_col) * features
            for i in range(n_out):
                place = pl.multiple_of(start + i * narrow, narrow)
                out_ref[:, pl.ds(place, narrow)] = piece[
                    k, i * out_rows : (i + 1) * out_rows, wide:
                ]

    for d in range(3):

        @pl.when(pl.program_id(0) == d)
        def _():
            store(pieces[d], 0)

    @pl.when(pl.program_id(0) == 3)
    def _():
        store(pieces[3], 0)
        store(pieces[4], pieces[3].shape[0])


def first_weights(dp, here, pieces, wide, n_out):
    n_col, in_rows, columns = pieces[0].shape
    out_rows = in_rows // n_out
    features = n_out * (columns - wide)
    whole = [
        pl.BlockSpec(piece.shape, lambda step, places: (0, 0, 0)) for piece in pieces
    ]
    return pl.pallas_call(
        functools.partial(first_weights_kernel, (n_col, n_out, out_rows, wide)),
        grid_spec=pltpu.PrefetchScalarGridSpec(
            num_scalar_prefetch=1,
            grid=(4,),
            in_specs=whole,
            out_specs=[
                pl.BlockSpec(
                    (n_col, in_rows, wide), lambda step, places: (0, places[0] ^ step, 0)
                ),
                pl.BlockSpec(
                    (out_rows, n_col * features), lambda step, places: (places[0] ^ step, 0)
                ),
            ],
        ),
        out_shape=[
            jax.ShapeDtypeStruct((n_col, 4 * in_rows, wide), BF),
            jax.ShapeDtypeStruct((4 * out_rows, n_col * features), BF),
        ],
        compiler_params=pltpu.CompilerParams(vmem_limit_bytes=32 << 20),
        cost_estimate=pl.CostEstimate(
            flops=0, bytes_accessed=8 * n_col * in_rows * columns * 2, transcendentals=0
        ),
        name="first_weights",
    )(jnp.stack([dp, here]).astype(jnp.int32), *pieces)


def pair_gradients_kernel(all_ref, gate_ref, up_ref):
    gate_ref[...] = all_ref[0, 0, 0].astype(F32)
    up_ref[...] = all_ref[0, 0, 1].astype(F32)


def pair_gradients(gathered):
    n_dp, n_col, pair, rows, hidden = gathered.shape
    side = pl.BlockSpec((rows, hidden), lambda p, z: (p, z))
    return pl.pallas_call(
        pair_gradients_kernel,
        grid=(n_dp, n_col),
        in_specs=[pl.BlockSpec((1, 1, pair, rows, hidden), lambda p, z: (p, z, 0, 0, 0))],
        out_specs=[side, side],
        out_shape=[jax.ShapeDtypeStruct((n_dp * rows, n_col * hidden), F32)] * 2,
        compiler_params=pltpu.CompilerParams(vmem_limit_bytes=56 << 20),
        cost_estimate=pl.CostEstimate(
            flops=0, bytes_accessed=6 * math.prod(gathered.shape), transcendentals=0
        ),
        name="pair_gradients",
    )(gathered)


def last_gradients_kernel(n_out, places_ref, *refs):
    pieces, outs = refs[:-4], refs[-4:]
    n_col = pieces[0].shape[0]
    features = outs[3].shape[3]
    head_cols = outs[0].shape[1] // n_col
    narrow = features // n_out

    def store(piece, first):
        rows = piece.shape[1] // n_out
        for k in range(piece.shape[0]):
            source = lax.rem(places_ref[1] + first + k, n_col)
            place = pl.ds(pl.multiple_of(source * head_cols, head_cols), head_cols)
            for i in range(3):
                outs[i][:, place] = piece[k, :, i * head_cols : (i + 1) * head_cols].astype(F32)
            for i in range(n_out):
                outs[3][source, 0, :, i * narrow : (i + 1) * narrow] = piece[
                    k, i * rows : (i + 1) * rows, 3 * head_cols :
                ].astype(F32)

    for d in range(3):

        @pl.when(pl.program_id(0) == d)
        def _():
            store(pieces[d], 0)

    @pl.when(pl.program_id(0) == 3)
    def _():
        store(pieces[3], 0)
        store(pieces[4], pieces[3].shape[0])


def last_gradients(dp, here, pieces, head_cols, n_out):
    n_col, rows, columns = pieces[0].shape
    features = n_out * (columns - 3 * head_cols)
    side = pl.BlockSpec(
        (rows, n_col * head_cols), lambda step, places: (places[0] ^ step, 0)
    )
    side_shape = jax.ShapeDtypeStruct((4 * rows, n_col * head_cols), F32)
    *sides, out = pl.pallas_call(
        functools.partial(last_gradients_kernel, n_out),
        grid_spec=pltpu.PrefetchScalarGridSpec(
            num_scalar_prefetch=1,
            grid=(4,),
            in_specs=[
                pl.BlockSpec(piece.shape, lambda step, places: (0, 0, 0)) for piece in pieces
            ],
            out_specs=[side] * 3
            + [
                pl.BlockSpec(
                    (n_col, 1, rows // n_out, features),
                    lambda step, places: (0, places[0] ^ step, 0, 0),
                )
            ],
        ),
        out_shape=[side_shape] * 3
        + [jax.ShapeDtypeStruct((n_col, 4, rows // n_out, features), F32)],
        compiler_params=pltpu.CompilerParams(vmem_limit_bytes=56 << 20),
        cost_estimate=pl.CostEstimate(
            flops=0, bytes_accessed=24 * n_col * rows * columns, transcendentals=0
        ),
        name="last_gradients",
    )(jnp.stack([dp, here]).astype(jnp.int32), *pieces)
    return sides, out.reshape(-1, features)


def own_block_kernel(here_ref, *refs):
    blocks, whole = refs[:-1], refs[-1]
    for step, block in enumerate(blocks):

        @pl.when(pl.program_id(0) == step)
        def _():
            whole[...] = block[...]


def own_rows(ring, blocks):
    size = len(blocks)
    rows, columns = blocks[0].shape[0] // size, blocks[0].shape[1]
    return pl.pallas_call(
        own_block_kernel,
        grid_spec=pltpu.PrefetchScalarGridSpec(
            num_scalar_prefetch=1,
            grid=(size,),
            in_specs=[pl.BlockSpec((rows, columns), lambda step, here: (here[0], 0))] * size,
            out_specs=pl.BlockSpec(
                (rows, columns), lambda step, here: (0, lax.rem(here[0] + step, size))
            ),
        ),
        out_shape=jax.ShapeDtypeStruct((rows, columns * size), blocks[0].dtype),
        compiler_params=pltpu.CompilerParams(vmem_limit_bytes=32 << 20),
        name="own_rows",
    )(ring.here.astype(jnp.int32)[None], *blocks)


def from_here(ring, values, size, axis):
    twice = jnp.concatenate([values, values], axis=axis)
    return lax.dynamic_slice_in_dim(twice, ring.here * size, size * ring.size, axis)


def to_order(ring, values, size, axis):
    twice = jnp.concatenate([values, values], axis=axis)
    start = lax.rem(ring.size - ring.here, ring.size) * size
    return lax.dynamic_slice_in_dim(twice, start, size * ring.size, axis)


def exchange(ring, block_for):
    return [ring.fetch(block_for(ring.at(-step)), step) for step in range(ring.size)]


def gather_tokens(row, col, values, early=(), beside=()):
    near, early, beside = gather_near(col, values, early, beside)
    blocks = [
        jnp.concatenate([row.fetch(block, j) for j in range(row.size)], axis=0)
        for block in near
    ]
    return blocks, early, beside


def sum_rows(row, partial):
    size = partial.shape[0] // row.size
    total = partial[:size]
    for j in range(1, row.size):
        total = total + row.give(partial[j * size : (j + 1) * size].astype(BF), j).astype(F32)
    return total


def sum_all(row, col, values, block_for):
    length = values.shape[1]
    size = length // row.size
    total = values
    for j in range(1, row.size):
        total = total + jnp.roll(row.fetch(values, j), j * size, axis=1)
    came = [
        col.fetch(jnp.concatenate([total, block_for(col.at(-k))], axis=1), k)
        for k in range(col.size)
    ]
    result = came[0]
    for part in came[1:]:
        result = result + part
    return result[:, :length], [part[:, length:] for part in came]


def rms_scale(values):
    return lax.rsqrt(jnp.mean(values * values, axis=1, keepdims=True) + EPSILON)


def rms_back(grad_normed, branch, scales, gains):
    weighted = grad_normed * gains
    inner = jnp.mean(weighted * branch, axis=1, keepdims=True)
    grad_branch = scales * weighted - branch * (scales * scales * scales) * inner
    grad_gains = jnp.sum(grad_normed * branch * scales, axis=0)
    return grad_branch, grad_gains


def turn(values, cosine, sine):
    return values * cosine + pltpu.roll(values, values.shape[-1] // 2, 1) * sine


def kernel_dot(a, b, dims):
    return lax.dot_general(a, b, (dims, ((), ())), preferred_element_type=F32)


def softmax_parts(queries, keys, doc_rows, slot_rows, lines):
    scores = kernel_dot(queries, keys, ((1,), (1,))) * (HEAD**-0.5)
    allowed = (doc_rows == lines[2:3, :]) & (lines[3:4, :] <= slot_rows)
    scores = jnp.where(allowed, scores, MASKED)
    weights = jnp.exp(scores - jnp.max(scores, axis=1, keepdims=True))
    return weights * (1.0 / jnp.sum(weights, axis=1, keepdims=True))


def place_of(block, here, n_col):
    row, index = block // n_col, block % n_col
    step = lax.rem(index + n_col - here, n_col)
    if n_col == 4:
        step = jnp.where((here == 3) & (step % 2 == 1), 4 - step, step)
    return step, row


def forward_kernel(
    sizes,
    here_ref,
    query_ref,
    key_ref,
    value_ref,
    lines_ref,
    query_gain_ref,
    key_gain_ref,
    cosine_ref,
    sine_ref,
    query_rot_ref,
    key_rot_ref,
    value_low_ref,
    mixture_ref,
):
    n_row, n_col, small, large = sizes
    cosine, sine, lines = cosine_ref[...], sine_ref[...], lines_ref[...]
    columns = jnp.transpose(lines)
    normed = query_ref[...] * columns[:, 0:1] * query_gain_ref[...]
    query_rot_ref[...] = turn(normed, cosine, sine).astype(BF)
    normed = key_ref[...] * columns[:, 1:2] * key_gain_ref[...]
    key_rot_ref[...] = turn(normed, cosine, sine).astype(BF)
    value_low_ref[...] = value_ref[...].astype(BF)
    keys, values = key_rot_ref[...], value_low_ref[...]
    for start in range(0, query_ref.shape[0], large):
        rows = slice(start, start + large)
        chances = softmax_parts(
            query_rot_ref[rows, :], keys, columns[rows, 2:3], columns[rows, 3:4], lines
        )
        mixture = kernel_dot(chances.astype(BF), values, ((1,), (0,))).astype(BF)
        for inner in range(0, large, small):
            step, row = place_of((start + inner) // small, here_ref[0], n_col)
            place = pl.multiple_of((step * n_row + row) * small, small)
            mixture_ref[pl.ds(place, small), :] = mixture[inner : inner + small]


def backward_kernel(
    sizes,
    here_ref,
    query_ref,
    key_ref,
    lines_ref,
    query_gain_ref,
    key_gain_ref,
    cosine_ref,
    sine_ref,
    query_rot_ref,
    key_rot_ref,
    value_low_ref,
    grad_ref,
    query_weighted_ref,
    key_weighted_ref,
    grad_value_ref,
    inner_ref,
    query_gain_grad_ref,
    key_gain_grad_ref,
    key_total,
    value_total,
):
    n_row, n_col, small, large = sizes
    cosine, sine, lines = cosine_ref[...], sine_ref[...], lines_ref[...]
    columns = jnp.transpose(lines)
    keys, values = key_rot_ref[...], value_low_ref[...]
    factor = HEAD**-0.5
    for start in range(0, query_ref.shape[0], large):
        rows = slice(start, start + large)
        queries = query_rot_ref[rows, :]
        grads = []
        for inner in range(0, large, small):
            step, row = place_of((start + inner) // small, here_ref[0], n_col)
            place = pl.multiple_of((step * n_row + row) * small, small)
            grads.append(grad_ref[pl.ds(place, small), :])
        grads = jnp.concatenate(grads, axis=0)
        chances = softmax_parts(
            queries, keys, columns[rows, 2:3], columns[rows, 3:4], lines
        )
        value_part = kernel_dot(chances.astype(BF), grads, ((0,), (0,)))
        grad_chances = kernel_dot(grads, values, ((1,), (1,)))
        inner = jnp.sum(chances * grad_chances, axis=1, keepdims=True)
        grad_scores = (chances * (grad_chances - inner)).astype(BF)
        query_weighted_ref[rows, :] = kernel_dot(grad_scores, keys, ((1,), (0,))) * factor
        key_part = kernel_dot(grad_scores, queries, ((0,), (0,))) * factor
        if start == 0:
            value_total[...] = value_part
            key_total[...] = key_part
        else:
            value_total[...] += value_part
            key_total[...] += key_part
    grad_value_ref[...] = value_total[...].astype(BF)
    ones = jnp.ones((8, HEAD), F32)
    inners = []
    for grad, raw_ref, which, gain_ref, weighted_ref, gain_grad_ref in (
        (
            query_weighted_ref[...],
            query_ref,
            0,
            query_gain_ref,
            query_weighted_ref,
            query_gain_grad_ref,
        ),
        (
            key_total[...],
            key_ref,
            1,
            key_gain_ref,
            key_weighted_ref,
            key_gain_grad_ref,
        ),
    ):
        unturned = turn(grad, cosine, -sine)
        raw = raw_ref[...]
        gain_grad_ref[0] = jnp.sum(
            unturned * raw * columns[:, which : which + 1], axis=0, keepdims=True
        )
        weighted = unturned * gain_ref[...]
        weighted_ref[...] = weighted
        inners.append(
            lax.dot_general(
                ones,
                weighted * raw,
                (((1,), (1,)), ((), ())),
                precision=lax.Precision.HIGHEST,
                preferred_element_type=F32,
            )
        )
    which = lax.broadcasted_iota(jnp.int32, inner_ref.shape, 0)
    both = jnp.where(which == 0, inners[0], inners[1])

    @pl.when(pl.program_id(0) == 0)
    def _():
        inner_ref[...] = both

    @pl.when(pl.program_id(0) > 0)
    def _():
        inner_ref[...] += both


def head_specs(length):
    return {
        "head": lambda first: pl.BlockSpec(
            (length, HEAD), lambda h, here, first=first: (0, first + h)
        ),
        "gain": pl.BlockSpec((1, HEAD), lambda h, here: (0, h)),
        "lines": pl.BlockSpec((8, length), lambda h, here: (0, 0)),
        "table": pl.BlockSpec((length, HEAD), lambda h, here: (0, 0)),
        "head_line": pl.BlockSpec((1, 1, HEAD), lambda h, here: (h, 0, 0)),
    }


def attend_forward(row, col, raw, lines, gains, tables):
    length = raw.shape[0]
    heads = raw.shape[1] // (3 * HEAD)
    spec = head_specs(length)
    small = length // (row.size * col.size)
    wide = jax.ShapeDtypeStruct((length, heads * HEAD), BF)
    return pl.pallas_call(
        functools.partial(
            forward_kernel, (row.size, col.size, small, max(small, min(256, length)))
        ),
        grid_spec=pltpu.PrefetchScalarGridSpec(
            num_scalar_prefetch=1,
            grid=(heads,),
            in_specs=[spec["head"](0), spec["head"](heads), spec["head"](2 * heads)]
            + [spec["lines"]]
            + [spec["gain"]] * 2
            + [spec["table"]] * 2,
            out_specs=[spec["head"](0)] * 4,
        ),
        out_shape=[wide] * 4,
        compiler_params=pltpu.CompilerParams(vmem_limit_bytes=56 << 20),
        cost_estimate=pl.CostEstimate(
            flops=heads * 4 * length * length * HEAD,
            bytes_accessed=heads * length * HEAD * 20,
            transcendentals=heads * length * length,
        ),
        name="attend_forward",
    )(col.here.astype(jnp.int32)[None], raw, raw, raw, lines, *gains, *tables)


def attend_backward(row, col, raw, lines, gains, tables, saved, grad):
    length = raw.shape[0]
    heads = raw.shape[1] // (3 * HEAD)
    spec = head_specs(length)
    small = length // (row.size * col.size)
    wide = jax.ShapeDtypeStruct((length, heads * HEAD), F32)
    low = jax.ShapeDtypeStruct((length, heads * HEAD), BF)
    flat = jax.ShapeDtypeStruct((heads, 1, HEAD), F32)
    return pl.pallas_call(
        functools.partial(
            backward_kernel, (row.size, col.size, small, max(small, min(256, length)))
        ),
        grid_spec=pltpu.PrefetchScalarGridSpec(
            num_scalar_prefetch=1,
            grid=(heads,),
            in_specs=[spec["head"](0), spec["head"](heads), spec["lines"]]
            + [spec["gain"]] * 2
            + [spec["table"]] * 2
            + [spec["head"](0)] * 4,
            out_specs=[spec["head"](0)] * 3 + [spec["lines"]] + [spec["head_line"]] * 2,
            scratch_shapes=[pltpu.VMEM((length, HEAD), F32)] * 2,
        ),
        out_shape=[wide, wide, low, jax.ShapeDtypeStruct((8, length), F32), flat, flat],
        compiler_params=pltpu.CompilerParams(vmem_limit_bytes=56 << 20),
        cost_estimate=pl.CostEstimate(
            flops=heads * 10 * length * length * HEAD,
            bytes_accessed=heads * length * HEAD * 30,
            transcendentals=heads * length * length,
        ),
        name="attend_backward",
    )(col.here.astype(jnp.int32)[None], raw, raw, lines, *gains, *tables, *saved, grad)


def device_program(sizes):
    n_dp, n_row, n_col = sizes["dp"], sizes["row"], sizes["col"]

    def per_device(
        layer_input,
        doc_ids,
        positions,
        w_query,
        w_key,
        w_value,
        w_out,
        w_gate,
        w_up,
        w_down,
        gain_query,
        gain_key,
        gain_attn,
        gain_ffn,
        grad_output,
    ):
        row, col = Ring("row", n_row), Ring("col", n_col)
        dp = lax.axis_index("dp")
        length = doc_ids.shape[0]
        row_tokens = layer_input.shape[0]
        own_tokens = row_tokens // n_col
        features = layer_input.shape[1]
        width = features * n_col
        head_cols = w_query.shape[1] // n_col
        hidden_cols = w_gate.shape[1] // n_col
        in_rows = features // n_dp
        out_rows = head_cols // n_dp
        down_rows = hidden_cols // n_dp

        def gather_dp(values):
            return lax.all_gather(values, "dp", axis=0, tiled=True)

        steps = [1 << bit for bit in range(n_dp.bit_length() - 1)]

        def partner(values, step):
            return lax.ppermute(values, "dp", [(i, i ^ step) for i in range(n_dp)])

        class GroupSum:
            def __init__(self, block_for):
                blocks = [block_for(dp ^ d) for d in range(n_dp)]
                self.halves = [
                    (dict(enumerate(left for left, _ in blocks)), list(steps)),
                    (dict(enumerate(right for _, right in blocks)), list(steps[::-1])),
                ]
                self.came = None
                self.send()

            def send(self):
                self.came = []
                for blocks, order in self.halves:
                    given = [blocks[d] for d in sorted(blocks) if d & order[0]]
                    self.came.append(partner(jnp.stack(given), order[0]))

            def land(self, chain, more=True):
                self.came, chain = lax.optimization_barrier((self.came, chain))
                for (blocks, order), came in zip(self.halves, self.came):
                    step = order.pop(0)
                    for place, d in enumerate([d for d in sorted(blocks) if d & step]):
                        kept = blocks[d ^ step].astype(F32) + came[place].astype(F32)
                        blocks[d ^ step] = kept.astype(BF)
                        del blocks[d]
                if self.halves[0][1]:
                    self.send()
                return chain

            def finish(self, chain):
                while self.halves[0][1]:
                    chain = self.land(chain)
                return [blocks[0] for blocks, _ in self.halves], chain

        def gather_four(values, beside=()):
            half = values.shape[0] // 2
            one, two = partner(values, 1), partner(values, 2)
            (one, two), beside = lax.optimization_barrier(((one, two), beside))
            far = [partner(one[:half], 2), partner(two[half:], 1)]
            return [[values], [one], [two], far], beside

        def halves_of(values):
            half = values.shape[-1] // 2
            return values[..., :half], values[..., half:]

        def qkv_block(index):
            return jnp.concatenate(
                [
                    lax.dynamic_slice(
                        w, (dp * in_rows, index * head_cols), (in_rows, head_cols)
                    )
                    for w in (w_query, w_key, w_value)
                ],
                axis=1,
            )

        def gate_up_block(index):
            return jnp.stack(
                [
                    lax.dynamic_slice(
                        w, (dp * in_rows, index * hidden_cols), (in_rows, hidden_cols)
                    )
                    for w in (w_gate, w_up)
                ]
            )

        def out_block(index):
            return lax.dynamic_slice_in_dim(
                w_out, index * head_cols + dp * out_rows, out_rows, 0
            )

        def down_block(index):
            return lax.dynamic_slice_in_dim(
                w_down, index * hidden_cols + dp * down_rows, down_rows, 0
            )

        def first_block(index):
            out = out_block(index).reshape(out_rows, n_out, -1).swapaxes(0, 1)
            return jnp.concatenate([qkv_block(index), out.reshape(in_rows, -1)], axis=1)

        n_out = in_rows // out_rows
        first_parts = exchange(col, first_block)

        turned_docs = from_here(row, doc_ids, row_tokens, 0)
        turned_positions = from_here(row, positions, row_tokens, 0)
        slots = lax.rem(jnp.arange(length) + row.here * row_tokens, length)
        tables = rope_tables(turned_positions)
        if n_dp == 4:
            pieces, _ = gather_four(jnp.stack(first_parts))
            near, arrived, tables = gather_col(col, layer_input, pieces[1] + pieces[2], tables)
            pieces = pieces[0] + arrived + pieces[3]
            w_qkv, w_out_all = first_weights(dp, col.here, pieces, 3 * head_cols, n_out)
        else:
            near, _, tables = gather_col(col, layer_input, (), tables)
            first = gather_dp(jnp.stack(first_parts)[None])
            w_qkv = first[..., : 3 * head_cols].swapaxes(0, 1).reshape(n_col, features, -1)
            w_out_all = first[..., 3 * head_cols :].reshape(n_dp, n_col, n_out, out_rows, -1)
            w_out_all = w_out_all.transpose(0, 3, 1, 2, 4).reshape(head_cols, width)
            w_out_all = to_order(col, w_out_all, features, 1)
        w_qkv = [w_qkv[k] for k in range(n_col)]
        input_rows = [
            jnp.concatenate([row.fetch(block, j) for j in range(n_row)], axis=0)
            for block in near
        ]
        own_input = own_rows(col, near).astype(F32)

        w_down = after(w_down, near)
        down_parts = exchange(col, down_block)

        raw = sum(dot(rows, w) for rows, w in zip(input_rows, w_qkv))
        query_raw = raw[:, :head_cols]
        key_raw = raw[:, head_cols : 2 * head_cols]
        squares = jnp.stack(
            [jnp.sum(query_raw * query_raw, axis=1), jnp.sum(key_raw * key_raw, axis=1)]
        )
        gains = jnp.stack([gain_attn, gain_ffn])
        squares, gains = sum_all(row, col, squares, lambda index: gains)
        squares, w_out_all, down_parts = lax.optimization_barrier(
            (squares, w_out_all, down_parts)
        )
        w_down_all = gather_dp(assemble(col, down_parts, 1))
        gains = assemble(col, gains, 1)
        gain_attn_all, gain_ffn_all = gains[0:1], gains[1:2]
        w_gate, w_up = after((w_gate, w_up), down_parts)
        gate_up_parts = exchange(col, gate_up_block)

        scales = lax.rsqrt(squares / width + EPSILON)
        query_scale, key_scale = scales[0][:, None], scales[1][:, None]
        head_gains = (gain_query[None, :], gain_key[None, :])
        marks = jnp.stack([turned_docs, slots]).astype(F32)
        lines = jnp.concatenate([scales, marks, jnp.zeros((4, length), F32)], axis=0)
        *saved, mixture = attend_forward(row, col, raw, lines, head_gains, tables)
        gate_up_parts, mixture = lax.optimization_barrier((gate_up_parts, mixture))
        attended = []
        for k in range(n_col):
            total, *others = (
                dot(block_at(mixture, k * n_row + j, own_tokens, 0), w_out_all)
                for j in range(n_row)
            )
            for j, other in enumerate(others):
                total = total + row.give(other.astype(BF), j + 1).astype(F32)
            attended.append(total)
        gate_up_parts = assemble(
            col, [part[:, None] for part in after(gate_up_parts, w_down_all)], 1
        )
        gate_up_parts, attended = lax.optimization_barrier((gate_up_parts, attended))
        attended, _ = reduce_near(col, attended)
        w_gate_up = lax.all_gather(gate_up_parts[:, :, None], "dp", axis=2, tiled=True)
        w_gate_up = w_gate_up.reshape(2, width, hidden_cols)
        attn_scale = rms_scale(attended)
        hidden_state = own_input + attended * attn_scale * gain_attn_all

        state_rows, _, w_gate_up = gather_tokens(
            row, col, hidden_state.astype(BF), (), w_gate_up
        )
        w_gate, w_up = w_gate_up[0], w_gate_up[1]
        grad_output = after(grad_output, state_rows)
        cotangent = exchange(
            col, lambda index: block_at(grad_output, index, own_tokens, 0)
        )
        kept, activated = [], []
        for block in state_rows:
            pair = lax.optimization_barrier((dot(block, w_gate), dot(block, w_up)))
            gate_values, up_values = pair
            kept.append(pair)
            activated.append((gate_values * jax.nn.sigmoid(gate_values) * up_values).astype(BF))
        lowered = [sum_rows(row, dot(block, w_down_all)) for block in activated]
        lowered, cotangent = lax.optimization_barrier((lowered, cotangent))
        cotangent = assemble(col, cotangent, 1).astype(F32)
        lowered, _ = reduce_near(col, lowered)
        ffn_scale = rms_scale(lowered)
        own_output = (hidden_state + lowered * ffn_scale * gain_ffn_all).astype(BF)

        grad_lowered, grad_gain_ffn = rms_back(cotangent, lowered, ffn_scale, gain_ffn_all)
        lowered_rows, _, _ = gather_tokens(row, col, grad_lowered.astype(BF))
        gate_grads, up_grads, state_part = [], [], []
        for block, (gate_values, up_values) in zip(lowered_rows, kept):
            sigmoid_gate = jax.nn.sigmoid(gate_values)
            grad_activated = dot_nt(block, w_down_all)
            grad_gate = (
                grad_activated
                * up_values
                * (sigmoid_gate * (1.0 + gate_values * (1.0 - sigmoid_gate)))
            )
            grad_up = grad_activated * (gate_values * sigmoid_gate)
            pair = lax.optimization_barrier((grad_gate.astype(BF), grad_up.astype(BF)))
            gate_grads.append(pair[0])
            up_grads.append(pair[1])
            state_part.append(sum_rows(row, dot_nt(pair[0], w_gate) + dot_nt(pair[1], w_up)))
        wide = (
            jnp.concatenate(activated),
            jnp.concatenate(lowered_rows),
            jnp.concatenate(state_rows),
            jnp.concatenate(gate_grads),
            jnp.concatenate(up_grads),
        )
        activated, lowered_rows, state_rows, gate_grads, up_grads = after(wide, state_part)
        grad_w_down = dot_tn(activated, lowered_rows).astype(BF)
        down_sum = GroupSum(
            lambda index: halves_of(block_at(grad_w_down, index, down_rows, 0))
        )
        gate_up_grads = [
            dot_tn(after(state_rows, grad_w_down), grads)
            .astype(BF)
            .reshape(n_col, n_dp, in_rows, hidden_cols)
            for grads in (gate_grads, up_grads)
        ]
        state_part, gate_up_grads = reduce_near(col, state_part, gate_up_grads)
        gate_up_sum = GroupSum(
            lambda index: [
                lax.dynamic_index_in_dim(grads, index, 1, False) for grads in gate_up_grads
            ]
        )
        state_part = down_sum.land(state_part)
        grad_state = cotangent + state_part
        grad_attended, grad_gain_attn = rms_back(
            grad_state, attended, attn_scale, gain_attn_all
        )

        def second_step(came):
            gate_up_sum.came = came
            gate_up_sum.land(())
            return gate_up_sum.came, down_sum.came

        attended_rows, _, (gate_up_sum.came, down_sum.came) = gather_tokens(
            row, col, grad_attended.astype(BF), gate_up_sum.came, second_step
        )
        down_parts, _ = down_sum.finish(())
        down_parts = jnp.concatenate(down_parts, axis=1)
        down_parts = exchange(
            col, lambda index, whole=down_parts: block_at(whole, index, features, 1)
        )
        gate_up_sum, _ = gate_up_sum.finish(())

        grad_mixture = [dot_nt(block, w_out_all).astype(BF) for block in attended_rows]
        attended_rows = jnp.concatenate(attended_rows)
        grad_mixture = jnp.concatenate(grad_mixture)
        (
            query_weighted,
            key_weighted,
            grad_value,
            inner,
            grad_gain_query,
            grad_gain_key,
        ) = attend_backward(row, col, raw, lines, head_gains, tables, saved, grad_mixture)
        down_parts, inner = lax.optimization_barrier((down_parts, inner))
        down_back = assemble(col, [part[None] for part in down_parts], 0)
        down_all = gather_dp(down_back[None])
        small = jnp.stack([grad_gain_attn, grad_gain_ffn])
        inner, small = sum_all(row, col, inner[:2], lambda index: block_at(small, index, features, 1))
        inner = inner / width
        gate_up_whole = after(jnp.stack(gate_up_sum), inner)
        gate_up_parts = exchange(
            col, lambda index: lax.dynamic_index_in_dim(gate_up_whole, index, 1, False)
        )
        small = sum(small[1:], small[0])
        head_gain_grads = [grad_gain_query.reshape(-1), grad_gain_key.reshape(-1)]
        small = sum((row.fetch(small, j) for j in range(1, n_row)), small)
        small = jnp.concatenate([small, jnp.stack(head_gain_grads)], axis=1)
        for step in steps:
            small = small + partner(small, step)
        grad_query = (
            query_scale * query_weighted
            - query_raw * (query_scale * query_scale * query_scale) * inner[0][:, None]
        )
        grad_key = (
            key_scale * key_weighted
            - key_raw * (key_scale * key_scale * key_scale) * inner[1][:, None]
        )
        grad_qkv = jnp.concatenate(
            [grad_query.astype(BF), grad_key.astype(BF), grad_value], axis=1
        )
        grad_w_qkv = jnp.stack([dot_tn(rows, grad_qkv).astype(BF) for rows in input_rows])
        qkv_grads = grad_w_qkv.reshape(n_col, n_dp, in_rows, 3 * head_cols)
        out_grads = dot_tn(mixture, after(attended_rows, inner)).astype(BF)
        out_grads = out_grads.reshape(n_dp, out_rows, n_col, n_out, -1)
        out_grads = out_grads.transpose(2, 0, 3, 1, 4).reshape(n_col, n_dp, in_rows, -1)
        out_grads = from_here(col, out_grads, 1, 0)

        def last_block(index):
            return halves_of(
                jnp.concatenate(
                    [
                        lax.dynamic_index_in_dim(grads, index, 1, False)
                        for grads in (qkv_grads, out_grads)
                    ],
                    axis=-1,
                )
            )

        qkv_grads, out_grads, small, gate_up_parts, grad_qkv = lax.optimization_barrier(
            (qkv_grads, out_grads, small, gate_up_parts, grad_qkv)
        )
        last_sum = GroupSum(last_block)
        gate_up_back = assemble(
            col, [part[None] for part in after(gate_up_parts, down_back)], 0
        )
        gate_up_all = gather_dp(gate_up_back[None])
        input_part = [sum_rows(row, dot_nt(grad_qkv, w)) for w in w_qkv]
        gate_up_back, input_part = lax.optimization_barrier((gate_up_back, input_part))
        grad_input, last_sum.came = reduce_near(
            col, by_arrival(col, input_part), last_sum.came
        )
        last_sum, _ = last_sum.finish(())
        last_sum = jnp.concatenate(last_sum, axis=-1)
        last_parts = [col.fetch(last_sum[-k % n_col], k) for k in range(n_col)]
        grad_w_down = down_all.swapaxes(0, 1).reshape(w_down.shape).astype(F32)
        last_parts, grad_w_down, grad_input = lax.optimization_barrier(
            (last_parts, grad_w_down, grad_input)
        )
        own_output, grad_state = after((own_output, grad_state), last_parts)
        own_state = grad_state.astype(BF)
        output_parts = exchange(col, lambda index: block_at(own_output, index, features, 1))
        state_parts = exchange(col, lambda index: block_at(own_state, index, features, 1))
        grad_w_wide = (
            *pair_gradients(gate_up_all),
            grad_w_down,
        )
        if n_dp == 4:
            pieces, (output_parts, state_parts) = gather_four(
                jnp.stack(last_parts), (output_parts, state_parts)
            )
            pieces, grad_w_wide = lax.optimization_barrier((pieces, grad_w_wide))
            (grad_w_query, grad_w_key, grad_w_value), grad_w_out = last_gradients(
                dp, col.here, sum(pieces, []), head_cols, n_out
            )
        else:
            last_parts = assemble(col, [part[None] for part in last_parts], 0)
            last_all = gather_dp(after(last_parts, gate_up_all)[None])

            def columns_of(whole):
                return jnp.concatenate(
                    [whole[:, k].reshape(features, -1) for k in range(n_col)], axis=1
                ).astype(F32)

            grad_w_query, grad_w_key, grad_w_value = (
                columns_of(last_all[..., i * head_cols : (i + 1) * head_cols])
                for i in range(3)
            )
            out_all = last_all[..., 3 * head_cols :].reshape(
                n_dp, n_col, n_out, out_rows, -1
            )
            grad_w_out = out_all.transpose(1, 0, 3, 2, 4).reshape(w_out.shape).astype(F32)
        grad_w_gate, grad_w_up, grad_w_down = grad_w_wide
        layer_output = assemble(col, output_parts, 0)
        grad_input = grad_input + assemble(col, state_parts, 0).astype(F32)
        return (
            layer_output,
            grad_input,
            grad_w_query,
            grad_w_key,
            grad_w_value,
            grad_w_out,
            grad_w_gate,
            grad_w_up,
            grad_w_down,
            small[0, features:],
            small[1, features:],
            small[0, :features],
            small[1, :features],
        )

    return per_device


def solution(mesh):
    in_specs = (
        P(("dp", "row"), "col"),
        P("dp"),
        P("dp"),
        P("col", "row"),
        P("col", "row"),
        P("col", "row"),
        P("row", "col"),
        P("col", "row"),
        P("col", "row"),
        P("row", "col"),
        P(("row", "col")),
        P(("row", "col")),
        P("col"),
        P("col"),
        P(("dp", "row"), "col"),
    )
    out_specs = (
        P(("dp", "row"), "col"),
        P(("dp", "row"), "col"),
        P("col", "row"),
        P("col", "row"),
        P("col", "row"),
        P("row", "col"),
        P("col", "row"),
        P("col", "row"),
        P("row", "col"),
        P(("row", "col")),
        P(("row", "col")),
        P("col"),
        P("col"),
    )
    return jax.shard_map(
        device_program(dict(mesh.shape)),
        mesh=mesh,
        in_specs=in_specs,
        out_specs=out_specs,
        check_vma=False,
    )
```

time: 993 us -> 874 us (0.88)
  local copies, waits for them, and re-layouts: 125 us -> 60.4 us
  waiting for transfers between devices: 423 us -> 382 us
  Pallas kernels: 21.3 us -> 54.2 us
  other arithmetic: 86.6 us -> 56.4 us
  matrix products: 107 us -> 83.2 us
  starting transfers between devices: 193 us -> 211 us
  blocking collectives: 9.93 us -> 0 us
    ppermute x80 -> x68, waiting for transfers between devices: 145 us -> 110 us  [fetch(): return lax.ppermute(values, self.name, pairs)]
    pallas_call x2 -> x14, Pallas kernels: 21.3 us -> 54.2 us  [the longest x1 14.4 us: attend_backward(): pl.pallas_call(functools.partial(backward_kernel, (row.size, col.size, sm...]
    dynamic_update_slice x39 -> x0, local copies, waits for them, and re-layouts: 28.5 us -> none  [assemble(): lax.dynamic_update_slice_in_dim(whole, block, ring.at(step) * size, axis)]
    ppermute x32, waiting for transfers between devices: 190 us -> 214 us  [send(): return lax.ppermute(values, self.name, pairs)]
    all_gather x8 -> x3, waiting for transfers between devices: 22.6 us -> 0.01 us  [gather_dp(): return lax.all_gather(values, 'dp', axis=0, tiled=True)]
    convert_element_type x15 -> x10, other arithmetic: 24.4 us -> 3.05 us  [the longest x4 1.82 us: reduce_near(): two = (blocks[2] + relayed.astype(F32)).astype(BF)]
    dot_general x7 -> x8, matrix products: 39.9 us -> 20.2 us  [dot_tn(): lax.dot_general(a, b, (((0,), (0,)), ((), ())), preferred_element_type=F32)]
    ppermute x16 -> x22, waiting for transfers between devices: 64.4 us -> 47.8 us  [partner(): return lax.ppermute(values, 'dp', [(i, i ^ step) for i in range(n_dp)])]
  transfers between devices with their start and end apart: 136 -> 126, of which waited for: 53 -> 49; matrix products, arithmetic and copies ran while one was open for 26% -> 20% of each run, Pallas kernels for 1% -> 5%
where the time goes in v2:
time: 874 us; the launch traced here: 865 us
  waiting for transfers between devices  382 us (44%)
  starting transfers between devices  211 us (24%)
  matrix products  83.2 us (10%)
  local copies, waits for them, and re-layouts  60.4 us (7%)
  other arithmetic  56.4 us (6%)
  Pallas kernels  54.2 us (6%)
  between operations  17.4 us (2%)
    ppermute x32, waiting for transfers between devices, send(): return lax.ppermute(values, self.name, pairs)  214 us
    ppermute x68, waiting for transfers between devices, fetch(): return lax.ppermute(values, self.name, pairs)  110 us
    ppermute x32, starting transfers between devices, send(): return lax.ppermute(values, self.name, pairs)  100 us
    ppermute x68, starting transfers between devices, fetch(): return lax.ppermute(values, self.name, pairs)  85.8 us
    ppermute x22, waiting for transfers between devices, partner(): return lax.ppermute(values, 'dp', [(i, i ^ step) for i in range(n_dp)])  47.8 us
    unnamed x225, local copies, waits for them, and re-layouts  31.4 us
    dot_general x24, matrix products, dot(): return jnp.dot(a, b, preferred_element_type=F32)  31.3 us
    dot_general x20, matrix products, dot_nt(): lax.dot_general(a, b, (((1,), (1,)), ((), ())), preferred_element_type=F32)  30.4 us
  transfers between devices with their start and end apart: 126, of which 49 were waited for; matrix products, arithmetic and copies ran while one was open for 20% of the time, Pallas kernels for 5%

profile of v2, /device:TPU:0, one launch (start us, length us, event | category | flops | bytes accessed | tf_op | source)
XLA Modules:
  0.0 864.8 jit_solution(11538887565843275173)
XLA Ops:
  8.7 6.4 collective-permute-start.9
  25.5 19.2 %collective-permute-done.2 = bf16[128,1024]{1,0:T(8,128)(2,1)S(1)} collective-permute-done((bf16[128,1024]{1,0:T(8,128)(2,1)S(1)}, bf16[128,1024]{1,0:T(8,128)(2,1)S(1)}, u32[]{:S(2)}, u32[]{:S(2)}) %collective-permute-start.2) | collective-permute-done | bytes 262176 | tf_op jit(solution)/shard_map/ppermute | solution.py:63
  52.4 16.1 %collective-permute-done.6.refs_2_ = bf16[4,128,1024]{2,1,0:T(8,128)(2,1)S(1)} collective-permute-done((bf16[4,128,1024]{2,1,0:T(8,128)(2,1)S(1)}, bf16[4,128,1024]{2,1,0:T(8,128)(2,1)S(1)}, u32[]{:S(2)}, u32[]{:S(2)}) %collective-permute-start.6) | collective-permute-done | bytes 1048608 | tf_op jit(solution)/shard_map/ppermute | solution.py:703
  78.4 24.4 %collective-permute-done.11 = bf16[512,512]{1,0:T(8,128)(2,1)S(1)} collective-permute-done((bf16[512,512]{1,0:T(8,128)(2,1)S(1)}, bf16[512,512]{1,0:T(8,128)(2,1)S(1)}, u32[]{:S(2)}, u32[]{:S(2)}) %collective-permute-start.11) | collective-permute-done | bytes 524320 | tf_op jit(solution)/shard_map/ppermute | solution.py:66
  112.3 4.5 collective-permute-start.21
  122.3 11.9 %collective-permute-done.18 = f32[2,1536]{1,0:T(2,128)S(1)} collective-permute-done((f32[2,1536]{1,0:T(2,128)S(1)}, f32[2,1536]{1,0:T(2,128)S(1)}, u32[]{:S(2)}, u32[]{:S(2)}) %collective-permute-start.18) | collective-permute-done | bytes 12320 | tf_op jit(solution)/shard_map/ppermute | solution.py:63
  134.1 5.9 collective-permute-done.17
  155.6 11.2 %attend_forward.1 = (bf16[1024,256]{1,0:T(8,128)(2,1)}, bf16[1024,256]{1,0:T(8,128)(2,1)}, bf16[1024,256]{1,0:T(8,128)(2,1)}, bf16[1024,256]{1,0:T(8,128)(2,1)}) custom-call(s32[1]{0:T(128)} %bitcast.here_ref, f32[1024,768]{1,0:T(8,128)} %copy-done.23, f32[1024,768]{1,0:T(8,128)} %copy-done.23, f32[1024,768]{1,0:T(8,128)} %copy-done.23, ...), custom_call_target="tpu_custom_call" | custom-call | flops 1073741824 | bytes 5242880 | tf_op jit(solution)/shard_map/attend_forward/pallas_call | solution.py:607
  166.9 28.7 %collective-permute-done.23 = bf16[2,128,1024]{2,1,0:T(8,128)(2,1)S(1)} collective-permute-done((bf16[2,128,1024]{2,1,0:T(8,128)(2,1)S(1)}, bf16[2,128,1024]{2,1,0:T(8,128)(2,1)S(1)}, u32[]{:S(2)}, u32[]{:S(2)}) %collective-permute-start.23) | collective-permute-done | bytes 524320 | tf_op jit(solution)/shard_map/ppermute | solution.py:63
  216.1 8.8 %collective-permute-done.31 = bf16[128,2048]{1,0:T(8,128)(2,1)S(1)} collective-permute-done((bf16[128,2048]{1,0:T(8,128)(2,1)}, bf16[128,2048]{1,0:T(8,128)(2,1)S(1)}, u32[]{:S(2)}, u32[]{:S(2)}) %collective-permute-start.31) | collective-permute-done | bytes 524320 | tf_op jit(solution)/shard_map/ppermute | solution.py:66
  236.1 19.6 %collective-permute-done.32 = bf16[128,2048]{1,0:T(8,128)(2,1)S(1)} collective-permute-done((bf16[128,2048]{1,0:T(8,128)(2,1)S(1)}, bf16[128,2048]{1,0:T(8,128)(2,1)S(1)}, u32[]{:S(2)}, u32[]{:S(2)}) %collective-permute-start.32) | collective-permute-done | bytes 524320 | tf_op jit(solution)/shard_map/ppermute | solution.py:66
  259.5 4.6 collective-permute-start.35
  264.2 15.0 %collective-permute-done.34 = bf16[128,2048]{1,0:T(8,128)(2,1)} collective-permute-done((bf16[128,2048]{1,0:T(8,128)(2,1)}, bf16[128,2048]{1,0:T(8,128)(2,1)}, u32[]{:S(2)}, u32[]{:S(2)}) %collective-permute-start.34) | collective-permute-done | bytes 524320 | tf_op jit(solution)/shard_map/ppermute | solution.py:66
  281.0 4.9 collective-permute-done.36
  285.9 10.5 %all-gather.10.cloned.1.call-done = bf16[2,4,512,1024]{3,2,1,0:T(8,128)(2,1)} async-done(((bf16[2,4,128,1024]{3,2,1,0:T(8,128)(2,1)}), bf16[2,4,512,1024]{3,2,1,0:T(8,128)(2,1)}) %all-gather.10.cloned.1.call-update) | async-done | bytes 8388624 | tf_op jit(solution)/shard_map/all_gather | solution.py:851
  342.6 9.6 %collective-permute-done.50 = bf16[128,2048]{1,0:T(8,128)(2,1)S(1)} collective-permute-done((bf16[128,2048]{1,0:T(8,128)(2,1)S(1)}, bf16[128,2048]{1,0:T(8,128)(2,1)S(1)}, u32[]{:S(2)}, u32[]{:S(2)}) %collective-permute-start.50) | collective-permute-done | bytes 524320 | tf_op jit(solution)/shard_map/ppermute | solution.py:66
  358.3 5.2 collective-permute-done.49
  363.4 16.5 %collective-permute-done.51 = bf16[128,2048]{1,0:T(8,128)(2,1)S(1)} collective-permute-done((bf16[128,2048]{1,0:T(8,128)(2,1)S(1)}, bf16[128,2048]{1,0:T(8,128)(2,1)S(1)}, u32[]{:S(2)}, u32[]{:S(2)}) %collective-permute-start.51) | collective-permute-done | bytes 524320 | tf_op jit(solution)/shard_map/ppermute | solution.py:66
  383.9 5.4 collective-permute-start.54
  393.4 12.0 %collective-permute-done.53 = bf16[128,2048]{1,0:T(8,128)(2,1)} collective-permute-done((bf16[128,2048]{1,0:T(8,128)(2,1)}, bf16[128,2048]{1,0:T(8,128)(2,1)}, u32[]{:S(2)}, u32[]{:S(2)}) %collective-permute-start.53) | collective-permute-done | bytes 524320 | tf_op jit(solution)/shard_map/ppermute | solution.py:66
  410.6 4.4 multiply_convert_fusion.6
  424.8 5.9 collective-permute-done.58
  449.0 5.2 collective-permute-start.68
  456.0 4.6 collective-permute-start.67
  460.6 5.9 collective-permute-done.68
  466.7 4.9 convolution_convert_fusion.2
  475.3 4.9 convolution_convert_fusion
  480.2 4.9 convolution_convert_fusion.1
  491.8 19.0 %collective-permute-done.69 = bf16[128,2048]{1,0:T(8,128)(2,1)S(1)} collective-permute-done((bf16[128,2048]{1,0:T(8,128)(2,1)S(1)}, bf16[128,2048]{1,0:T(8,128)(2,1)S(1)}, u32[]{:S(2)}, u32[]{:S(2)}) %collective-permute-start.69) | collective-permute-done | bytes 524320 | tf_op jit(solution)/shard_map/ppermute | solution.py:66
  516.7 20.3 %collective-permute-done.71 = bf16[128,2048]{1,0:T(8,128)(2,1)S(1)} collective-permute-done((bf16[128,2048]{1,0:T(8,128)(2,1)S(1)}, bf16[128,2048]{1,0:T(8,128)(2,1)S(1)}, u32[]{:S(2)}, u32[]{:S(2)}) %collective-permute-start.71) | collective-permute-done | bytes 524320 | tf_op jit(solution)/shard_map/ppermute | solution.py:66
  537.0 4.9 collective-permute-done.73
  549.5 4.8 collective-permute-done.79
  556.6 4.6 collective-permute-start.74
  563.3 16.1 %collective-permute-done.78 = bf16[1,256,1024]{2,1,0:T(8,128)(2,1)} collective-permute-done((bf16[1,256,1024]{2,1,0:T(8,128)(2,1)}, bf16[1,256,1024]{2,1,0:T(8,128)(2,1)}, u32[]{:S(2)}, u32[]{:S(2)}) %collective-permute-start.78) | collective-permute-done | bytes 524320 | tf_op jit(solution)/shard_map/ppermute | solution.py:703
  588.3 9.9 %collective-permute-done.82 = bf16[128,2048]{1,0:T(8,128)(2,1)S(1)} collective-permute-done((bf16[128,2048]{1,0:T(8,128)(2,1)S(1)}, bf16[128,2048]{1,0:T(8,128)(2,1)S(1)}, u32[]{:S(2)}, u32[]{:S(2)}) %collective-permute-start.82) | collective-permute-done | bytes 524320 | tf_op jit(solution)/shard_map/ppermute | solution.py:66
  606.0 14.4 %attend_backward.1 = (f32[1024,256]{1,0:T(8,128)}, f32[1024,256]{1,0:T(8,128)}, bf16[1024,256]{1,0:T(8,128)(2,1)}, f32[8,1024]{1,0:T(8,128)}, f32[2,1,128]{2,1,0:T(1,128)}, /*index=5*/f32[2,1,128]{2,1,0:T(1,128)}) custom-call(s32[1]{0:T(128)} %bitcast.here_ref, f32[1024,768]{1,0:T(8,128)} %copy-done.23, f32[1024,768]{1,0:T(8,128)} %copy-done.23, ...), custom_call_target="tpu_custom_call" | custom-call | flops 2684354560 | bytes 7864320 | tf_op jit(solution)/shard_map/attend_backward/pallas_call | solution.py:639
  620.4 6.1 collective-permute-done.85
  665.3 16.3 %collective-permute-done.95 = bf16[2,128,1024]{2,1,0:T(8,128)(2,1)S(1)} collective-permute-done((bf16[2,128,1024]{2,1,0:T(8,128)(2,1)}, bf16[2,128,1024]{2,1,0:T(8,128)(2,1)S(1)}, u32[]{:S(2)}, u32[]{:S(2)}) %collective-permute-start.95) | collective-permute-done | bytes 524320 | tf_op jit(solution)/shard_map/ppermute | solution.py:63
  700.5 12.7 %collective-permute-start.101 = (bf16[512,512]{1,0:T(8,128)(2,1)S(1)}, bf16[512,512]{1,0:T(8,128)(2,1)S(1)}, u32[]{:S(2)}, u32[]{:S(2)}) collective-permute-start(bf16[512,512]{1,0:T(8,128)(2,1)S(1)} %get-tuple-element.355), channel_id=1, source_target_pairs={{3,2},{0,1},{7,6},{4,5},{11,10},{8,9},{15,14},{12,13},{19,18},{16,... | collective-permute-start | bytes 1572872 | tf_op jit(solution)/shard_map/ppermute | solution.py:66
  713.1 11.4 %collective-permute-done.101 = bf16[512,512]{1,0:T(8,128)(2,1)S(1)} collective-permute-done((bf16[512,512]{1,0:T(8,128)(2,1)S(1)}, bf16[512,512]{1,0:T(8,128)(2,1)S(1)}, u32[]{:S(2)}, u32[]{:S(2)}) %collective-permute-start.101) | collective-permute-done | bytes 524320 | tf_op jit(solution)/shard_map/ppermute | solution.py:66
  730.9 23.2 %collective-permute-start.110 = (bf16[512,512]{1,0:T(8,128)(2,1)S(1)}, bf16[512,512]{1,0:T(8,128)(2,1)S(1)}, u32[]{:S(2)}, u32[]{:S(2)}) collective-permute-start(bf16[512,512]{1,0:T(8,128)(2,1)S(1)} %get-tuple-element.354), channel_id=1, source_target_pairs={{0,1},{1,2},{2,3},{4,5},{5,6},{6,7},{8,9},{9,10},{10,11},{12,13},{... | collective-permute-start | bytes 1572872 | tf_op jit(solution)/shard_map/ppermute | solution.py:66
  757.1 8.0 collective-permute-start.108
  765.1 18.4 %collective-permute-start.107 = (bf16[128,1024]{1,0:T(8,128)(2,1)S(1)}, bf16[128,1024]{1,0:T(8,128)(2,1)}, u32[]{:S(2)}, u32[]{:S(2)}) collective-permute-start(bf16[128,1024]{1,0:T(8,128)(2,1)S(1)} %get-tuple-element.434), channel_id=1, source_target_pairs={{0,2},{1,3},{2,0},{3,1},{4,6},{5,7},{6,4},{7,5},{8,10},{9,11},{10,... | collective-permute-start | bytes 786440 | tf_op jit(solution)/shard_map/ppermute | solution.py:63
  783.5 14.2 %collective-permute-done.111 = bf16[512,512]{1,0:T(8,128)(2,1)S(1)} collective-permute-done((bf16[512,512]{1,0:T(8,128)(2,1)S(1)}, bf16[512,512]{1,0:T(8,128)(2,1)S(1)}, u32[]{:S(2)}, u32[]{:S(2)}) %collective-permute-start.111) | collective-permute-done | bytes 524320 | tf_op jit(solution)/shard_map/ppermute | solution.py:66
  802.4 4.4 copy.77
  812.2 4.8 collective-permute-start.115
  837.2 13.1 %pair_gradients.1 = (f32[512,4096]{1,0:T(8,128)}, f32[512,4096]{1,0:T(8,128)}) custom-call(bf16[4,4,2,128,1024]{4,3,2,1,0:T(8,128)(2,1)} %bitcast.348), custom_call_target="tpu_custom_call" | custom-call | bytes 25165824 | tf_op jit(solution)/shard_map/pair_gradients/pallas_call | solution.py:260
  851.3 6.5 last_gradients.1
  (675 shorter events, 333.3 us)
Async XLA Ops:
  7.2 197.7 %all-gather.8.cloned.1.call-start = ((), (), s32[]{:S(2)}) async-start(), calls=%async_computation | async-start | bytes 5242880 | tf_op jit(solution)/shard_map/all_gather | solution.py:698
  7.2 63.6 %collective-permute-start.10 = (bf16[512,512]{1,0:T(8,128)(2,1)}, bf16[512,512]{1,0:T(8,128)(2,1)}, u32[]{:S(2)}, u32[]{:S(2)}) collective-permute-start(bf16[512,512]{1,0:T(8,128)(2,1)} %refs_0_.1), channel_id=1, source_target_pairs={{1,0},{2,1},{3,2},{5,4},{6,5},{7,6},{9,8},{10,9},{11,10},{13,12},{... | collective-permute-start | bytes 1572872 | tf_op jit(solution)/shard_map/ppermute | solution.py:66
  8.7 62.2 %collective-permute-start.9 = (bf16[512,512]{1,0:T(8,128)(2,1)}, bf16[512,512]{1,0:T(8,128)(2,1)}, u32[]{:S(2)}, u32[]{:S(2)}) collective-permute-start(bf16[512,512]{1,0:T(8,128)(2,1)} %refs_0_.1), channel_id=1, source_target_pairs={{0,1},{1,2},{2,3},{4,5},{5,6},{6,7},{8,9},{9,10},{10,11},{12,13},{... | collective-permute-start | bytes 1572872 | tf_op jit(solution)/shard_map/ppermute | solution.py:66
  18.3 26.5 %collective-permute-start.2 = (bf16[128,1024]{1,0:T(8,128)(2,1)S(1)}, bf16[128,1024]{1,0:T(8,128)(2,1)S(1)}, u32[]{:S(2)}, u32[]{:S(2)}) collective-permute-start(bf16[128,1024]{1,0:T(8,128)(2,1)S(1)} %pad_maximum_fusion.34), channel_id=1, source_target_pairs={{0,2},{1,3},{2,0},{3,1},{4,6},{5,7},{6,4},{7,5},{8,10},{9,11},{10,... | collective-permute-start | bytes 786440 | tf_op jit(solution)/shard_map/ppermute | solution.py:63
  44.8 26.1 %collective-permute-start.4 = (bf16[512,512]{1,0:T(8,128)(2,1)S(1)}, bf16[512,512]{1,0:T(8,128)(2,1)S(1)}, u32[]{:S(2)}, u32[]{:S(2)}) collective-permute-start(bf16[512,512]{1,0:T(8,128)(2,1)S(1)} %copy-done.9), channel_id=1, source_target_pairs={{0,2},{1,3},{2,0},{3,1},{4,6},{5,7},{6,4},{7,5},{8,10},{9,11},{10,... | collective-permute-start | bytes 1572872 | tf_op jit(solution)/shard_map/ppermute | solution.py:66
  70.9 31.9 %collective-permute-start.11 = (bf16[512,512]{1,0:T(8,128)(2,1)S(1)}, bf16[512,512]{1,0:T(8,128)(2,1)S(1)}, u32[]{:S(2)}, u32[]{:S(2)}) collective-permute-start(bf16[512,512]{1,0:T(8,128)(2,1)S(1)} %collective-permute-done.4.refs_2_), channel_id=1, source_target_pairs={{2,3},{1,0},{6,7},{5,4},{10,11},{9,8},{14,15},{13,12},{18,19},{17,... | collective-permute-start | bytes 1572872 | tf_op jit(solution)/shard_map/ppermute | solution.py:66
  72.3 32.2 %collective-permute-start.13 = (bf16[512,512]{1,0:T(8,128)(2,1)S(1)}, bf16[512,512]{1,0:T(8,128)(2,1)S(1)}, u32[]{:S(2)}, u32[]{:S(2)}) collective-permute-start(bf16[512,512]{1,0:T(8,128)(2,1)S(1)} %collective-permute-done.4.refs_2_), channel_id=1, source_target_pairs={{0,4},{4,0},{1,5},{5,1},{2,6},{6,2},{3,7},{7,3},{8,12},{12,8},{9,1... | collective-permute-start | bytes 1572872 | tf_op jit(solution)/shard_map/ppermute | solution.py:63
  75.3 29.3 %collective-permute-start.8 = (bf16[2,128,1024]{2,1,0:T(8,128)(2,1)S(1)}, bf16[2,128,1024]{2,1,0:T(8,128)(2,1)S(1)}, u32[]{:S(2)}, u32[]{:S(2)}) collective-permute-start(bf16[2,128,1024]{2,1,0:T(8,128)(2,1)S(1)} %slice.300), channel_id=1, source_target_pairs={{0,8},{8,0},{16,24},{24,16},{1,9},{9,1},{17,25},{25,17},{2,10},{10... | collective-permute-start | bytes 1572872 | tf_op jit(solution)/shard_map/ppermute | solution.py:703
  76.8 27.7 %collective-permute-start.7 = (bf16[2,128,1024]{2,1,0:T(8,128)(2,1)S(1)}, bf16[2,128,1024]{2,1,0:T(8,128)(2,1)S(1)}, u32[]{:S(2)}, u32[]{:S(2)}) collective-permute-start(bf16[2,128,1024]{2,1,0:T(8,128)(2,1)S(1)} %slice.299), channel_id=1, source_target_pairs={{0,16},{8,24},{16,0},{24,8},{1,17},{9,25},{17,1},{25,9},{2,18},{10... | collective-permute-start | bytes 1572872 | tf_op jit(solution)/shard_map/ppermute | solution.py:703
  112.3 32.0 %collective-permute-start.21 = (bf16[256,512]{1,0:T(8,128)(2,1)S(1)}, bf16[256,512]{1,0:T(8,128)(2,1)S(1)}, u32[]{:S(2)}, u32[]{:S(2)}) collective-permute-start(bf16[256,512]{1,0:T(8,128)(2,1)S(1)} %get-tuple-element.406), channel_id=1, source_target_pairs={{0,1},{1,2},{2,3},{3,0},{4,5},{5,6},{6,7},{7,4},{8,9},{9,10},{10,1... | collective-permute-start | bytes 786440 | tf_op jit(solution)/shard_map/ppermute | solution.py:63
  116.7 27.5 %collective-permute-start.20 = (bf16[256,512]{1,0:T(8,128)(2,1)S(1)}, bf16[256,512]{1,0:T(8,128)(2,1)S(1)}, u32[]{:S(2)}, u32[]{:S(2)}) collective-permute-start(bf16[256,512]{1,0:T(8,128)(2,1)S(1)} %get-tuple-element.407), channel_id=1, source_target_pairs={{0,2},{1,3},{2,0},{3,1},{4,6},{5,7},{6,4},{7,5},{8,10},{9,11},{10,... | collective-permute-start | bytes 786440 | tf_op jit(solution)/shard_map/ppermute | solution.py:63
  118.7 25.5 %collective-permute-start.19 = (bf16[256,512]{1,0:T(8,128)(2,1)S(1)}, bf16[256,512]{1,0:T(8,128)(2,1)S(1)}, u32[]{:S(2)}, u32[]{:S(2)}) collective-permute-start(bf16[256,512]{1,0:T(8,128)(2,1)S(1)} %get-tuple-element.408), channel_id=1, source_target_pairs={{0,3},{1,0},{2,1},{3,2},{4,7},{5,4},{6,5},{7,6},{8,11},{9,8},{10,9... | collective-permute-start | bytes 786440 | tf_op jit(solution)/shard_map/ppermute | solution.py:63
  145.6 150.8 %all-gather.10.cloned.1.call-start = ((), (), s32[]{:S(2)}) async-start(), calls=%async_computation.1 | async-start | bytes 10485760 | tf_op jit(solution)/shard_map/all_gather | solution.py:851
  151.6 44.0 %collective-permute-start.23 = (bf16[2,128,1024]{2,1,0:T(8,128)(2,1)S(1)}, bf16[2,128,1024]{2,1,0:T(8,128)(2,1)S(1)}, u32[]{:S(2)}, u32[]{:S(2)}) collective-permute-start(bf16[2,128,1024]{2,1,0:T(8,128)(2,1)S(1)} %pad_maximum_fusion.29), channel_id=1, source_target_pairs={{0,2},{1,3},{2,0},{3,1},{4,6},{5,7},{6,4},{7,5},{8,10},{9,11},{10,... | collective-permute-start | bytes 1572872 | tf_op jit(solution)/shard_map/ppermute | solution.py:63
  152.6 43.0 %collective-permute-start.24 = (bf16[2,128,1024]{2,1,0:T(8,128)(2,1)S(1)}, bf16[2,128,1024]{2,1,0:T(8,128)(2,1)S(1)}, u32[]{:S(2)}, u32[]{:S(2)}) collective-permute-start(bf16[2,128,1024]{2,1,0:T(8,128)(2,1)S(1)} %pad_maximum_fusion.30), channel_id=1, source_target_pairs={{0,1},{1,2},{2,3},{3,0},{4,5},{5,6},{6,7},{7,4},{8,9},{9,10},{10,1... | collective-permute-start | bytes 1572872 | tf_op jit(solution)/shard_map/ppermute | solution.py:63
  209.9 589.1 %all-gather.12.cloned.1.call-start = ((), (), s32[]{:S(2)}) async-start(), calls=%async_computation.2 | async-start | bytes 5242880 | tf_op jit(solution)/shard_map/all_gather | solution.py:698
  226.2 29.4 %collective-permute-start.32 = (bf16[128,2048]{1,0:T(8,128)(2,1)S(1)}, bf16[128,2048]{1,0:T(8,128)(2,1)S(1)}, u32[]{:S(2)}, u32[]{:S(2)}) collective-permute-start(bf16[128,2048]{1,0:T(8,128)(2,1)S(1)} %add_convert_fusion.6), channel_id=1, source_target_pairs={{0,2},{1,3},{2,0},{3,1},{4,6},{5,7},{6,4},{7,5},{8,10},{9,11},{10,... | collective-permute-start | bytes 1572872 | tf_op jit(solution)/shard_map/ppermute | solution.py:66
  258.2 27.7 %collective-permute-start.36 = (bf16[128,2048]{1,0:T(8,128)(2,1)}, bf16[128,2048]{1,0:T(8,128)(2,1)}, u32[]{:S(2)}, u32[]{:S(2)}) collective-permute-start(bf16[128,2048]{1,0:T(8,128)(2,1)} %get-tuple-element.375), channel_id=1, source_target_pairs={{1,0},{2,1},{3,2},{5,4},{6,5},{7,6},{9,8},{10,9},{11,10},{13,12},{... | collective-permute-start | bytes 1572872 | tf_op jit(solution)/shard_map/ppermute | solution.py:66
  259.5 26.4 %collective-permute-start.35 = (bf16[128,2048]{1,0:T(8,128)(2,1)}, bf16[128,2048]{1,0:T(8,128)(2,1)S(1)}, u32[]{:S(2)}, u32[]{:S(2)}) collective-permute-start(bf16[128,2048]{1,0:T(8,128)(2,1)} %get-tuple-element.375), channel_id=1, source_target_pairs={{0,1},{1,2},{2,3},{4,5},{5,6},{6,7},{8,9},{9,10},{10,11},{12,13},{... | collective-permute-start | bytes 1572872 | tf_op jit(solution)/shard_map/ppermute | solution.py:66
  296.5 27.7 %collective-permute-start.42 = (bf16[128,2048]{1,0:T(8,128)(2,1)}, bf16[128,2048]{1,0:T(8,128)(2,1)S(1)}, u32[]{:S(2)}, u32[]{:S(2)}) collective-permute-start(bf16[128,2048]{1,0:T(8,128)(2,1)} %collective-permute-done.34), channel_id=1, source_target_pairs={{2,3},{1,0},{6,7},{5,4},{10,11},{9,8},{14,15},{13,12},{18,19},{17,... | collective-permute-start | bytes 1572872 | tf_op jit(solution)/shard_map/ppermute | solution.py:66
  352.3 27.6 %collective-permute-start.51 = (bf16[128,2048]{1,0:T(8,128)(2,1)S(1)}, bf16[128,2048]{1,0:T(8,128)(2,1)S(1)}, u32[]{:S(2)}, u32[]{:S(2)}) collective-permute-start(bf16[128,2048]{1,0:T(8,128)(2,1)S(1)} %add_convert_fusion.5), channel_id=1, source_target_pairs={{0,2},{1,3},{2,0},{3,1},{4,6},{5,7},{6,4},{7,5},{8,10},{9,11},{10,... | collective-permute-start | bytes 1572872 | tf_op jit(solution)/shard_map/ppermute | solution.py:66
  382.6 26.4 %collective-permute-start.55 = (bf16[128,2048]{1,0:T(8,128)(2,1)}, bf16[128,2048]{1,0:T(8,128)(2,1)}, u32[]{:S(2)}, u32[]{:S(2)}) collective-permute-start(bf16[128,2048]{1,0:T(8,128)(2,1)} %get-tuple-element.381), channel_id=1, source_target_pairs={{1,0},{2,1},{3,2},{5,4},{6,5},{7,6},{9,8},{10,9},{11,10},{13,12},{... | collective-permute-start | bytes 1572872 | tf_op jit(solution)/shard_map/ppermute | solution.py:66
  420.6 27.9 %collective-permute-start.60 = (bf16[128,2048]{1,0:T(8,128)(2,1)S(1)}, bf16[128,2048]{1,0:T(8,128)(2,1)S(1)}, u32[]{:S(2)}, u32[]{:S(2)}) collective-permute-start(bf16[128,2048]{1,0:T(8,128)(2,1)S(1)} %slice.661), channel_id=1, source_target_pairs={{0,4},{4,0},{1,5},{5,1},{2,6},{6,2},{3,7},{7,3},{8,12},{12,8},{9,1... | collective-permute-start | bytes 1572872 | tf_op jit(solution)/shard_map/ppermute | solution.py:63
  454.7 35.0 %collective-permute-start.66 = (bf16[128,2048]{1,0:T(8,128)(2,1)S(1)}, bf16[128,2048]{1,0:T(8,128)(2,1)S(1)}, u32[]{:S(2)}, u32[]{:S(2)}) collective-permute-start(bf16[128,2048]{1,0:T(8,128)(2,1)S(1)} %get-tuple-element.365), channel_id=1, source_target_pairs={{1,0},{2,1},{3,2},{5,4},{6,5},{7,6},{9,8},{10,9},{11,10},{13,12},{... | collective-permute-start | bytes 1572872 | tf_op jit(solution)/shard_map/ppermute | solution.py:66
  456.0 35.3 %collective-permute-start.67 = (bf16[128,2048]{1,0:T(8,128)(2,1)S(1)}, bf16[128,2048]{1,0:T(8,128)(2,1)S(1)}, u32[]{:S(2)}, u32[]{:S(2)}) collective-permute-start(bf16[128,2048]{1,0:T(8,128)(2,1)S(1)} %get-tuple-element.367), channel_id=1, source_target_pairs={{0,1},{1,2},{2,3},{4,5},{5,6},{6,7},{8,9},{9,10},{10,11},{12,13},{... | collective-permute-start | bytes 1572872 | tf_op jit(solution)/shard_map/ppermute | solution.py:66
  472.0 39.0 %collective-permute-start.64 = (bf16[2,256,1024]{2,1,0:T(8,128)(2,1)S(1)}, bf16[2,256,1024]{2,1,0:T(8,128)(2,1)S(1)}, u32[]{:S(2)}, u32[]{:S(2)}) collective-permute-start(bf16[2,256,1024]{2,1,0:T(8,128)(2,1)S(1)} %pad_maximum_fusion.14), channel_id=1, source_target_pairs={{0,8},{8,0},{16,24},{24,16},{1,9},{9,1},{17,25},{25,17},{2,10},{10... | collective-permute-start | bytes 3145736 | tf_op jit(solution)/shard_map/ppermute | solution.py:703
  473.6 37.4 %collective-permute-start.65 = (bf16[2,256,1024]{2,1,0:T(8,128)(2,1)S(1)}, bf16[2,256,1024]{2,1,0:T(8,128)(2,1)S(1)}, u32[]{:S(2)}, u32[]{:S(2)}) collective-permute-start(bf16[2,256,1024]{2,1,0:T(8,128)(2,1)S(1)} %pad_maximum_fusion.15), channel_id=1, source_target_pairs={{0,16},{8,24},{16,0},{24,8},{1,17},{9,25},{17,1},{25,9},{2,18},{10... | collective-permute-start | bytes 3145736 | tf_op jit(solution)/shard_map/ppermute | solution.py:703
  485.2 25.6 %collective-permute-start.69 = (bf16[128,2048]{1,0:T(8,128)(2,1)S(1)}, bf16[128,2048]{1,0:T(8,128)(2,1)S(1)}, u32[]{:S(2)}, u32[]{:S(2)}) collective-permute-start(bf16[128,2048]{1,0:T(8,128)(2,1)S(1)} %add_convert_fusion.4), channel_id=1, source_target_pairs={{0,2},{1,3},{2,0},{3,1},{4,6},{5,7},{6,4},{7,5},{8,10},{9,11},{10,... | collective-permute-start | bytes 1572872 | tf_op jit(solution)/shard_map/ppermute | solution.py:66
  489.7 52.2 %collective-permute-start.73 = (bf16[2,4,128,1024]{3,2,0,1:T(8,128)(2,1)S(1)}, bf16[2,4,128,1024]{3,2,0,1:T(8,128)(2,1)S(1)}, u32[]{:S(2)}, u32[]{:S(2)}) collective-permute-start(bf16[2,4,128,1024]{3,2,0,1:T(8,128)(2,1)S(1)} %pad_maximum_fusion.5), channel_id=1, source_target_pairs={{0,16},{8,24},{16,0},{24,8},{1,17},{9,25},{17,1},{25,9},{2,18},{10... | collective-permute-start | bytes 6291464 | tf_op jit(solution)/shard_map/ppermute | solution.py:703
  491.2 51.9 %collective-permute-start.72 = (bf16[2,4,128,1024]{3,2,0,1:T(8,128)(2,1)S(1)}, bf16[2,4,128,1024]{3,2,0,1:T(8,128)(2,1)S(1)}, u32[]{:S(2)}, u32[]{:S(2)}) collective-permute-start(bf16[2,4,128,1024]{3,2,0,1:T(8,128)(2,1)S(1)} %pad_maximum_fusion.4), channel_id=1, source_target_pairs={{0,8},{8,0},{16,24},{24,16},{1,9},{9,1},{17,25},{25,17},{2,10},{10... | collective-permute-start | bytes 6291464 | tf_op jit(solution)/shard_map/ppermute | solution.py:703
  514.0 41.8 %collective-permute-start.70 = (bf16[128,2048]{1,0:T(8,128)(2,1)S(1)}, bf16[128,2048]{1,0:T(8,128)(2,1)S(1)}, u32[]{:S(2)}, u32[]{:S(2)}) collective-permute-start(bf16[128,2048]{1,0:T(8,128)(2,1)S(1)} %get-tuple-element.363), channel_id=1, source_target_pairs={{0,4},{4,0},{1,5},{5,1},{2,6},{6,2},{3,7},{7,3},{8,12},{12,8},{9,1... | collective-permute-start | bytes 1572872 | tf_op jit(solution)/shard_map/ppermute | solution.py:63
  515.2 39.1 %collective-permute-start.79 = (bf16[1,256,1024]{2,1,0:T(8,128)(2,1)S(1)}, bf16[1,256,1024]{2,1,0:T(8,128)(2,1)S(1)}, u32[]{:S(2)}, u32[]{:S(2)}) collective-permute-start(bf16[1,256,1024]{2,1,0:T(8,128)(2,1)S(1)} %get-tuple-element.388), channel_id=1, source_target_pairs={{0,8},{8,0},{16,24},{24,16},{1,9},{9,1},{17,25},{25,17},{2,10},{10... | collective-permute-start | bytes 1572872 | tf_op jit(solution)/shard_map/ppermute | solution.py:703
  546.2 33.2 %collective-permute-start.77 = (bf16[1,4,128,1024]{3,2,0,1:T(8,128)(2,1)}, bf16[1,4,128,1024]{3,2,0,1:T(8,128)(2,1)}, u32[]{:S(2)}, u32[]{:S(2)}) collective-permute-start(bf16[1,4,128,1024]{3,2,0,1:T(8,128)(2,1)} %fusion.46), channel_id=1, source_target_pairs={{0,8},{8,0},{16,24},{24,16},{1,9},{9,1},{17,25},{25,17},{2,10},{10... | collective-permute-start | bytes 3145736 | tf_op jit(solution)/shard_map/ppermute | solution.py:703
  547.7 31.7 %collective-permute-start.76 = (bf16[1,4,128,1024]{3,2,0,1:T(8,128)(2,1)}, bf16[1,4,128,1024]{3,2,0,1:T(8,128)(2,1)}, u32[]{:S(2)}, u32[]{:S(2)}) collective-permute-start(bf16[1,4,128,1024]{3,2,0,1:T(8,128)(2,1)} %fusion.47), channel_id=1, source_target_pairs={{0,16},{8,24},{16,0},{24,8},{1,17},{9,25},{17,1},{25,9},{2,18},{10... | collective-permute-start | bytes 3145736 | tf_op jit(solution)/shard_map/ppermute | solution.py:703
  548.2 31.1 %collective-permute-start.75 = (bf16[128,2048]{1,0:T(8,128)(2,1)S(1)}, bf16[128,2048]{1,0:T(8,128)(2,1)}, u32[]{:S(2)}, u32[]{:S(2)}) collective-permute-start(bf16[128,2048]{1,0:T(8,128)(2,1)S(1)} %get-tuple-element.363), channel_id=1, source_target_pairs={{1,0},{2,1},{3,2},{5,4},{6,5},{7,6},{9,8},{10,9},{11,10},{13,12},{... | collective-permute-start | bytes 1572872 | tf_op jit(solution)/shard_map/ppermute | solution.py:66
  628.2 208.9 %all-gather.14.cloned.1.call-start = ((), (), s32[]{:S(2)}) async-start(), calls=%async_computation.3 | async-start | bytes 10485760 | tf_op jit(solution)/shard_map/all_gather | solution.py:698
  643.2 38.4 %collective-permute-start.95 = (bf16[2,128,1024]{2,1,0:T(8,128)(2,1)}, bf16[2,128,1024]{2,1,0:T(8,128)(2,1)S(1)}, u32[]{:S(2)}, u32[]{:S(2)}) collective-permute-start(bf16[2,128,1024]{2,1,0:T(8,128)(2,1)} %get-tuple-element.417), channel_id=1, source_target_pairs={{0,2},{1,3},{2,0},{3,1},{4,6},{5,7},{6,4},{7,5},{8,10},{9,11},{10,... | collective-permute-start | bytes 1572872 | tf_op jit(solution)/shard_map/ppermute | solution.py:63
  645.2 37.1 %collective-permute-start.94 = (bf16[2,128,1024]{2,1,0:T(8,128)(2,1)}, bf16[2,128,1024]{2,1,0:T(8,128)(2,1)S(1)}, u32[]{:S(2)}, u32[]{:S(2)}) collective-permute-start(bf16[2,128,1024]{2,1,0:T(8,128)(2,1)} %get-tuple-element.418), channel_id=1, source_target_pairs={{0,3},{1,0},{2,1},{3,2},{4,7},{5,4},{6,5},{7,6},{8,11},{9,8},{10,9... | collective-permute-start | bytes 1572872 | tf_op jit(solution)/shard_map/ppermute | solution.py:63
  690.8 34.1 %collective-permute-start.102 = (bf16[2,4,128,512]{3,2,1,0:T(8,128)(2,1)S(1)}, bf16[2,4,128,512]{3,2,1,0:T(8,128)(2,1)S(1)}, u32[]{:S(2)}, u32[]{:S(2)}) collective-permute-start(bf16[2,4,128,512]{3,2,1,0:T(8,128)(2,1)S(1)} %pad_maximum_fusion.16), channel_id=1, source_target_pairs={{0,8},{8,0},{16,24},{24,16},{1,9},{9,1},{17,25},{25,17},{2,10},{10... | collective-permute-start | bytes 3145736 | tf_op jit(solution)/shard_map/ppermute | solution.py:703
  692.4 35.0 %collective-permute-start.103 = (bf16[2,4,128,512]{3,2,1,0:T(8,128)(2,1)S(1)}, bf16[2,4,128,512]{3,2,1,0:T(8,128)(2,1)S(1)}, u32[]{:S(2)}, u32[]{:S(2)}) collective-permute-start(bf16[2,4,128,512]{3,2,1,0:T(8,128)(2,1)S(1)} %pad_maximum_fusion.17), channel_id=1, source_target_pairs={{0,16},{8,24},{16,0},{24,8},{1,17},{9,25},{17,1},{25,9},{2,18},{10... | collective-permute-start | bytes 3145736 | tf_op jit(solution)/shard_map/ppermute | solution.py:703
  727.5 28.2 %collective-permute-start.104 = (bf16[1,4,128,512]{3,2,1,0:T(8,128)(2,1)S(1)}, bf16[1,4,128,512]{3,2,1,0:T(8,128)(2,1)S(1)}, u32[]{:S(2)}, u32[]{:S(2)}) collective-permute-start(bf16[1,4,128,512]{3,2,1,0:T(8,128)(2,1)S(1)} %fusion.145), channel_id=1, source_target_pairs={{0,16},{8,24},{16,0},{24,8},{1,17},{9,25},{17,1},{25,9},{2,18},{10... | collective-permute-start | bytes 1572872 | tf_op jit(solution)/shard_map/ppermute | solution.py:703
  727.9 27.8 %collective-permute-start.105 = (bf16[1,4,128,512]{3,2,1,0:T(8,128)(2,1)S(1)}, bf16[1,4,128,512]{3,2,1,0:T(8,128)(2,1)S(1)}, u32[]{:S(2)}, u32[]{:S(2)}) collective-permute-start(bf16[1,4,128,512]{3,2,1,0:T(8,128)(2,1)S(1)} %fusion.146), channel_id=1, source_target_pairs={{0,8},{8,0},{16,24},{24,16},{1,9},{9,1},{17,25},{25,17},{2,10},{10... | collective-permute-start | bytes 1572872 | tf_op jit(solution)/shard_map/ppermute | solution.py:703
  729.6 35.5 %collective-permute-start.109 = (bf16[512,512]{1,0:T(8,128)(2,1)S(1)}, bf16[512,512]{1,0:T(8,128)(2,1)S(1)}, u32[]{:S(2)}, u32[]{:S(2)}) collective-permute-start(bf16[512,512]{1,0:T(8,128)(2,1)S(1)} %get-tuple-element.353), channel_id=1, source_target_pairs={{1,0},{2,1},{3,2},{5,4},{6,5},{7,6},{9,8},{10,9},{11,10},{13,12},{... | collective-permute-start | bytes 1572872 | tf_op jit(solution)/shard_map/ppermute | solution.py:66
  730.9 52.6 %collective-permute-start.110 = (bf16[512,512]{1,0:T(8,128)(2,1)S(1)}, bf16[512,512]{1,0:T(8,128)(2,1)S(1)}, u32[]{:S(2)}, u32[]{:S(2)}) collective-permute-start(bf16[512,512]{1,0:T(8,128)(2,1)S(1)} %get-tuple-element.354), channel_id=1, source_target_pairs={{0,1},{1,2},{2,3},{4,5},{5,6},{6,7},{8,9},{9,10},{10,11},{12,13},{... | collective-permute-start | bytes 1572872 | tf_op jit(solution)/shard_map/ppermute | solution.py:66
  754.2 43.6 %collective-permute-start.111 = (bf16[512,512]{1,0:T(8,128)(2,1)S(1)}, bf16[512,512]{1,0:T(8,128)(2,1)S(1)}, u32[]{:S(2)}, u32[]{:S(2)}) collective-permute-start(bf16[512,512]{1,0:T(8,128)(2,1)S(1)} %add_convert_fusion.3), channel_id=1, source_target_pairs={{0,2},{1,3},{2,0},{3,1},{4,6},{5,7},{6,4},{7,5},{8,10},{9,11},{10,... | collective-permute-start | bytes 1572872 | tf_op jit(solution)/shard_map/ppermute | solution.py:66
  757.1 49.8 %collective-permute-start.108 = (bf16[128,1024]{1,0:T(8,128)(2,1)}, bf16[128,1024]{1,0:T(8,128)(2,1)S(1)}, u32[]{:S(2)}, u32[]{:S(2)}) collective-permute-start(bf16[128,1024]{1,0:T(8,128)(2,1)} %get-tuple-element.431), channel_id=1, source_target_pairs={{0,1},{1,2},{2,3},{3,0},{4,5},{5,6},{6,7},{7,4},{8,9},{9,10},{10,1... | collective-permute-start | bytes 786440 | tf_op jit(solution)/shard_map/ppermute | solution.py:63
  765.1 41.7 %collective-permute-start.106 = (bf16[128,1024]{1,0:T(8,128)(2,1)}, bf16[128,1024]{1,0:T(8,128)(2,1)}, u32[]{:S(2)}, u32[]{:S(2)}) collective-permute-start(bf16[128,1024]{1,0:T(8,128)(2,1)} %get-tuple-element.433), channel_id=1, source_target_pairs={{0,3},{1,0},{2,1},{3,2},{4,7},{5,4},{6,5},{7,6},{8,11},{9,8},{10,9... | collective-permute-start | bytes 786440 | tf_op jit(solution)/shard_map/ppermute | solution.py:63
  765.1 41.7 %collective-permute-start.107 = (bf16[128,1024]{1,0:T(8,128)(2,1)S(1)}, bf16[128,1024]{1,0:T(8,128)(2,1)}, u32[]{:S(2)}, u32[]{:S(2)}) collective-permute-start(bf16[128,1024]{1,0:T(8,128)(2,1)S(1)} %get-tuple-element.434), channel_id=1, source_target_pairs={{0,2},{1,3},{2,0},{3,1},{4,6},{5,7},{6,4},{7,5},{8,10},{9,11},{10,... | collective-permute-start | bytes 786440 | tf_op jit(solution)/shard_map/ppermute | solution.py:63
  (184 other events, 2140.9 us)
Sparse Core Ops, SparseCore 0:
  145.7 53.2 all-gather.7
  210.1 86.3 all-gather.9
  628.4 50.0 all-gather.11
  687.2 116.1 all-gather.13

commit v3 on v2

--- a/solution.py
+++ b/solution.py
@@ -127,13 +127,13 @@
     return near, early, beside
 
 
-def reduce_near(col, blocks, between=()):
+def reduce_near(col, blocks, between=(), beside=()):
     low = [block.astype(BF) for block in blocks]
     result = blocks[0]
     if col.size != 4:
         for k in range(1, col.size):
             result = result + col.give(low[k], k).astype(F32)
-        return result, between
+        return result, between, beside
     relayed = col.send(low[3], [(3, 2), (0, 1)])
     below = col.send(low[1], [(0, 1), (1, 2), (2, 3)])
     above = col.send(
@@ -142,7 +142,9 @@
     two = (blocks[2] + relayed.astype(F32)).astype(BF)
     two, between = lax.optimization_barrier((two, between))
     two = col.send(two, [(0, 2), (1, 3), (2, 0), (3, 1)])
-    return result + above.astype(F32) + below.astype(F32) + two.astype(F32), between
+    above, below, beside = lax.optimization_barrier((above, below, beside))
+    result = result + above.astype(F32) + below.astype(F32) + two.astype(F32)
+    return result, between, beside
 
 
 def block_at(values, index, size, axis):
@@ -250,17 +252,23 @@
 
 
 def pair_gradients_kernel(all_ref, gate_ref, up_ref):
-    gate_ref[...] = all_ref[0, 0, 0].astype(F32)
-    up_ref[...] = all_ref[0, 0, 1].astype(F32)
+    hidden = all_ref.shape[4]
+    for k in range(all_ref.shape[1]):
+        place = slice(k * hidden, (k + 1) * hidden)
+        gate_ref[:, place] = all_ref[0, k, 0].astype(F32)
+        up_ref[:, place] = all_ref[0, k, 1].astype(F32)
 
 
 def pair_gradients(gathered):
     n_dp, n_col, pair, rows, hidden = gathered.shape
-    side = pl.BlockSpec((rows, hidden), lambda p, z: (p, z))
+    cut = 2 if rows % 32 == 0 else 1
+    side = pl.BlockSpec((rows // cut, n_col * hidden), lambda p, i: (p * cut + i, 0))
     return pl.pallas_call(
         pair_gradients_kernel,
-        grid=(n_dp, n_col),
-        in_specs=[pl.BlockSpec((1, 1, pair, rows, hidden), lambda p, z: (p, z, 0, 0, 0))],
+        grid=(n_dp, cut),
+        in_specs=[
+            pl.BlockSpec((1, n_col, pair, rows // cut, hidden), lambda p, i: (p, 0, 0, i, 0))
+        ],
         out_specs=[side, side],
         out_shape=[jax.ShapeDtypeStruct((n_dp * rows, n_col * hidden), F32)] * 2,
         compiler_params=pltpu.CompilerParams(vmem_limit_bytes=56 << 20),
@@ -269,6 +277,28 @@
         ),
         name="pair_gradients",
     )(gathered)
+
+
+def down_gradients_kernel(all_ref, down_ref):
+    down_ref[...] = all_ref[...].astype(F32)
+
+
+def down_gradients(gathered):
+    n_dp, n_col, rows, features = gathered.shape
+    block = (1, 1, rows, features)
+    whole = pl.pallas_call(
+        down_gradients_kernel,
+        grid=(n_dp, n_col),
+        in_specs=[pl.BlockSpec(block, lambda p, z: (p, z, 0, 0))],
+        out_specs=pl.BlockSpec(block, lambda p, z: (z, p, 0, 0)),
+        out_shape=jax.ShapeDtypeStruct((n_col, n_dp, rows, features), F32),
+        compiler_params=pltpu.CompilerParams(vmem_limit_bytes=56 << 20),
+        cost_estimate=pl.CostEstimate(
+            flops=0, bytes_accessed=6 * math.prod(gathered.shape), transcendentals=0
+        ),
+        name="down_gradients",
+    )(gathered)
+    return whole.reshape(-1, features)
 
 
 def last_gradients_kernel(n_out, places_ref, *refs):
@@ -788,18 +818,20 @@
         turned_positions = from_here(row, positions, row_tokens, 0)
         slots = lax.rem(jnp.arange(length) + row.here * row_tokens, length)
         tables = rope_tables(turned_positions)
+        first_parts, layer_input = lax.optimization_barrier((first_parts, layer_input))
+        near, _, tables = gather_col(col, layer_input, (), tables)
         if n_dp == 4:
             pieces, _ = gather_four(jnp.stack(first_parts))
-            near, arrived, tables = gather_col(col, layer_input, pieces[1] + pieces[2], tables)
-            pieces = pieces[0] + arrived + pieces[3]
+            pieces = sum(pieces, [])
             w_qkv, w_out_all = first_weights(dp, col.here, pieces, 3 * head_cols, n_out)
         else:
-            near, _, tables = gather_col(col, layer_input, (), tables)
             first = gather_dp(jnp.stack(first_parts)[None])
             w_qkv = first[..., : 3 * head_cols].swapaxes(0, 1).reshape(n_col, features, -1)
             w_out_all = first[..., 3 * head_cols :].reshape(n_dp, n_col, n_out, out_rows, -1)
             w_out_all = w_out_all.transpose(0, 3, 1, 2, 4).reshape(head_cols, width)
             w_out_all = to_order(col, w_out_all, features, 1)
+        w_down = after(w_down, near)
+        down_parts = exchange(col, down_block)
         w_qkv = [w_qkv[k] for k in range(n_col)]
         input_rows = [
             jnp.concatenate([row.fetch(block, j) for j in range(n_row)], axis=0)
@@ -807,24 +839,23 @@
         ]
         own_input = own_rows(col, near).astype(F32)
 
-        w_down = after(w_down, near)
-        down_parts = exchange(col, down_block)
-
         raw = sum(dot(rows, w) for rows, w in zip(input_rows, w_qkv))
         query_raw = raw[:, :head_cols]
         key_raw = raw[:, head_cols : 2 * head_cols]
         squares = jnp.stack(
             [jnp.sum(query_raw * query_raw, axis=1), jnp.sum(key_raw * key_raw, axis=1)]
         )
+        squares, down_parts = lax.optimization_barrier((squares, down_parts))
+        down_parts = assemble(col, down_parts, 1)
         gains = jnp.stack([gain_attn, gain_ffn])
         squares, gains = sum_all(row, col, squares, lambda index: gains)
         squares, w_out_all, down_parts = lax.optimization_barrier(
             (squares, w_out_all, down_parts)
         )
-        w_down_all = gather_dp(assemble(col, down_parts, 1))
+        w_down_all = gather_dp(down_parts)
         gains = assemble(col, gains, 1)
         gain_attn_all, gain_ffn_all = gains[0:1], gains[1:2]
-        w_gate, w_up = after((w_gate, w_up), down_parts)
+        w_gate, w_up = after((w_gate, w_up), squares)
         gate_up_parts = exchange(col, gate_up_block)
 
         scales = lax.rsqrt(squares / width + EPSILON)
@@ -833,7 +864,7 @@
         marks = jnp.stack([turned_docs, slots]).astype(F32)
         lines = jnp.concatenate([scales, marks, jnp.zeros((4, length), F32)], axis=0)
         *saved, mixture = attend_forward(row, col, raw, lines, head_gains, tables)
-        gate_up_parts, mixture = lax.optimization_barrier((gate_up_parts, mixture))
+        gate_up_parts[1::2], mixture = lax.optimization_barrier((gate_up_parts[1::2], mixture))
         attended = []
         for k in range(n_col):
             total, *others = (
@@ -843,11 +874,12 @@
             for j, other in enumerate(others):
                 total = total + row.give(other.astype(BF), j + 1).astype(F32)
             attended.append(total)
+        gate_up_parts, attended = lax.optimization_barrier((gate_up_parts, attended))
         gate_up_parts = assemble(
             col, [part[:, None] for part in after(gate_up_parts, w_down_all)], 1
         )
         gate_up_parts, attended = lax.optimization_barrier((gate_up_parts, attended))
-        attended, _ = reduce_near(col, attended)
+        attended, _, _ = reduce_near(col, attended)
         w_gate_up = lax.all_gather(gate_up_parts[:, :, None], "dp", axis=2, tiled=True)
         w_gate_up = w_gate_up.reshape(2, width, hidden_cols)
         attn_scale = rms_scale(attended)
@@ -870,7 +902,7 @@
         lowered = [sum_rows(row, dot(block, w_down_all)) for block in activated]
         lowered, cotangent = lax.optimization_barrier((lowered, cotangent))
         cotangent = assemble(col, cotangent, 1).astype(F32)
-        lowered, _ = reduce_near(col, lowered)
+        lowered, _, _ = reduce_near(col, lowered)
         ffn_scale = rms_scale(lowered)
         own_output = (hidden_state + lowered * ffn_scale * gain_ffn_all).astype(BF)
 
@@ -908,7 +940,9 @@
             .reshape(n_col, n_dp, in_rows, hidden_cols)
             for grads in (gate_grads, up_grads)
         ]
-        state_part, gate_up_grads = reduce_near(col, state_part, gate_up_grads)
+        state_part, _, gate_up_grads = reduce_near(
+            col, state_part, grad_w_down, gate_up_grads
+        )
         gate_up_sum = GroupSum(
             lambda index: [
                 lax.dynamic_index_in_dim(grads, index, 1, False) for grads in gate_up_grads
@@ -919,14 +953,12 @@
         grad_attended, grad_gain_attn = rms_back(
             grad_state, attended, attn_scale, gain_attn_all
         )
-
-        def second_step(came):
-            gate_up_sum.came = came
-            gate_up_sum.land(())
-            return gate_up_sum.came, down_sum.came
-
-        attended_rows, _, (gate_up_sum.came, down_sum.came) = gather_tokens(
-            row, col, grad_attended.astype(BF), gate_up_sum.came, second_step
+        attended_rows, (gate_up_sum.came, down_sum.came), _ = gather_tokens(
+            row, col, grad_attended.astype(BF), (gate_up_sum.came, down_sum.came)
+        )
+        gate_up_sum.land(())
+        gate_up_sum.came, attended_rows = lax.optimization_barrier(
+            (gate_up_sum.came, attended_rows)
         )
         down_parts, _ = down_sum.finish(())
         down_parts = jnp.concatenate(down_parts, axis=1)
@@ -991,25 +1023,27 @@
                 )
             )
 
-        qkv_grads, out_grads, small, gate_up_parts, grad_qkv = lax.optimization_barrier(
-            (qkv_grads, out_grads, small, gate_up_parts, grad_qkv)
+        qkv_grads, out_grads, small, grad_qkv = lax.optimization_barrier(
+            (qkv_grads, out_grads, small, grad_qkv)
         )
         last_sum = GroupSum(last_block)
+        input_part = [dot_nt(grad_qkv, w) for w in w_qkv]
+        gate_up_parts, last_sum.came, input_part = lax.optimization_barrier(
+            (gate_up_parts, last_sum.came, input_part)
+        )
+        last_sum.land(())
         gate_up_back = assemble(
             col, [part[None] for part in after(gate_up_parts, down_back)], 0
         )
         gate_up_all = gather_dp(gate_up_back[None])
-        input_part = [sum_rows(row, dot_nt(grad_qkv, w)) for w in w_qkv]
+        input_part = [sum_rows(row, partial) for partial in input_part]
         gate_up_back, input_part = lax.optimization_barrier((gate_up_back, input_part))
-        grad_input, last_sum.came = reduce_near(
-            col, by_arrival(col, input_part), last_sum.came
-        )
         last_sum, _ = last_sum.finish(())
         last_sum = jnp.concatenate(last_sum, axis=-1)
         last_parts = [col.fetch(last_sum[-k % n_col], k) for k in range(n_col)]
-        grad_w_down = down_all.swapaxes(0, 1).reshape(w_down.shape).astype(F32)
-        last_parts, grad_w_down, grad_input = lax.optimization_barrier(
-            (last_parts, grad_w_down, grad_input)
+        grad_w_down = down_gradients(down_all)
+        grad_input, (last_parts, grad_w_down), _ = reduce_near(
+            col, by_arrival(col, input_part), (last_parts, grad_w_down)
         )
         own_output, grad_state = after((own_output, grad_state), last_parts)
         own_state = grad_state.astype(BF)

time: 874 us -> 840 us (0.961)
  starting transfers between devices: 211 us -> 160 us
  local copies, waits for them, and re-layouts: 60.4 us -> 44.9 us
  waiting for transfers between devices: 382 us -> 396 us
  Pallas kernels: 54.2 us -> 64.7 us
    ppermute x22, waiting for transfers between devices: 47.8 us -> 109 us  [partner(): return lax.ppermute(values, 'dp', [(i, i ^ step) for i in range(n_dp)])]
    ppermute x32, waiting for transfers between devices: 214 us -> 180 us  [send(): return lax.ppermute(values, self.name, pairs)]
    ppermute x32, starting transfers between devices: 100 us -> 72.1 us  [send(): return lax.ppermute(values, self.name, pairs)]
    ppermute x68, waiting for transfers between devices: 110 us -> 85.1 us  [fetch(): return lax.ppermute(values, self.name, pairs)]
    ppermute x68, starting transfers between devices: 85.8 us -> 61.5 us  [fetch(): return lax.ppermute(values, self.name, pairs)]
    unnamed x225 -> x199, local copies, waits for them, and re-layouts: 31.4 us -> 20.9 us
    all_gather x3, waiting for transfers between devices: 0.01 us -> 8.97 us  [gather_dp(): return lax.all_gather(values, 'dp', axis=0, tiled=True)]
    pallas_call x1 -> x2, Pallas kernels: 13.1 us -> 21.2 us  [the longest x1 10.9 us: down_gradients(): pl.pallas_call(down_gradients_kernel, grid=(n_dp, n_col), in_specs=[pl.Bl...]
  transfers between devices with their start and end apart: 126 -> 126, of which waited for: 49 -> 56; matrix products, arithmetic and copies ran while one was open for 20% -> 21% of each run, Pallas kernels for 5% -> 7%
where the time goes in v3:
time: 840 us; the launch traced here: 828 us
  waiting for transfers between devices  396 us (47%)
  starting transfers between devices  160 us (19%)
  matrix products  91.4 us (11%)
  Pallas kernels  64.7 us (8%)
  other arithmetic  54.7 us (7%)
  local copies, waits for them, and re-layouts  44.9 us (5%)
  between operations  17.3 us (2%)
    ppermute x32, waiting for transfers between devices, send(): return lax.ppermute(values, self.name, pairs)  180 us
    ppermute x22, waiting for transfers between devices, partner(): return lax.ppermute(values, 'dp', [(i, i ^ step) for i in range(n_dp)])  109 us
    ppermute x68, waiting for transfers between devices, fetch(): return lax.ppermute(values, self.name, pairs)  85.1 us
    ppermute x32, starting transfers between devices, send(): return lax.ppermute(values, self.name, pairs)  72.1 us
    ppermute x68, starting transfers between devices, fetch(): return lax.ppermute(values, self.name, pairs)  61.5 us
    dot_general x20, matrix products, dot_nt(): lax.dot_general(a, b, (((1,), (1,)), ((), ())), preferred_element_type=F32)  37.5 us
    dot_general x24, matrix products, dot(): return jnp.dot(a, b, preferred_element_type=F32)  31.5 us
    ppermute x22, starting transfers between devices, partner(): return lax.ppermute(values, 'dp', [(i, i ^ step) for i in range(n_dp)])  25.8 us
  transfers between devices with their start and end apart: 126, of which 56 were waited for; matrix products, arithmetic and copies ran while one was open for 21% of the time, Pallas kernels for 7%

profile of v3, /device:TPU:0, one launch (start us, length us, event | category | flops | bytes accessed | tf_op | source)
XLA Modules:
  0.0 828.2 jit_solution(8706652152824771182)
XLA Ops:
  17.3 10.9 %collective-permute-done.1 = bf16[128,1024]{1,0:T(8,128)(2,1)S(1)} collective-permute-done((bf16[128,1024]{1,0:T(8,128)(2,1)S(1)}, bf16[128,1024]{1,0:T(8,128)(2,1)S(1)}, u32[]{:S(2)}, u32[]{:S(2)}) %collective-permute-start.1) | collective-permute-done | bytes 262176 | tf_op jit(solution)/shard_map/ppermute | solution.py:63
  28.2 5.1 collective-permute-done.2
  33.3 7.1 collective-permute-start.3
  42.3 5.4 collective-permute-start.4
  51.5 12.8 %collective-permute-done.3.refs_2_ = bf16[512,512]{1,0:T(8,128)(2,1)} collective-permute-done((bf16[512,512]{1,0:T(8,128)(2,1)}, bf16[512,512]{1,0:T(8,128)(2,1)}, u32[]{:S(2)}, u32[]{:S(2)}) %collective-permute-start.3) | collective-permute-done | bytes 524320 | tf_op jit(solution)/shard_map/ppermute | solution.py:66
  75.8 13.7 %collective-permute-done.6 = bf16[512,512]{1,0:T(8,128)(2,1)} collective-permute-done((bf16[512,512]{1,0:T(8,128)(2,1)}, bf16[512,512]{1,0:T(8,128)(2,1)}, u32[]{:S(2)}, u32[]{:S(2)}) %collective-permute-start.6) | collective-permute-done | bytes 524320 | tf_op jit(solution)/shard_map/ppermute | solution.py:66
  106.2 8.0 collective-permute-done.16.refs_2_
  115.4 5.4 collective-permute-start.21
  133.5 11.6 %attend_forward.1 = (bf16[1024,256]{1,0:T(8,128)(2,1)}, bf16[1024,256]{1,0:T(8,128)(2,1)}, bf16[1024,256]{1,0:T(8,128)(2,1)}, bf16[1024,256]{1,0:T(8,128)(2,1)}) custom-call(s32[1]{0:T(128)} %bitcast.here_ref, f32[1024,768]{1,0:T(8,128)} %copy-done.13, f32[1024,768]{1,0:T(8,128)} %copy-done.13, f32[1024,768]{1,0:T(8,128)} %copy-done.13, ...), custom_call_target="tpu_custom_call" | custom-call | flops 1073741824 | bytes 5242880 | tf_op jit(solution)/shard_map/attend_forward/pallas_call | solution.py:637
  145.2 7.6 collective-permute-done.22
  165.1 9.7 %collective-permute-done.24 = bf16[2,128,1024]{2,1,0:T(8,128)(2,1)S(1)} collective-permute-done((bf16[2,128,1024]{2,1,0:T(8,128)(2,1)S(1)}, bf16[2,128,1024]{2,1,0:T(8,128)(2,1)S(1)}, u32[]{:S(2)}, u32[]{:S(2)}) %collective-permute-start.24) | collective-permute-done | bytes 524320 | tf_op jit(solution)/shard_map/ppermute | solution.py:63
  190.6 8.8 %collective-permute-done.31 = bf16[128,2048]{1,0:T(8,128)(2,1)S(1)} collective-permute-done((bf16[128,2048]{1,0:T(8,128)(2,1)}, bf16[128,2048]{1,0:T(8,128)(2,1)S(1)}, u32[]{:S(2)}, u32[]{:S(2)}) %collective-permute-start.31) | collective-permute-done | bytes 524320 | tf_op jit(solution)/shard_map/ppermute | solution.py:66
  204.6 6.1 collective-permute-done.30
  210.7 17.9 %collective-permute-done.32 = bf16[128,2048]{1,0:T(8,128)(2,1)S(1)} collective-permute-done((bf16[128,2048]{1,0:T(8,128)(2,1)S(1)}, bf16[128,2048]{1,0:T(8,128)(2,1)S(1)}, u32[]{:S(2)}, u32[]{:S(2)}) %collective-permute-start.32) | collective-permute-done | bytes 524320 | tf_op jit(solution)/shard_map/ppermute | solution.py:66
  232.5 4.6 collective-permute-start.35
  237.1 14.3 %collective-permute-done.34 = bf16[128,2048]{1,0:T(8,128)(2,1)S(1)} collective-permute-done((bf16[128,2048]{1,0:T(8,128)(2,1)}, bf16[128,2048]{1,0:T(8,128)(2,1)S(1)}, u32[]{:S(2)}, u32[]{:S(2)}) %collective-permute-start.34) | collective-permute-done | bytes 524320 | tf_op jit(solution)/shard_map/ppermute | solution.py:66
  253.3 5.5 collective-permute-done.36
  258.9 12.2 %all-gather.10.cloned.1.call-done = bf16[2,4,512,1024]{3,2,1,0:T(8,128)(2,1)} async-done(((bf16[2,4,128,1024]{3,2,1,0:T(8,128)(2,1)}), bf16[2,4,512,1024]{3,2,1,0:T(8,128)(2,1)}) %all-gather.10.cloned.1.call-update) | async-done | bytes 8388624 | tf_op jit(solution)/shard_map/all_gather | solution.py:883
  318.2 9.6 %collective-permute-done.50 = bf16[128,2048]{1,0:T(8,128)(2,1)S(1)} collective-permute-done((bf16[128,2048]{1,0:T(8,128)(2,1)S(1)}, bf16[128,2048]{1,0:T(8,128)(2,1)S(1)}, u32[]{:S(2)}, u32[]{:S(2)}) %collective-permute-start.50) | collective-permute-done | bytes 524320 | tf_op jit(solution)/shard_map/ppermute | solution.py:66
  333.8 5.2 collective-permute-done.49
  339.0 16.5 %collective-permute-done.51 = bf16[128,2048]{1,0:T(8,128)(2,1)S(1)} collective-permute-done((bf16[128,2048]{1,0:T(8,128)(2,1)S(1)}, bf16[128,2048]{1,0:T(8,128)(2,1)S(1)}, u32[]{:S(2)}, u32[]{:S(2)}) %collective-permute-start.51) | collective-permute-done | bytes 524320 | tf_op jit(solution)/shard_map/ppermute | solution.py:66
  368.2 12.7 %collective-permute-done.52 = bf16[128,2048]{1,0:T(8,128)(2,1)} collective-permute-done((bf16[128,2048]{1,0:T(8,128)(2,1)}, bf16[128,2048]{1,0:T(8,128)(2,1)}, u32[]{:S(2)}, u32[]{:S(2)}) %collective-permute-start.52) | collective-permute-done | bytes 524320 | tf_op jit(solution)/shard_map/ppermute | solution.py:66
  401.2 5.5 collective-permute-done.57
  424.6 4.6 collective-permute-start.68
  430.9 5.0 collective-permute-start.61
  435.9 5.5 collective-permute-done.68
  441.6 4.9 convolution_convert_fusion.2
  452.8 4.9 convolution_convert_fusion
  457.7 4.9 convolution_convert_fusion.1
  483.6 22.3 %collective-permute-done.70 = bf16[128,2048]{1,0:T(8,128)(2,1)} collective-permute-done((bf16[128,2048]{1,0:T(8,128)(2,1)S(1)}, bf16[128,2048]{1,0:T(8,128)(2,1)}, u32[]{:S(2)}, u32[]{:S(2)}) %collective-permute-start.70) | collective-permute-done | bytes 524320 | tf_op jit(solution)/shard_map/ppermute | solution.py:66
  507.3 23.3 %collective-permute-done.74 = bf16[1,256,1024]{2,1,0:T(8,128)(2,1)S(1)} collective-permute-done((bf16[1,256,1024]{2,1,0:T(8,128)(2,1)}, bf16[1,256,1024]{2,1,0:T(8,128)(2,1)S(1)}, u32[]{:S(2)}, u32[]{:S(2)}) %collective-permute-start.74) | collective-permute-done | bytes 524320 | tf_op jit(solution)/shard_map/ppermute | solution.py:733
  533.2 8.9 %collective-permute-done.73 = bf16[1,256,1024]{2,1,0:T(8,128)(2,1)S(1)} collective-permute-done((bf16[1,256,1024]{2,1,0:T(8,128)(2,1)S(1)}, bf16[1,256,1024]{2,1,0:T(8,128)(2,1)S(1)}, u32[]{:S(2)}, u32[]{:S(2)}) %collective-permute-start.73) | collective-permute-done | bytes 524320 | tf_op jit(solution)/shard_map/ppermute | solution.py:733
  549.8 5.2 collective-permute-done.82
  564.4 6.7 collective-permute-done.76
  579.4 14.3 %attend_backward.1 = (f32[1024,256]{1,0:T(8,128)}, f32[1024,256]{1,0:T(8,128)}, bf16[1024,256]{1,0:T(8,128)(2,1)}, f32[8,1024]{1,0:T(8,128)}, f32[2,1,128]{2,1,0:T(1,128)}, /*index=5*/f32[2,1,128]{2,1,0:T(1,128)}) custom-call(s32[1]{0:T(128)} %bitcast.here_ref, f32[1024,768]{1,0:T(8,128)} %copy-done.13, f32[1024,768]{1,0:T(8,128)} %copy-done.13, ...), custom_call_target="tpu_custom_call" | custom-call | flops 2684354560 | bytes 7864320 | tf_op jit(solution)/shard_map/attend_backward/pallas_call | solution.py:669
  648.0 7.0 collective-permute-done.92
  655.0 20.2 %collective-permute-done.97 = bf16[2,4,128,512]{3,2,1,0:T(8,128)(2,1)S(1)} collective-permute-done((bf16[2,4,128,512]{3,2,1,0:T(8,128)(2,1)S(1)}, bf16[2,4,128,512]{3,2,1,0:T(8,128)(2,1)S(1)}, u32[]{:S(2)}, u32[]{:S(2)}) %collective-permute-start.97) | collective-permute-done | bytes 1048608 | tf_op jit(solution)/shard_map/ppermute | solution.py:733
  692.3 12.5 %collective-permute-done.104 = bf16[1,4,128,512]{3,2,1,0:T(8,128)(2,1)S(1)} collective-permute-done((bf16[1,4,128,512]{3,2,1,0:T(8,128)(2,1)S(1)}, bf16[1,4,128,512]{3,2,1,0:T(8,128)(2,1)S(1)}, u32[]{:S(2)}, u32[]{:S(2)}) %collective-permute-start.104) | collective-permute-done | bytes 524320 | tf_op jit(solution)/shard_map/ppermute | solution.py:733
  704.8 5.8 collective-permute-done.105
  717.8 10.9 %down_gradients.1 = f32[4,4,256,512]{3,2,1,0:T(8,128)} custom-call(bf16[4,4,256,512]{3,2,1,0:T(8,128)(2,1)} %bitcast.350), custom_call_target="tpu_custom_call" | custom-call | bytes 12582912 | tf_op jit(solution)/shard_map/down_gradients/pallas_call | solution.py:289
  728.7 7.8 collective-permute-done.107
  747.7 7.7 collective-permute-done.112.refs_2_
  756.8 5.9 collective-permute-done.115.refs_2_
  768.2 16.2 %collective-permute-done.110.refs_2_ = bf16[4,128,1024]{2,1,0:T(8,128)(2,1)S(1)} collective-permute-done((bf16[4,128,1024]{2,1,0:T(8,128)(2,1)S(1)}, bf16[4,128,1024]{2,1,0:T(8,128)(2,1)S(1)}, u32[]{:S(2)}, u32[]{:S(2)}) %collective-permute-start.110) | collective-permute-done | bytes 1048608 | tf_op jit(solution)/shard_map/ppermute | solution.py:733
  793.2 4.8 collective-permute-done.119
  799.3 5.2 all-gather.14.cloned.1.call-done
  804.5 10.2 %pair_gradients.1 = (f32[512,4096]{1,0:T(8,128)}, f32[512,4096]{1,0:T(8,128)}) custom-call(bf16[4,4,2,128,1024]{4,3,2,1,0:T(8,128)(2,1)} %bitcast.349), custom_call_target="tpu_custom_call" | custom-call | bytes 25165824 | tf_op jit(solution)/shard_map/pair_gradients/pallas_call | solution.py:266
  814.8 6.5 last_gradients.1
  (650 shorter events, 363.7 us)
Async XLA Ops:
  7.2 172.1 %all-gather.8.cloned.1.call-start = ((), (), s32[]{:S(2)}) async-start(), calls=%async_computation | async-start | bytes 5242880 | tf_op jit(solution)/shard_map/all_gather | solution.py:728
  33.3 31.0 %collective-permute-start.3 = (bf16[512,512]{1,0:T(8,128)(2,1)}, bf16[512,512]{1,0:T(8,128)(2,1)}, u32[]{:S(2)}, u32[]{:S(2)}) collective-permute-start(bf16[512,512]{1,0:T(8,128)(2,1)} %refs_0_), channel_id=1, source_target_pairs={{0,2},{1,3},{2,0},{3,1},{4,6},{5,7},{6,4},{7,5},{8,10},{9,11},{10,... | collective-permute-start | bytes 1572872 | tf_op jit(solution)/shard_map/ppermute | solution.py:66
  41.0 26.7 %collective-permute-start.5 = (bf16[512,512]{1,0:T(8,128)(2,1)}, bf16[512,512]{1,0:T(8,128)(2,1)}, u32[]{:S(2)}, u32[]{:S(2)}) collective-permute-start(bf16[512,512]{1,0:T(8,128)(2,1)} %refs_0_), channel_id=1, source_target_pairs={{1,0},{2,1},{3,2},{5,4},{6,5},{7,6},{9,8},{10,9},{11,10},{13,12},{... | collective-permute-start | bytes 1572872 | tf_op jit(solution)/shard_map/ppermute | solution.py:66
  42.3 25.5 %collective-permute-start.4 = (bf16[512,512]{1,0:T(8,128)(2,1)}, bf16[512,512]{1,0:T(8,128)(2,1)}, u32[]{:S(2)}, u32[]{:S(2)}) collective-permute-start(bf16[512,512]{1,0:T(8,128)(2,1)} %refs_0_), channel_id=1, source_target_pairs={{0,1},{1,2},{2,3},{4,5},{5,6},{6,7},{8,9},{9,10},{10,11},{12,13},{... | collective-permute-start | bytes 1572872 | tf_op jit(solution)/shard_map/ppermute | solution.py:66
  47.8 24.7 %collective-permute-start.9 = (bf16[4,128,1024]{2,1,0:T(8,128)(2,1)S(1)}, bf16[4,128,1024]{2,1,0:T(8,128)(2,1)S(1)}, u32[]{:S(2)}, u32[]{:S(2)}) collective-permute-start(bf16[4,128,1024]{2,1,0:T(8,128)(2,1)S(1)} %pad_maximum_fusion.9.refs_0_), channel_id=1, source_target_pairs={{0,16},{8,24},{16,0},{24,8},{1,17},{9,25},{17,1},{25,9},{2,18},{10... | collective-permute-start | bytes 3145736 | tf_op jit(solution)/shard_map/ppermute | solution.py:733
  125.4 145.6 %all-gather.10.cloned.1.call-start = ((), (), s32[]{:S(2)}) async-start(), calls=%async_computation.1 | async-start | bytes 10485760 | tf_op jit(solution)/shard_map/all_gather | solution.py:883
  132.1 42.6 %collective-permute-start.24 = (bf16[2,128,1024]{2,1,0:T(8,128)(2,1)S(1)}, bf16[2,128,1024]{2,1,0:T(8,128)(2,1)S(1)}, u32[]{:S(2)}, u32[]{:S(2)}) collective-permute-start(bf16[2,128,1024]{2,1,0:T(8,128)(2,1)S(1)} %pad_maximum_fusion.35), channel_id=1, source_target_pairs={{0,2},{1,3},{2,0},{3,1},{4,6},{5,7},{6,4},{7,5},{8,10},{9,11},{10,... | collective-permute-start | bytes 1572872 | tf_op jit(solution)/shard_map/ppermute | solution.py:63
  183.2 534.5 %all-gather.12.cloned.1.call-start = ((), (), s32[]{:S(2)}) async-start(), calls=%async_computation.2 | async-start | bytes 5242880 | tf_op jit(solution)/shard_map/all_gather | solution.py:728
  199.6 29.0 %collective-permute-start.32 = (bf16[128,2048]{1,0:T(8,128)(2,1)S(1)}, bf16[128,2048]{1,0:T(8,128)(2,1)S(1)}, u32[]{:S(2)}, u32[]{:S(2)}) collective-permute-start(bf16[128,2048]{1,0:T(8,128)(2,1)S(1)} %add_convert_fusion.6), channel_id=1, source_target_pairs={{0,2},{1,3},{2,0},{3,1},{4,6},{5,7},{6,4},{7,5},{8,10},{9,11},{10,... | collective-permute-start | bytes 1572872 | tf_op jit(solution)/shard_map/ppermute | solution.py:66
  231.2 27.7 %collective-permute-start.36 = (bf16[128,2048]{1,0:T(8,128)(2,1)}, bf16[128,2048]{1,0:T(8,128)(2,1)}, u32[]{:S(2)}, u32[]{:S(2)}) collective-permute-start(bf16[128,2048]{1,0:T(8,128)(2,1)} %get-tuple-element.419), channel_id=1, source_target_pairs={{1,0},{2,1},{3,2},{5,4},{6,5},{7,6},{9,8},{10,9},{11,10},{13,12},{... | collective-permute-start | bytes 1572872 | tf_op jit(solution)/shard_map/ppermute | solution.py:66
  232.5 26.4 %collective-permute-start.35 = (bf16[128,2048]{1,0:T(8,128)(2,1)}, bf16[128,2048]{1,0:T(8,128)(2,1)S(1)}, u32[]{:S(2)}, u32[]{:S(2)}) collective-permute-start(bf16[128,2048]{1,0:T(8,128)(2,1)} %get-tuple-element.419), channel_id=1, source_target_pairs={{0,1},{1,2},{2,3},{4,5},{5,6},{6,7},{8,9},{9,10},{10,11},{12,13},{... | collective-permute-start | bytes 1572872 | tf_op jit(solution)/shard_map/ppermute | solution.py:66
  271.0 27.7 %collective-permute-start.42 = (bf16[128,2048]{1,0:T(8,128)(2,1)S(1)}, bf16[128,2048]{1,0:T(8,128)(2,1)S(1)}, u32[]{:S(2)}, u32[]{:S(2)}) collective-permute-start(bf16[128,2048]{1,0:T(8,128)(2,1)S(1)} %collective-permute-done.34), channel_id=1, source_target_pairs={{2,3},{1,0},{6,7},{5,4},{10,11},{9,8},{14,15},{13,12},{18,19},{17,... | collective-permute-start | bytes 1572872 | tf_op jit(solution)/shard_map/ppermute | solution.py:66
  289.4 24.7 %collective-permute-start.47 = (bf16[128,512]{1,0:T(8,128)(2,1)S(1)}, bf16[128,512]{1,0:T(8,128)(2,1)S(1)}, u32[]{:S(2)}, u32[]{:S(2)}) collective-permute-start(bf16[128,512]{1,0:T(8,128)(2,1)S(1)} %get-tuple-element.518), channel_id=1, source_target_pairs={{0,1},{1,2},{2,3},{3,0},{4,5},{5,6},{6,7},{7,4},{8,9},{9,10},{10,1... | collective-permute-start | bytes 393224 | tf_op jit(solution)/shard_map/ppermute | solution.py:63
  327.9 27.6 %collective-permute-start.51 = (bf16[128,2048]{1,0:T(8,128)(2,1)S(1)}, bf16[128,2048]{1,0:T(8,128)(2,1)S(1)}, u32[]{:S(2)}, u32[]{:S(2)}) collective-permute-start(bf16[128,2048]{1,0:T(8,128)(2,1)S(1)} %add_convert_fusion.5), channel_id=1, source_target_pairs={{0,2},{1,3},{2,0},{3,1},{4,6},{5,7},{6,4},{7,5},{8,10},{9,11},{10,... | collective-permute-start | bytes 1572872 | tf_op jit(solution)/shard_map/ppermute | solution.py:66
  358.1 26.4 %collective-permute-start.54 = (bf16[128,2048]{1,0:T(8,128)(2,1)}, bf16[128,2048]{1,0:T(8,128)(2,1)}, u32[]{:S(2)}, u32[]{:S(2)}) collective-permute-start(bf16[128,2048]{1,0:T(8,128)(2,1)} %get-tuple-element.425), channel_id=1, source_target_pairs={{1,0},{2,1},{3,2},{5,4},{6,5},{7,6},{9,8},{10,9},{11,10},{13,12},{... | collective-permute-start | bytes 1572872 | tf_op jit(solution)/shard_map/ppermute | solution.py:66
  359.4 25.1 %collective-permute-start.53 = (bf16[128,2048]{1,0:T(8,128)(2,1)}, bf16[128,2048]{1,0:T(8,128)(2,1)S(1)}, u32[]{:S(2)}, u32[]{:S(2)}) collective-permute-start(bf16[128,2048]{1,0:T(8,128)(2,1)} %get-tuple-element.425), channel_id=1, source_target_pairs={{0,1},{1,2},{2,3},{4,5},{5,6},{6,7},{8,9},{9,10},{10,11},{12,13},{... | collective-permute-start | bytes 1572872 | tf_op jit(solution)/shard_map/ppermute | solution.py:66
  396.0 28.0 %collective-permute-start.64 = (bf16[128,2048]{1,0:T(8,128)(2,1)S(1)}, bf16[128,2048]{1,0:T(8,128)(2,1)S(1)}, u32[]{:S(2)}, u32[]{:S(2)}) collective-permute-start(bf16[128,2048]{1,0:T(8,128)(2,1)S(1)} %slice.655), channel_id=1, source_target_pairs={{0,4},{4,0},{1,5},{5,1},{2,6},{6,2},{3,7},{7,3},{8,12},{12,8},{9,1... | collective-permute-start | bytes 1572872 | tf_op jit(solution)/shard_map/ppermute | solution.py:63
  429.6 33.0 %collective-permute-start.60 = (bf16[128,2048]{1,0:T(8,128)(2,1)S(1)}, bf16[128,2048]{1,0:T(8,128)(2,1)S(1)}, u32[]{:S(2)}, u32[]{:S(2)}) collective-permute-start(bf16[128,2048]{1,0:T(8,128)(2,1)S(1)} %get-tuple-element.409), channel_id=1, source_target_pairs={{1,0},{2,1},{3,2},{5,4},{6,5},{7,6},{9,8},{10,9},{11,10},{13,12},{... | collective-permute-start | bytes 1572872 | tf_op jit(solution)/shard_map/ppermute | solution.py:66
  430.9 31.7 %collective-permute-start.61 = (bf16[128,2048]{1,0:T(8,128)(2,1)S(1)}, bf16[128,2048]{1,0:T(8,128)(2,1)S(1)}, u32[]{:S(2)}, u32[]{:S(2)}) collective-permute-start(bf16[128,2048]{1,0:T(8,128)(2,1)S(1)} %get-tuple-element.411), channel_id=1, source_target_pairs={{0,1},{1,2},{2,3},{4,5},{5,6},{6,7},{8,9},{9,10},{10,11},{12,13},{... | collective-permute-start | bytes 1572872 | tf_op jit(solution)/shard_map/ppermute | solution.py:66
  446.6 25.9 %collective-permute-start.69 = (bf16[128,2048]{1,0:T(8,128)(2,1)S(1)}, bf16[128,2048]{1,0:T(8,128)(2,1)S(1)}, u32[]{:S(2)}, u32[]{:S(2)}) collective-permute-start(bf16[128,2048]{1,0:T(8,128)(2,1)S(1)} %add_convert_fusion.4), channel_id=1, source_target_pairs={{0,2},{1,3},{2,0},{3,1},{4,6},{5,7},{6,4},{7,5},{8,10},{9,11},{10,... | collective-permute-start | bytes 1572872 | tf_op jit(solution)/shard_map/ppermute | solution.py:66
  450.5 26.2 %collective-permute-start.66 = (bf16[2,256,1024]{2,1,0:T(8,128)(2,1)S(1)}, bf16[2,256,1024]{2,1,0:T(8,128)(2,1)S(1)}, u32[]{:S(2)}, u32[]{:S(2)}) collective-permute-start(bf16[2,256,1024]{2,1,0:T(8,128)(2,1)S(1)} %pad_maximum_fusion.15), channel_id=1, source_target_pairs={{0,8},{8,0},{16,24},{24,16},{1,9},{9,1},{17,25},{25,17},{2,10},{10... | collective-permute-start | bytes 3145736 | tf_op jit(solution)/shard_map/ppermute | solution.py:733
  452.1 26.2 %collective-permute-start.67 = (bf16[2,256,1024]{2,1,0:T(8,128)(2,1)S(1)}, bf16[2,256,1024]{2,1,0:T(8,128)(2,1)S(1)}, u32[]{:S(2)}, u32[]{:S(2)}) collective-permute-start(bf16[2,256,1024]{2,1,0:T(8,128)(2,1)S(1)} %pad_maximum_fusion.16), channel_id=1, source_target_pairs={{0,16},{8,24},{16,0},{24,8},{1,17},{9,25},{17,1},{25,9},{2,18},{10... | collective-permute-start | bytes 3145736 | tf_op jit(solution)/shard_map/ppermute | solution.py:733
  464.6 77.6 %collective-permute-start.72 = (bf16[2,4,128,1024]{3,2,0,1:T(8,128)(2,1)}, bf16[2,4,128,1024]{3,2,0,1:T(8,128)(2,1)}, u32[]{:S(2)}, u32[]{:S(2)}) collective-permute-start(bf16[2,4,128,1024]{3,2,0,1:T(8,128)(2,1)} %pad_maximum_fusion.6), channel_id=1, source_target_pairs={{0,16},{8,24},{16,0},{24,8},{1,17},{9,25},{17,1},{25,9},{2,18},{10... | collective-permute-start | bytes 6291464 | tf_op jit(solution)/shard_map/ppermute | solution.py:733
  467.8 74.4 %collective-permute-start.71 = (bf16[2,4,128,1024]{3,2,0,1:T(8,128)(2,1)}, bf16[2,4,128,1024]{3,2,0,1:T(8,128)(2,1)}, u32[]{:S(2)}, u32[]{:S(2)}) collective-permute-start(bf16[2,4,128,1024]{3,2,0,1:T(8,128)(2,1)} %pad_maximum_fusion.5), channel_id=1, source_target_pairs={{0,8},{8,0},{16,24},{24,16},{1,9},{9,1},{17,25},{25,17},{2,10},{10... | collective-permute-start | bytes 6291464 | tf_op jit(solution)/shard_map/ppermute | solution.py:733
  480.3 25.7 %collective-permute-start.70 = (bf16[128,2048]{1,0:T(8,128)(2,1)S(1)}, bf16[128,2048]{1,0:T(8,128)(2,1)}, u32[]{:S(2)}, u32[]{:S(2)}) collective-permute-start(bf16[128,2048]{1,0:T(8,128)(2,1)S(1)} %get-tuple-element.475), channel_id=1, source_target_pairs={{0,2},{1,3},{2,0},{3,1},{4,6},{5,7},{6,4},{7,5},{8,10},{9,11},{10,... | collective-permute-start | bytes 1572872 | tf_op jit(solution)/shard_map/ppermute | solution.py:66
  481.5 49.0 %collective-permute-start.74 = (bf16[1,256,1024]{2,1,0:T(8,128)(2,1)}, bf16[1,256,1024]{2,1,0:T(8,128)(2,1)S(1)}, u32[]{:S(2)}, u32[]{:S(2)}) collective-permute-start(bf16[1,256,1024]{2,1,0:T(8,128)(2,1)} %get-tuple-element.432), channel_id=1, source_target_pairs={{0,8},{8,0},{16,24},{24,16},{1,9},{9,1},{17,25},{25,17},{2,10},{10... | collective-permute-start | bytes 1572872 | tf_op jit(solution)/shard_map/ppermute | solution.py:733
  482.3 59.8 %collective-permute-start.79 = (bf16[128,2048]{1,0:T(8,128)(2,1)S(1)}, bf16[128,2048]{1,0:T(8,128)(2,1)S(1)}, u32[]{:S(2)}, u32[]{:S(2)}) collective-permute-start(bf16[128,2048]{1,0:T(8,128)(2,1)S(1)} %get-tuple-element.475), channel_id=1, source_target_pairs={{1,0},{2,1},{3,2},{5,4},{6,5},{7,6},{9,8},{10,9},{11,10},{13,12},{... | collective-permute-start | bytes 1572872 | tf_op jit(solution)/shard_map/ppermute | solution.py:66
  505.9 36.2 %collective-permute-start.78 = (bf16[128,2048]{1,0:T(8,128)(2,1)S(1)}, bf16[128,2048]{1,0:T(8,128)(2,1)S(1)}, u32[]{:S(2)}, u32[]{:S(2)}) collective-permute-start(bf16[128,2048]{1,0:T(8,128)(2,1)S(1)} %get-tuple-element.475), channel_id=1, source_target_pairs={{0,1},{1,2},{2,3},{4,5},{5,6},{6,7},{8,9},{9,10},{10,11},{12,13},{... | collective-permute-start | bytes 1572872 | tf_op jit(solution)/shard_map/ppermute | solution.py:66
  545.5 25.6 %collective-permute-start.76 = (bf16[1,4,128,1024]{3,2,0,1:T(8,128)(2,1)S(1)}, bf16[1,4,128,1024]{3,2,0,1:T(8,128)(2,1)S(1)}, u32[]{:S(2)}, u32[]{:S(2)}) collective-permute-start(bf16[1,4,128,1024]{3,2,0,1:T(8,128)(2,1)S(1)} %fusion.45), channel_id=1, source_target_pairs={{0,8},{8,0},{16,24},{24,16},{1,9},{9,1},{17,25},{25,17},{2,10},{10... | collective-permute-start | bytes 3145736 | tf_op jit(solution)/shard_map/ppermute | solution.py:733
  549.0 25.3 %collective-permute-start.75 = (bf16[1,4,128,1024]{3,2,0,1:T(8,128)(2,1)S(1)}, bf16[1,4,128,1024]{3,2,0,1:T(8,128)(2,1)S(1)}, u32[]{:S(2)}, u32[]{:S(2)}) collective-permute-start(bf16[1,4,128,1024]{3,2,0,1:T(8,128)(2,1)S(1)} %fusion.46), channel_id=1, source_target_pairs={{0,16},{8,24},{16,0},{24,8},{1,17},{9,25},{17,1},{25,9},{2,18},{10... | collective-permute-start | bytes 3145736 | tf_op jit(solution)/shard_map/ppermute | solution.py:733
  559.0 34.8 %collective-permute-start.86 = (bf16[256,512]{1,0:T(8,128)(2,1)}, bf16[256,512]{1,0:T(8,128)(2,1)S(1)}, u32[]{:S(2)}, u32[]{:S(2)}) collective-permute-start(bf16[256,512]{1,0:T(8,128)(2,1)} %get-tuple-element.484), channel_id=1, source_target_pairs={{0,1},{1,2},{2,3},{3,0},{4,5},{5,6},{6,7},{7,4},{8,9},{9,10},{10,1... | collective-permute-start | bytes 786440 | tf_op jit(solution)/shard_map/ppermute | solution.py:63
  560.1 33.6 %collective-permute-start.84 = (bf16[256,512]{1,0:T(8,128)(2,1)}, bf16[256,512]{1,0:T(8,128)(2,1)S(1)}, u32[]{:S(2)}, u32[]{:S(2)}) collective-permute-start(bf16[256,512]{1,0:T(8,128)(2,1)} %get-tuple-element.486), channel_id=1, source_target_pairs={{0,3},{1,0},{2,1},{3,2},{4,7},{5,4},{6,5},{7,6},{8,11},{9,8},{10,9... | collective-permute-start | bytes 786440 | tf_op jit(solution)/shard_map/ppermute | solution.py:63
  564.3 29.5 %collective-permute-start.85 = (bf16[256,512]{1,0:T(8,128)(2,1)S(1)}, bf16[256,512]{1,0:T(8,128)(2,1)S(1)}, u32[]{:S(2)}, u32[]{:S(2)}) collective-permute-start(bf16[256,512]{1,0:T(8,128)(2,1)S(1)} %get-tuple-element.487), channel_id=1, source_target_pairs={{0,2},{1,3},{2,0},{3,1},{4,6},{5,7},{6,4},{7,5},{8,10},{9,11},{10,... | collective-permute-start | bytes 786440 | tf_op jit(solution)/shard_map/ppermute | solution.py:63
  600.6 203.9 %all-gather.14.cloned.1.call-start = ((), (), s32[]{:S(2)}) async-start(), calls=%async_computation.3 | async-start | bytes 10485760 | tf_op jit(solution)/shard_map/all_gather | solution.py:728
  617.4 30.6 %collective-permute-start.93 = (bf16[2,128,1024]{2,1,0:T(8,128)(2,1)S(1)}, bf16[2,128,1024]{2,1,0:T(8,128)(2,1)S(1)}, u32[]{:S(2)}, u32[]{:S(2)}) collective-permute-start(bf16[2,128,1024]{2,1,0:T(8,128)(2,1)S(1)} %get-tuple-element.460), channel_id=1, source_target_pairs={{0,1},{1,2},{2,3},{3,0},{4,5},{5,6},{6,7},{7,4},{8,9},{9,10},{10,1... | collective-permute-start | bytes 1572872 | tf_op jit(solution)/shard_map/ppermute | solution.py:63
  617.5 37.6 %collective-permute-start.92 = (bf16[2,128,1024]{2,1,0:T(8,128)(2,1)S(1)}, bf16[2,128,1024]{2,1,0:T(8,128)(2,1)S(1)}, u32[]{:S(2)}, u32[]{:S(2)}) collective-permute-start(bf16[2,128,1024]{2,1,0:T(8,128)(2,1)S(1)} %get-tuple-element.461), channel_id=1, source_target_pairs={{0,2},{1,3},{2,0},{3,1},{4,6},{5,7},{6,4},{7,5},{8,10},{9,11},{10,... | collective-permute-start | bytes 1572872 | tf_op jit(solution)/shard_map/ppermute | solution.py:63
  617.9 37.2 %collective-permute-start.91 = (bf16[2,128,1024]{2,1,0:T(8,128)(2,1)S(1)}, bf16[2,128,1024]{2,1,0:T(8,128)(2,1)S(1)}, u32[]{:S(2)}, u32[]{:S(2)}) collective-permute-start(bf16[2,128,1024]{2,1,0:T(8,128)(2,1)S(1)} %get-tuple-element.462), channel_id=1, source_target_pairs={{0,3},{1,0},{2,1},{3,2},{4,7},{5,4},{6,5},{7,6},{8,11},{9,8},{10,9... | collective-permute-start | bytes 1572872 | tf_op jit(solution)/shard_map/ppermute | solution.py:63
  636.4 38.8 %collective-permute-start.97 = (bf16[2,4,128,512]{3,2,1,0:T(8,128)(2,1)S(1)}, bf16[2,4,128,512]{3,2,1,0:T(8,128)(2,1)S(1)}, u32[]{:S(2)}, u32[]{:S(2)}) collective-permute-start(bf16[2,4,128,512]{3,2,1,0:T(8,128)(2,1)S(1)} %pad_maximum_fusion.21), channel_id=1, source_target_pairs={{0,8},{8,0},{16,24},{24,16},{1,9},{9,1},{17,25},{25,17},{2,10},{10... | collective-permute-start | bytes 3145736 | tf_op jit(solution)/shard_map/ppermute | solution.py:733
  637.4 38.0 %collective-permute-start.98 = (bf16[2,4,128,512]{3,2,1,0:T(8,128)(2,1)S(1)}, bf16[2,4,128,512]{3,2,1,0:T(8,128)(2,1)}, u32[]{:S(2)}, u32[]{:S(2)}) collective-permute-start(bf16[2,4,128,512]{3,2,1,0:T(8,128)(2,1)S(1)} %pad_maximum_fusion.22), channel_id=1, source_target_pairs={{0,16},{8,24},{16,0},{24,8},{1,17},{9,25},{17,1},{25,9},{2,18},{10... | collective-permute-start | bytes 3145736 | tf_op jit(solution)/shard_map/ppermute | solution.py:733
  685.6 24.9 %collective-permute-start.105 = (bf16[1,4,128,512]{3,2,1,0:T(8,128)(2,1)S(1)}, bf16[1,4,128,512]{3,2,1,0:T(8,128)(2,1)S(1)}, u32[]{:S(2)}, u32[]{:S(2)}) collective-permute-start(bf16[1,4,128,512]{3,2,1,0:T(8,128)(2,1)S(1)} %fusion.134), channel_id=1, source_target_pairs={{0,8},{8,0},{16,24},{24,16},{1,9},{9,1},{17,25},{25,17},{2,10},{10... | collective-permute-start | bytes 1572872 | tf_op jit(solution)/shard_map/ppermute | solution.py:733
  688.9 27.9 %collective-permute-start.103 = (bf16[512,512]{1,0:T(8,128)(2,1)S(1)}, bf16[512,512]{1,0:T(8,128)(2,1)S(1)}, u32[]{:S(2)}, u32[]{:S(2)}) collective-permute-start(bf16[512,512]{1,0:T(8,128)(2,1)S(1)} %get-tuple-element.405), channel_id=1, source_target_pairs={{3,2},{0,1},{7,6},{4,5},{11,10},{8,9},{15,14},{12,13},{19,18},{16,... | collective-permute-start | bytes 1572872 | tf_op jit(solution)/shard_map/ppermute | solution.py:66
  736.6 47.8 %collective-permute-start.110 = (bf16[4,128,1024]{2,1,0:T(8,128)(2,1)S(1)}, bf16[4,128,1024]{2,1,0:T(8,128)(2,1)S(1)}, u32[]{:S(2)}, u32[]{:S(2)}) collective-permute-start(bf16[4,128,1024]{2,1,0:T(8,128)(2,1)S(1)} %pad_maximum_fusion.23.refs_0_), channel_id=1, source_target_pairs={{0,16},{8,24},{16,0},{24,8},{1,17},{9,25},{17,1},{25,9},{2,18},{10... | collective-permute-start | bytes 3145736 | tf_op jit(solution)/shard_map/ppermute | solution.py:733
  736.7 48.5 %collective-permute-start.109 = (bf16[4,128,1024]{2,1,0:T(8,128)(2,1)S(1)}, bf16[4,128,1024]{2,1,0:T(8,128)(2,1)S(1)}, u32[]{:S(2)}, u32[]{:S(2)}) collective-permute-start(bf16[4,128,1024]{2,1,0:T(8,128)(2,1)S(1)} %pad_maximum_fusion.23.refs_0_), channel_id=1, source_target_pairs={{0,8},{8,0},{16,24},{24,16},{1,9},{9,1},{17,25},{25,17},{2,10},{10... | collective-permute-start | bytes 3145736 | tf_op jit(solution)/shard_map/ppermute | solution.py:733
  755.5 36.0 %collective-permute-start.117 = (bf16[512,512]{1,0:T(8,128)(2,1)S(1)}, bf16[512,512]{1,0:T(8,128)(2,1)S(1)}, u32[]{:S(2)}, u32[]{:S(2)}) collective-permute-start(bf16[512,512]{1,0:T(8,128)(2,1)S(1)} %copy-done.79), channel_id=1, source_target_pairs={{1,0},{2,1},{3,2},{5,4},{6,5},{7,6},{9,8},{10,9},{11,10},{13,12},{... | collective-permute-start | bytes 1572872 | tf_op jit(solution)/shard_map/ppermute | solution.py:66
  762.7 28.9 %collective-permute-start.118 = (bf16[512,512]{1,0:T(8,128)(2,1)S(1)}, bf16[512,512]{1,0:T(8,128)(2,1)S(1)}, u32[]{:S(2)}, u32[]{:S(2)}) collective-permute-start(bf16[512,512]{1,0:T(8,128)(2,1)S(1)} %copy-done.78), channel_id=1, source_target_pairs={{0,1},{1,2},{2,3},{4,5},{5,6},{6,7},{8,9},{9,10},{10,11},{12,13},{... | collective-permute-start | bytes 1572872 | tf_op jit(solution)/shard_map/ppermute | solution.py:66
  765.1 32.9 %collective-permute-start.119 = (bf16[512,512]{1,0:T(8,128)(2,1)S(1)}, bf16[512,512]{1,0:T(8,128)(2,1)S(1)}, u32[]{:S(2)}, u32[]{:S(2)}) collective-permute-start(bf16[512,512]{1,0:T(8,128)(2,1)S(1)} %copy-done.81), channel_id=1, source_target_pairs={{0,2},{1,3},{2,0},{3,1},{4,6},{5,7},{6,4},{7,5},{8,10},{9,11},{10,... | collective-permute-start | bytes 1572872 | tf_op jit(solution)/shard_map/ppermute | solution.py:66
  787.8 26.9 %collective-permute-start.121 = (bf16[2,128,1024]{2,1,0:T(8,128)(2,1)}, bf16[2,128,1024]{2,1,0:T(8,128)(2,1)}, u32[]{:S(2)}, u32[]{:S(2)}) collective-permute-start(bf16[2,128,1024]{2,1,0:T(8,128)(2,1)} %slice.389), channel_id=1, source_target_pairs={{0,8},{8,0},{16,24},{24,16},{1,9},{9,1},{17,25},{25,17},{2,10},{10... | collective-permute-start | bytes 1572872 | tf_op jit(solution)/shard_map/ppermute | solution.py:733
  789.8 25.0 %collective-permute-start.120 = (bf16[2,128,1024]{2,1,0:T(8,128)(2,1)}, bf16[2,128,1024]{2,1,0:T(8,128)(2,1)}, u32[]{:S(2)}, u32[]{:S(2)}) collective-permute-start(bf16[2,128,1024]{2,1,0:T(8,128)(2,1)} %slice.388), channel_id=1, source_target_pairs={{0,16},{8,24},{16,0},{24,8},{1,17},{9,25},{17,1},{25,9},{2,18},{10... | collective-permute-start | bytes 1572872 | tf_op jit(solution)/shard_map/ppermute | solution.py:733
  (173 other events, 1916.0 us)
Sparse Core Ops, SparseCore 0:
  125.6 53.6 all-gather.7
  183.4 87.5 all-gather.9
  600.7 67.8 all-gather.11
  677.3 127.1 all-gather.13

commit v4 on v3

--- a/solution.py
+++ b/solution.py
@@ -76,21 +76,21 @@
     return lax.optimization_barrier((values, earlier))[0]
 
 
-def gather_steps(col, values, early=(), beside=()):
+def gather_steps(col, values, early=(), beside=(), late=()):
     two = col.send(values, [(0, 2), (1, 3), (2, 0), (3, 1)])
     below = col.send(values, [(0, 1), (1, 2), (2, 3)])
     above = col.send(values, [(1, 0), (2, 1), (3, 2)])
     two, early = lax.optimization_barrier((two, early))
-    beside = beside(early) if callable(beside) else beside
     two, below, above, beside = lax.optimization_barrier((two, below, above, beside))
     relayed = col.send(two, [(2, 3), (1, 0)])
-    return two, below, above, relayed, early, beside
+    relayed, late = lax.optimization_barrier((relayed, late))
+    return two, below, above, relayed, early, beside, late
 
 
 def gather_col(col, values, early, beside):
     if col.size != 4:
         return [col.fetch(values, k) for k in range(col.size)], early, beside
-    two, below, above, relayed, early, beside = gather_steps(col, values, early, beside)
+    two, below, above, relayed, early, beside, _ = gather_steps(col, values, early, beside)
     near = [
         values,
         jnp.where(col.here == 3, relayed, above),
@@ -112,11 +112,10 @@
     ]
 
 
-def gather_near(col, values, early=(), beside=()):
+def gather_near(col, values, early=(), late=()):
     if col.size != 4:
-        beside = beside(early) if callable(beside) else beside
-        return [col.fetch(values, k) for k in range(col.size)], early, beside
-    two, below, above, relayed, early, beside = gather_steps(col, values, early, beside)
+        return [col.fetch(values, k) for k in range(col.size)], early, late
+    two, below, above, relayed, early, _, late = gather_steps(col, values, early, (), late)
     inside = (col.here == 1) | (col.here == 2)
     near = [
         values,
@@ -124,7 +123,7 @@
         two,
         jnp.where(inside, below, relayed),
     ]
-    return near, early, beside
+    return near, early, late
 
 
 def reduce_near(col, blocks, between=(), beside=()):
@@ -409,13 +408,13 @@
     return [ring.fetch(block_for(ring.at(-step)), step) for step in range(ring.size)]
 
 
-def gather_tokens(row, col, values, early=(), beside=()):
-    near, early, beside = gather_near(col, values, early, beside)
+def gather_tokens(row, col, values, early=(), late=()):
+    near, early, late = gather_near(col, values, early, late)
     blocks = [
         jnp.concatenate([row.fetch(block, j) for j in range(row.size)], axis=0)
         for block in near
     ]
-    return blocks, early, beside
+    return blocks, early, late
 
 
 def sum_rows(row, partial):
@@ -847,16 +846,16 @@
         )
         squares, down_parts = lax.optimization_barrier((squares, down_parts))
         down_parts = assemble(col, down_parts, 1)
+        w_gate, w_up = after((w_gate, w_up), down_parts)
+        gate_up_parts = exchange(col, gate_up_block)
         gains = jnp.stack([gain_attn, gain_ffn])
         squares, gains = sum_all(row, col, squares, lambda index: gains)
-        squares, w_out_all, down_parts = lax.optimization_barrier(
-            (squares, w_out_all, down_parts)
+        squares, w_out_all, gate_up_parts[1::2] = lax.optimization_barrier(
+            (squares, w_out_all, gate_up_parts[1::2])
         )
         w_down_all = gather_dp(down_parts)
         gains = assemble(col, gains, 1)
         gain_attn_all, gain_ffn_all = gains[0:1], gains[1:2]
-        w_gate, w_up = after((w_gate, w_up), squares)
-        gate_up_parts = exchange(col, gate_up_block)
 
         scales = lax.rsqrt(squares / width + EPSILON)
         query_scale, key_scale = scales[0][:, None], scales[1][:, None]
@@ -864,7 +863,6 @@
         marks = jnp.stack([turned_docs, slots]).astype(F32)
         lines = jnp.concatenate([scales, marks, jnp.zeros((4, length), F32)], axis=0)
         *saved, mixture = attend_forward(row, col, raw, lines, head_gains, tables)
-        gate_up_parts[1::2], mixture = lax.optimization_barrier((gate_up_parts[1::2], mixture))
         attended = []
         for k in range(n_col):
             total, *others = (
@@ -953,19 +951,15 @@
         grad_attended, grad_gain_attn = rms_back(
             grad_state, attended, attn_scale, gain_attn_all
         )
-        attended_rows, (gate_up_sum.came, down_sum.came), _ = gather_tokens(
-            row, col, grad_attended.astype(BF), (gate_up_sum.came, down_sum.came)
+        attended_rows, gate_up_sum.came, _ = gather_tokens(
+            row, col, grad_attended.astype(BF), gate_up_sum.came
         )
         gate_up_sum.land(())
-        gate_up_sum.came, attended_rows = lax.optimization_barrier(
-            (gate_up_sum.came, attended_rows)
-        )
-        down_parts, _ = down_sum.finish(())
+        down_parts, attended_rows = down_sum.finish(attended_rows)
         down_parts = jnp.concatenate(down_parts, axis=1)
         down_parts = exchange(
             col, lambda index, whole=down_parts: block_at(whole, index, features, 1)
         )
-        gate_up_sum, _ = gate_up_sum.finish(())
 
         grad_mixture = [dot_nt(block, w_out_all).astype(BF) for block in attended_rows]
         attended_rows = jnp.concatenate(attended_rows)
@@ -978,7 +972,10 @@
             grad_gain_query,
             grad_gain_key,
         ) = attend_backward(row, col, raw, lines, head_gains, tables, saved, grad_mixture)
-        down_parts, inner = lax.optimization_barrier((down_parts, inner))
+        gate_up_sum.came, down_parts, inner = lax.optimization_barrier(
+            (gate_up_sum.came, down_parts, inner)
+        )
+        gate_up_sum, _ = gate_up_sum.finish(())
         down_back = assemble(col, [part[None] for part in down_parts], 0)
         down_all = gather_dp(down_back[None])
         small = jnp.stack([grad_gain_attn, grad_gain_ffn])

time: 840 us -> 811 us (0.965)
  waiting for transfers between devices: 396 us -> 361 us
    ppermute x22, waiting for transfers between devices: 109 us -> 85.2 us  [partner(): return lax.ppermute(values, 'dp', [(i, i ^ step) for i in range(n_dp)])]
    all_gather x1, waiting for transfers between devices: 12.2 us -> 0.01 us  [per_device(): lax.all_gather(gate_up_parts[:, :, None], 'dp', axis=2, tiled=True)]
    unnamed x199 -> x221, local copies, waits for them, and re-layouts: 20.9 us -> 24.3 us
  transfers between devices with their start and end apart: 126 -> 126, of which waited for: 56 -> 52; matrix products, arithmetic and copies ran while one was open for 21% -> 22% of each run, Pallas kernels for 7% -> 7%
where the time goes in v4:
time: 811 us; the launch traced here: 800 us
  waiting for transfers between devices  361 us (45%)
  starting transfers between devices  158 us (19%)
  matrix products  94.2 us (12%)
  Pallas kernels  64.5 us (8%)
  other arithmetic  54.9 us (7%)
  local copies, waits for them, and re-layouts  49.3 us (6%)
  between operations  17.4 us (2%)
    ppermute x32, waiting for transfers between devices, send(): return lax.ppermute(values, self.name, pairs)  186 us
    ppermute x22, waiting for transfers between devices, partner(): return lax.ppermute(values, 'dp', [(i, i ^ step) for i in range(n_dp)])  85.2 us
    ppermute x68, waiting for transfers between devices, fetch(): return lax.ppermute(values, self.name, pairs)  83.3 us
    ppermute x32, starting transfers between devices, send(): return lax.ppermute(values, self.name, pairs)  70.3 us
    ppermute x68, starting transfers between devices, fetch(): return lax.ppermute(values, self.name, pairs)  61.1 us
    dot_general x20, matrix products, dot_nt(): lax.dot_general(a, b, (((1,), (1,)), ((), ())), preferred_element_type=F32)  37.9 us
    dot_general x24, matrix products, dot(): return jnp.dot(a, b, preferred_element_type=F32)  33.9 us
    ppermute x22, starting transfers between devices, partner(): return lax.ppermute(values, 'dp', [(i, i ^ step) for i in range(n_dp)])  26.7 us
  transfers between devices with their start and end apart: 126, of which 52 were waited for; matrix products, arithmetic and copies ran while one was open for 22% of the time, Pallas kernels for 7%

profile of v4, /device:TPU:0, one launch (start us, length us, event | category | flops | bytes accessed | tf_op | source)
XLA Modules:
  0.0 799.5 jit_solution(5551191785900864187)
XLA Ops:
  17.3 10.9 %collective-permute-done.1 = bf16[128,1024]{1,0:T(8,128)(2,1)S(1)} collective-permute-done((bf16[128,1024]{1,0:T(8,128)(2,1)S(1)}, bf16[128,1024]{1,0:T(8,128)(2,1)S(1)}, u32[]{:S(2)}, u32[]{:S(2)}) %collective-permute-start.1) | collective-permute-done | bytes 262176 | tf_op jit(solution)/shard_map/ppermute | solution.py:63
  28.2 5.1 collective-permute-done.2
  33.3 7.1 collective-permute-start.3
  42.3 5.4 collective-permute-start.4
  51.5 12.8 %collective-permute-done.3.refs_2_ = bf16[512,512]{1,0:T(8,128)(2,1)} collective-permute-done((bf16[512,512]{1,0:T(8,128)(2,1)}, bf16[512,512]{1,0:T(8,128)(2,1)}, u32[]{:S(2)}, u32[]{:S(2)}) %collective-permute-start.3) | collective-permute-done | bytes 524320 | tf_op jit(solution)/shard_map/ppermute | solution.py:66
  75.8 13.7 %collective-permute-done.6 = bf16[512,512]{1,0:T(8,128)(2,1)} collective-permute-done((bf16[512,512]{1,0:T(8,128)(2,1)}, bf16[512,512]{1,0:T(8,128)(2,1)}, u32[]{:S(2)}, u32[]{:S(2)}) %collective-permute-start.6) | collective-permute-done | bytes 524320 | tf_op jit(solution)/shard_map/ppermute | solution.py:66
  106.1 8.1 %collective-permute-done.16.refs_2_ = bf16[256,512]{1,0:T(8,128)(2,1)S(1)} collective-permute-done((bf16[256,512]{1,0:T(8,128)(2,1)S(1)}, bf16[256,512]{1,0:T(8,128)(2,1)S(1)}, u32[]{:S(2)}, u32[]{:S(2)}) %collective-permute-start.16) | collective-permute-done | bytes 262176 | tf_op jit(solution)/shard_map/ppermute | solution.py:63
  129.1 19.6 %collective-permute-done.21 = f32[2,1536]{1,0:T(2,128)S(1)} collective-permute-done((f32[2,1536]{1,0:T(2,128)S(1)}, f32[2,1536]{1,0:T(2,128)S(1)}, u32[]{:S(2)}, u32[]{:S(2)}) %collective-permute-start.21) | collective-permute-done | bytes 12320 | tf_op jit(solution)/shard_map/ppermute | solution.py:63
  151.5 11.2 %attend_forward.1 = (bf16[1024,256]{1,0:T(8,128)(2,1)}, bf16[1024,256]{1,0:T(8,128)(2,1)}, bf16[1024,256]{1,0:T(8,128)(2,1)}, bf16[1024,256]{1,0:T(8,128)(2,1)}) custom-call(s32[1]{0:T(128)} %bitcast.here_ref, f32[1024,768]{1,0:T(8,128)} %copy-done.13, f32[1024,768]{1,0:T(8,128)} %copy-done.13, f32[1024,768]{1,0:T(8,128)} %copy-done.13, ...), custom_call_target="tpu_custom_call" | custom-call | flops 1073741824 | bytes 5242880 | tf_op jit(solution)/shard_map/attend_forward/pallas_call | solution.py:636
  184.3 8.8 %collective-permute-done.31 = bf16[128,2048]{1,0:T(8,128)(2,1)S(1)} collective-permute-done((bf16[128,2048]{1,0:T(8,128)(2,1)}, bf16[128,2048]{1,0:T(8,128)(2,1)S(1)}, u32[]{:S(2)}, u32[]{:S(2)}) %collective-permute-start.31) | collective-permute-done | bytes 524320 | tf_op jit(solution)/shard_map/ppermute | solution.py:66
  198.3 6.1 collective-permute-done.30
  204.4 28.6 %collective-permute-done.32 = bf16[128,2048]{1,0:T(8,128)(2,1)S(1)} collective-permute-done((bf16[128,2048]{1,0:T(8,128)(2,1)S(1)}, bf16[128,2048]{1,0:T(8,128)(2,1)S(1)}, u32[]{:S(2)}, u32[]{:S(2)}) %collective-permute-start.32) | collective-permute-done | bytes 524320 | tf_op jit(solution)/shard_map/ppermute | solution.py:66
  236.0 4.6 collective-permute-start.35
  240.7 9.9 %collective-permute-done.34 = bf16[128,2048]{1,0:T(8,128)(2,1)} collective-permute-done((bf16[128,2048]{1,0:T(8,128)(2,1)S(1)}, bf16[128,2048]{1,0:T(8,128)(2,1)}, u32[]{:S(2)}, u32[]{:S(2)}) %collective-permute-start.34) | collective-permute-done | bytes 524320 | tf_op jit(solution)/shard_map/ppermute | solution.py:66
  262.6 5.7 collective-permute-start.47
  271.2 9.0 %collective-permute-done.37 = bf16[128,2048]{1,0:T(8,128)(2,1)} collective-permute-done((bf16[128,2048]{1,0:T(8,128)(2,1)}, bf16[128,2048]{1,0:T(8,128)(2,1)}, u32[]{:S(2)}, u32[]{:S(2)}) %collective-permute-start.37) | collective-permute-done | bytes 524320 | tf_op jit(solution)/shard_map/ppermute | solution.py:66
  316.6 9.5 %collective-permute-done.50 = bf16[128,2048]{1,0:T(8,128)(2,1)S(1)} collective-permute-done((bf16[128,2048]{1,0:T(8,128)(2,1)S(1)}, bf16[128,2048]{1,0:T(8,128)(2,1)S(1)}, u32[]{:S(2)}, u32[]{:S(2)}) %collective-permute-start.50) | collective-permute-done | bytes 524320 | tf_op jit(solution)/shard_map/ppermute | solution.py:66
  326.5 8.2 %collective-permute-done.48 = bf16[128,2048]{1,0:T(8,128)(2,1)S(1)} collective-permute-done((bf16[128,2048]{1,0:T(8,128)(2,1)S(1)}, bf16[128,2048]{1,0:T(8,128)(2,1)S(1)}, u32[]{:S(2)}, u32[]{:S(2)}) %collective-permute-start.48) | collective-permute-done | bytes 524320 | tf_op jit(solution)/shard_map/ppermute | solution.py:66
  337.3 20.2 %collective-permute-done.51 = bf16[128,2048]{1,0:T(8,128)(2,1)S(1)} collective-permute-done((bf16[128,2048]{1,0:T(8,128)(2,1)S(1)}, bf16[128,2048]{1,0:T(8,128)(2,1)S(1)}, u32[]{:S(2)}, u32[]{:S(2)}) %collective-permute-start.51) | collective-permute-done | bytes 524320 | tf_op jit(solution)/shard_map/ppermute | solution.py:66
  361.5 4.6 collective-permute-start.53
  370.2 6.0 collective-permute-done.52
  376.2 9.8 %collective-permute-done.54 = bf16[128,2048]{1,0:T(8,128)(2,1)} collective-permute-done((bf16[128,2048]{1,0:T(8,128)(2,1)}, bf16[128,2048]{1,0:T(8,128)(2,1)}, u32[]{:S(2)}, u32[]{:S(2)}) %collective-permute-start.54) | collective-permute-done | bytes 524320 | tf_op jit(solution)/shard_map/ppermute | solution.py:66
  387.4 4.4 multiply_convert_fusion.2
  412.5 4.2 multiply_convert_fusion.4
  427.1 4.6 collective-permute-start.61
  431.7 5.9 collective-permute-done.68
  437.8 4.9 convolution_convert_fusion.2
  449.5 4.9 convolution_convert_fusion
  454.4 4.9 convolution_convert_fusion.1
  477.5 4.8 collective-permute-start.78
  482.3 14.7 %collective-permute-done.70 = bf16[128,2048]{1,0:T(8,128)(2,1)S(1)} collective-permute-done((bf16[128,2048]{1,0:T(8,128)(2,1)S(1)}, bf16[128,2048]{1,0:T(8,128)(2,1)S(1)}, u32[]{:S(2)}, u32[]{:S(2)}) %collective-permute-start.70) | collective-permute-done | bytes 524320 | tf_op jit(solution)/shard_map/ppermute | solution.py:66
  499.2 17.3 %collective-permute-done.72 = bf16[2,4,128,1024]{3,2,0,1:T(8,128)(2,1)} collective-permute-done((bf16[2,4,128,1024]{3,2,0,1:T(8,128)(2,1)}, bf16[2,4,128,1024]{3,2,0,1:T(8,128)(2,1)}, u32[]{:S(2)}, u32[]{:S(2)}) %collective-permute-start.72) | collective-permute-done | bytes 2097184 | tf_op jit(solution)/shard_map/ppermute | solution.py:732
  523.1 8.1 %collective-permute-done.82 = bf16[128,2048]{1,0:T(8,128)(2,1)S(1)} collective-permute-done((bf16[128,2048]{1,0:T(8,128)(2,1)S(1)}, bf16[128,2048]{1,0:T(8,128)(2,1)S(1)}, u32[]{:S(2)}, u32[]{:S(2)}) %collective-permute-start.82) | collective-permute-done | bytes 524320 | tf_op jit(solution)/shard_map/ppermute | solution.py:66
  549.4 14.4 %attend_backward.1 = (f32[1024,256]{1,0:T(8,128)}, f32[1024,256]{1,0:T(8,128)}, bf16[1024,256]{1,0:T(8,128)(2,1)}, f32[8,1024]{1,0:T(8,128)}, f32[2,1,128]{2,1,0:T(1,128)}, /*index=5*/f32[2,1,128]{2,1,0:T(1,128)}) custom-call(s32[1]{0:T(128)} %bitcast.here_ref, f32[1024,768]{1,0:T(8,128)} %copy-done.13, f32[1024,768]{1,0:T(8,128)} %copy-done.13, ...), custom_call_target="tpu_custom_call" | custom-call | flops 2684354560 | bytes 7864320 | tf_op jit(solution)/shard_map/attend_backward/pallas_call | solution.py:668
  617.6 7.0 collective-permute-done.92
  624.6 21.5 %collective-permute-done.97 = bf16[2,4,128,512]{3,2,1,0:T(8,128)(2,1)S(1)} collective-permute-done((bf16[2,4,128,512]{3,2,1,0:T(8,128)(2,1)S(1)}, bf16[2,4,128,512]{3,2,1,0:T(8,128)(2,1)S(1)}, u32[]{:S(2)}, u32[]{:S(2)}) %collective-permute-start.97) | collective-permute-done | bytes 1048608 | tf_op jit(solution)/shard_map/ppermute | solution.py:732
  663.2 12.5 %collective-permute-done.104 = bf16[1,4,128,512]{3,2,1,0:T(8,128)(2,1)S(1)} collective-permute-done((bf16[1,4,128,512]{3,2,1,0:T(8,128)(2,1)S(1)}, bf16[1,4,128,512]{3,2,1,0:T(8,128)(2,1)S(1)}, u32[]{:S(2)}, u32[]{:S(2)}) %collective-permute-start.104) | collective-permute-done | bytes 524320 | tf_op jit(solution)/shard_map/ppermute | solution.py:732
  675.7 5.7 collective-permute-done.105
  688.7 10.9 %down_gradients.1 = f32[4,4,256,512]{3,2,1,0:T(8,128)} custom-call(bf16[4,4,256,512]{3,2,1,0:T(8,128)(2,1)} %bitcast.350), custom_call_target="tpu_custom_call" | custom-call | bytes 12582912 | tf_op jit(solution)/shard_map/down_gradients/pallas_call | solution.py:288
  699.6 7.5 collective-permute-done.107
  714.0 4.3 collective-permute-done.113.refs_3_
  718.4 4.7 collective-permute-done.112.refs_2_
  727.3 5.6 collective-permute-done.115.refs_2_
  738.7 16.2 %collective-permute-done.110.refs_2_ = bf16[4,128,1024]{2,1,0:T(8,128)(2,1)S(1)} collective-permute-done((bf16[4,128,1024]{2,1,0:T(8,128)(2,1)S(1)}, bf16[4,128,1024]{2,1,0:T(8,128)(2,1)S(1)}, u32[]{:S(2)}, u32[]{:S(2)}) %collective-permute-start.110) | collective-permute-done | bytes 1048608 | tf_op jit(solution)/shard_map/ppermute | solution.py:732
  763.8 4.7 collective-permute-done.119
  769.8 6.1 all-gather.14.cloned.1.call-done
  775.8 10.2 %pair_gradients.1 = (f32[512,4096]{1,0:T(8,128)}, f32[512,4096]{1,0:T(8,128)}) custom-call(bf16[4,4,2,128,1024]{4,3,2,1,0:T(8,128)(2,1)} %bitcast.349), custom_call_target="tpu_custom_call" | custom-call | bytes 25165824 | tf_op jit(solution)/shard_map/pair_gradients/pallas_call | solution.py:265
  786.1 6.5 last_gradients.1
  (672 shorter events, 340.7 us)
Async XLA Ops:
  7.2 167.4 %all-gather.8.cloned.1.call-start = ((), (), s32[]{:S(2)}) async-start(), calls=%async_computation | async-start | bytes 5242880 | tf_op jit(solution)/shard_map/all_gather | solution.py:727
  33.3 31.1 %collective-permute-start.3 = (bf16[512,512]{1,0:T(8,128)(2,1)}, bf16[512,512]{1,0:T(8,128)(2,1)}, u32[]{:S(2)}, u32[]{:S(2)}) collective-permute-start(bf16[512,512]{1,0:T(8,128)(2,1)} %refs_0_), channel_id=1, source_target_pairs={{0,2},{1,3},{2,0},{3,1},{4,6},{5,7},{6,4},{7,5},{8,10},{9,11},{10,... | collective-permute-start | bytes 1572872 | tf_op jit(solution)/shard_map/ppermute | solution.py:66
  41.0 26.8 %collective-permute-start.5 = (bf16[512,512]{1,0:T(8,128)(2,1)}, bf16[512,512]{1,0:T(8,128)(2,1)}, u32[]{:S(2)}, u32[]{:S(2)}) collective-permute-start(bf16[512,512]{1,0:T(8,128)(2,1)} %refs_0_), channel_id=1, source_target_pairs={{1,0},{2,1},{3,2},{5,4},{6,5},{7,6},{9,8},{10,9},{11,10},{13,12},{... | collective-permute-start | bytes 1572872 | tf_op jit(solution)/shard_map/ppermute | solution.py:66
  42.3 25.5 %collective-permute-start.4 = (bf16[512,512]{1,0:T(8,128)(2,1)}, bf16[512,512]{1,0:T(8,128)(2,1)}, u32[]{:S(2)}, u32[]{:S(2)}) collective-permute-start(bf16[512,512]{1,0:T(8,128)(2,1)} %refs_0_), channel_id=1, source_target_pairs={{0,1},{1,2},{2,3},{4,5},{5,6},{6,7},{8,9},{9,10},{10,11},{12,13},{... | collective-permute-start | bytes 1572872 | tf_op jit(solution)/shard_map/ppermute | solution.py:66
  47.8 24.7 %collective-permute-start.9 = (bf16[4,128,1024]{2,1,0:T(8,128)(2,1)S(1)}, bf16[4,128,1024]{2,1,0:T(8,128)(2,1)S(1)}, u32[]{:S(2)}, u32[]{:S(2)}) collective-permute-start(bf16[4,128,1024]{2,1,0:T(8,128)(2,1)S(1)} %pad_maximum_fusion.9.refs_0_), channel_id=1, source_target_pairs={{0,16},{8,24},{16,0},{24,8},{1,17},{9,25},{17,1},{25,9},{2,18},{10... | collective-permute-start | bytes 3145736 | tf_op jit(solution)/shard_map/ppermute | solution.py:732
  49.4 24.0 %collective-permute-start.8 = (bf16[4,128,1024]{2,1,0:T(8,128)(2,1)S(1)}, bf16[4,128,1024]{2,1,0:T(8,128)(2,1)S(1)}, u32[]{:S(2)}, u32[]{:S(2)}) collective-permute-start(bf16[4,128,1024]{2,1,0:T(8,128)(2,1)S(1)} %pad_maximum_fusion.9.refs_0_), channel_id=1, source_target_pairs={{0,8},{8,0},{16,24},{24,16},{1,9},{9,1},{17,25},{25,17},{2,10},{10... | collective-permute-start | bytes 3145736 | tf_op jit(solution)/shard_map/ppermute | solution.py:732
  115.8 164.5 %all-gather.10.cloned.1.call-start = ((), (), s32[]{:S(2)}) async-start(), calls=%async_computation.1 | async-start | bytes 10485760 | tf_op jit(solution)/shard_map/all_gather | solution.py:881
  118.7 31.3 %collective-permute-start.22 = (bf16[2,128,1024]{2,1,0:T(8,128)(2,1)S(1)}, bf16[2,128,1024]{2,1,0:T(8,128)(2,1)S(1)}, u32[]{:S(2)}, u32[]{:S(2)}) collective-permute-start(bf16[2,128,1024]{2,1,0:T(8,128)(2,1)S(1)} %pad_maximum_fusion.33), channel_id=1, source_target_pairs={{0,3},{1,0},{2,1},{3,2},{4,7},{5,4},{6,5},{7,6},{8,11},{9,8},{10,9... | collective-permute-start | bytes 1572872 | tf_op jit(solution)/shard_map/ppermute | solution.py:63
  122.8 27.2 %collective-permute-start.23 = (bf16[2,128,1024]{2,1,0:T(8,128)(2,1)S(1)}, bf16[2,128,1024]{2,1,0:T(8,128)(2,1)S(1)}, u32[]{:S(2)}, u32[]{:S(2)}) collective-permute-start(bf16[2,128,1024]{2,1,0:T(8,128)(2,1)S(1)} %pad_maximum_fusion.34), channel_id=1, source_target_pairs={{0,1},{1,2},{2,3},{3,0},{4,5},{5,6},{6,7},{7,4},{8,9},{9,10},{10,1... | collective-permute-start | bytes 1572872 | tf_op jit(solution)/shard_map/ppermute | solution.py:63
  124.3 24.3 %collective-permute-start.21 = (f32[2,1536]{1,0:T(2,128)S(1)}, f32[2,1536]{1,0:T(2,128)S(1)}, u32[]{:S(2)}, u32[]{:S(2)}) collective-permute-start(f32[2,1536]{1,0:T(2,128)S(1)} %maximum_maximum_fusion.1), channel_id=1, source_target_pairs={{0,1},{1,2},{2,3},{3,0},{4,5},{5,6},{6,7},{7,4},{8,9},{9,10},{10,1... | collective-permute-start | bytes 36872 | tf_op jit(solution)/shard_map/ppermute | solution.py:63
  148.6 25.2 %collective-permute-start.24 = (bf16[2,128,1024]{2,1,0:T(8,128)(2,1)S(1)}, bf16[2,128,1024]{2,1,0:T(8,128)(2,1)S(1)}, u32[]{:S(2)}, u32[]{:S(2)}) collective-permute-start(bf16[2,128,1024]{2,1,0:T(8,128)(2,1)S(1)} %pad_maximum_fusion.35), channel_id=1, source_target_pairs={{0,2},{1,3},{2,0},{3,1},{4,6},{5,7},{6,4},{7,5},{8,10},{9,11},{10,... | collective-permute-start | bytes 1572872 | tf_op jit(solution)/shard_map/ppermute | solution.py:63
  178.6 510.1 %all-gather.12.cloned.1.call-start = ((), (), s32[]{:S(2)}) async-start(), calls=%async_computation.2 | async-start | bytes 5242880 | tf_op jit(solution)/shard_map/all_gather | solution.py:727
  180.5 23.8 %collective-permute-start.30 = (bf16[128,2048]{1,0:T(8,128)(2,1)}, bf16[128,2048]{1,0:T(8,128)(2,1)S(1)}, u32[]{:S(2)}, u32[]{:S(2)}) collective-permute-start(bf16[128,2048]{1,0:T(8,128)(2,1)} %convolution_add_fusion.2), channel_id=1, source_target_pairs={{0,1},{1,2},{2,3},{4,5},{5,6},{6,7},{8,9},{9,10},{10,11},{12,13},{... | collective-permute-start | bytes 1572872 | tf_op jit(solution)/shard_map/ppermute | solution.py:66
  193.3 39.7 %collective-permute-start.32 = (bf16[128,2048]{1,0:T(8,128)(2,1)S(1)}, bf16[128,2048]{1,0:T(8,128)(2,1)S(1)}, u32[]{:S(2)}, u32[]{:S(2)}) collective-permute-start(bf16[128,2048]{1,0:T(8,128)(2,1)S(1)} %add_convert_fusion.6), channel_id=1, source_target_pairs={{0,2},{1,3},{2,0},{3,1},{4,6},{5,7},{6,4},{7,5},{8,10},{9,11},{10,... | collective-permute-start | bytes 1572872 | tf_op jit(solution)/shard_map/ppermute | solution.py:66
  254.5 25.7 %collective-permute-start.37 = (bf16[128,2048]{1,0:T(8,128)(2,1)}, bf16[128,2048]{1,0:T(8,128)(2,1)}, u32[]{:S(2)}, u32[]{:S(2)}) collective-permute-start(bf16[128,2048]{1,0:T(8,128)(2,1)} %collective-permute-done.34), channel_id=1, source_target_pairs={{2,3},{1,0},{6,7},{5,4},{10,11},{9,8},{14,15},{13,12},{18,19},{17,... | collective-permute-start | bytes 1572872 | tf_op jit(solution)/shard_map/ppermute | solution.py:66
  262.6 49.9 %collective-permute-start.47 = (bf16[128,512]{1,0:T(8,128)(2,1)S(1)}, bf16[128,512]{1,0:T(8,128)(2,1)S(1)}, u32[]{:S(2)}, u32[]{:S(2)}) collective-permute-start(bf16[128,512]{1,0:T(8,128)(2,1)S(1)} %get-tuple-element.512), channel_id=1, source_target_pairs={{0,1},{1,2},{2,3},{3,0},{4,5},{5,6},{6,7},{7,4},{8,9},{9,10},{10,1... | collective-permute-start | bytes 393224 | tf_op jit(solution)/shard_map/ppermute | solution.py:63
  268.3 44.2 %collective-permute-start.46 = (bf16[128,512]{1,0:T(8,128)(2,1)S(1)}, bf16[128,512]{1,0:T(8,128)(2,1)S(1)}, u32[]{:S(2)}, u32[]{:S(2)}) collective-permute-start(bf16[128,512]{1,0:T(8,128)(2,1)S(1)} %get-tuple-element.513), channel_id=1, source_target_pairs={{0,2},{1,3},{2,0},{3,1},{4,6},{5,7},{6,4},{7,5},{8,10},{9,11},{10,... | collective-permute-start | bytes 393224 | tf_op jit(solution)/shard_map/ppermute | solution.py:63
  268.3 44.2 %collective-permute-start.45 = (bf16[128,512]{1,0:T(8,128)(2,1)S(1)}, bf16[128,512]{1,0:T(8,128)(2,1)S(1)}, u32[]{:S(2)}, u32[]{:S(2)}) collective-permute-start(bf16[128,512]{1,0:T(8,128)(2,1)S(1)} %get-tuple-element.514), channel_id=1, source_target_pairs={{0,3},{1,0},{2,1},{3,2},{4,7},{5,4},{6,5},{7,6},{8,11},{9,8},{10,9... | collective-permute-start | bytes 393224 | tf_op jit(solution)/shard_map/ppermute | solution.py:63
  326.2 31.3 %collective-permute-start.51 = (bf16[128,2048]{1,0:T(8,128)(2,1)S(1)}, bf16[128,2048]{1,0:T(8,128)(2,1)S(1)}, u32[]{:S(2)}, u32[]{:S(2)}) collective-permute-start(bf16[128,2048]{1,0:T(8,128)(2,1)S(1)} %add_convert_fusion.5), channel_id=1, source_target_pairs={{0,2},{1,3},{2,0},{3,1},{4,6},{5,7},{6,4},{7,5},{8,10},{9,11},{10,... | collective-permute-start | bytes 1572872 | tf_op jit(solution)/shard_map/ppermute | solution.py:66
  360.2 25.9 %collective-permute-start.54 = (bf16[128,2048]{1,0:T(8,128)(2,1)}, bf16[128,2048]{1,0:T(8,128)(2,1)}, u32[]{:S(2)}, u32[]{:S(2)}) collective-permute-start(bf16[128,2048]{1,0:T(8,128)(2,1)} %get-tuple-element.419), channel_id=1, source_target_pairs={{1,0},{2,1},{3,2},{5,4},{6,5},{7,6},{9,8},{10,9},{11,10},{13,12},{... | collective-permute-start | bytes 1572872 | tf_op jit(solution)/shard_map/ppermute | solution.py:66
  361.5 24.6 %collective-permute-start.53 = (bf16[128,2048]{1,0:T(8,128)(2,1)}, bf16[128,2048]{1,0:T(8,128)(2,1)S(1)}, u32[]{:S(2)}, u32[]{:S(2)}) collective-permute-start(bf16[128,2048]{1,0:T(8,128)(2,1)} %get-tuple-element.419), channel_id=1, source_target_pairs={{0,1},{1,2},{2,3},{4,5},{5,6},{6,7},{8,9},{9,10},{10,11},{12,13},{... | collective-permute-start | bytes 1572872 | tf_op jit(solution)/shard_map/ppermute | solution.py:66
  397.3 24.1 %collective-permute-start.64 = (bf16[128,2048]{1,0:T(8,128)(2,1)S(1)}, bf16[128,2048]{1,0:T(8,128)(2,1)S(1)}, u32[]{:S(2)}, u32[]{:S(2)}) collective-permute-start(bf16[128,2048]{1,0:T(8,128)(2,1)S(1)} %slice.655), channel_id=1, source_target_pairs={{0,4},{4,0},{1,5},{5,1},{2,6},{6,2},{3,7},{7,3},{8,12},{12,8},{9,1... | collective-permute-start | bytes 1572872 | tf_op jit(solution)/shard_map/ppermute | solution.py:63
  425.8 33.6 %collective-permute-start.60 = (bf16[128,2048]{1,0:T(8,128)(2,1)S(1)}, bf16[128,2048]{1,0:T(8,128)(2,1)S(1)}, u32[]{:S(2)}, u32[]{:S(2)}) collective-permute-start(bf16[128,2048]{1,0:T(8,128)(2,1)S(1)} %get-tuple-element.403), channel_id=1, source_target_pairs={{1,0},{2,1},{3,2},{5,4},{6,5},{7,6},{9,8},{10,9},{11,10},{13,12},{... | collective-permute-start | bytes 1572872 | tf_op jit(solution)/shard_map/ppermute | solution.py:66
  427.1 32.3 %collective-permute-start.61 = (bf16[128,2048]{1,0:T(8,128)(2,1)S(1)}, bf16[128,2048]{1,0:T(8,128)(2,1)S(1)}, u32[]{:S(2)}, u32[]{:S(2)}) collective-permute-start(bf16[128,2048]{1,0:T(8,128)(2,1)S(1)} %get-tuple-element.405), channel_id=1, source_target_pairs={{0,1},{1,2},{2,3},{4,5},{5,6},{6,7},{8,9},{9,10},{10,11},{12,13},{... | collective-permute-start | bytes 1572872 | tf_op jit(solution)/shard_map/ppermute | solution.py:66
  442.7 25.5 %collective-permute-start.69 = (bf16[128,2048]{1,0:T(8,128)(2,1)S(1)}, bf16[128,2048]{1,0:T(8,128)(2,1)S(1)}, u32[]{:S(2)}, u32[]{:S(2)}) collective-permute-start(bf16[128,2048]{1,0:T(8,128)(2,1)S(1)} %add_convert_fusion.4), channel_id=1, source_target_pairs={{0,2},{1,3},{2,0},{3,1},{4,6},{5,7},{6,4},{7,5},{8,10},{9,11},{10,... | collective-permute-start | bytes 1572872 | tf_op jit(solution)/shard_map/ppermute | solution.py:66
  446.2 26.2 %collective-permute-start.66 = (bf16[2,256,1024]{2,1,0:T(8,128)(2,1)S(1)}, bf16[2,256,1024]{2,1,0:T(8,128)(2,1)S(1)}, u32[]{:S(2)}, u32[]{:S(2)}) collective-permute-start(bf16[2,256,1024]{2,1,0:T(8,128)(2,1)S(1)} %pad_maximum_fusion.15), channel_id=1, source_target_pairs={{0,8},{8,0},{16,24},{24,16},{1,9},{9,1},{17,25},{25,17},{2,10},{10... | collective-permute-start | bytes 3145736 | tf_op jit(solution)/shard_map/ppermute | solution.py:732
  447.9 26.2 %collective-permute-start.67 = (bf16[2,256,1024]{2,1,0:T(8,128)(2,1)S(1)}, bf16[2,256,1024]{2,1,0:T(8,128)(2,1)S(1)}, u32[]{:S(2)}, u32[]{:S(2)}) collective-permute-start(bf16[2,256,1024]{2,1,0:T(8,128)(2,1)S(1)} %pad_maximum_fusion.16), channel_id=1, source_target_pairs={{0,16},{8,24},{16,0},{24,8},{1,17},{9,25},{17,1},{25,9},{2,18},{10... | collective-permute-start | bytes 3145736 | tf_op jit(solution)/shard_map/ppermute | solution.py:732
  461.3 55.2 %collective-permute-start.72 = (bf16[2,4,128,1024]{3,2,0,1:T(8,128)(2,1)}, bf16[2,4,128,1024]{3,2,0,1:T(8,128)(2,1)}, u32[]{:S(2)}, u32[]{:S(2)}) collective-permute-start(bf16[2,4,128,1024]{3,2,0,1:T(8,128)(2,1)} %pad_maximum_fusion.6), channel_id=1, source_target_pairs={{0,16},{8,24},{16,0},{24,8},{1,17},{9,25},{17,1},{25,9},{2,18},{10... | collective-permute-start | bytes 6291464 | tf_op jit(solution)/shard_map/ppermute | solution.py:732
  463.7 53.3 %collective-permute-start.71 = (bf16[2,4,128,1024]{3,2,0,1:T(8,128)(2,1)}, bf16[2,4,128,1024]{3,2,0,1:T(8,128)(2,1)}, u32[]{:S(2)}, u32[]{:S(2)}) collective-permute-start(bf16[2,4,128,1024]{3,2,0,1:T(8,128)(2,1)} %pad_maximum_fusion.5), channel_id=1, source_target_pairs={{0,8},{8,0},{16,24},{24,16},{1,9},{9,1},{17,25},{25,17},{2,10},{10... | collective-permute-start | bytes 6291464 | tf_op jit(solution)/shard_map/ppermute | solution.py:732
  476.2 42.3 %collective-permute-start.79 = (bf16[128,2048]{1,0:T(8,128)(2,1)S(1)}, bf16[128,2048]{1,0:T(8,128)(2,1)S(1)}, u32[]{:S(2)}, u32[]{:S(2)}) collective-permute-start(bf16[128,2048]{1,0:T(8,128)(2,1)S(1)} %get-tuple-element.469), channel_id=1, source_target_pairs={{1,0},{2,1},{3,2},{5,4},{6,5},{7,6},{9,8},{10,9},{11,10},{13,12},{... | collective-permute-start | bytes 1572872 | tf_op jit(solution)/shard_map/ppermute | solution.py:66
  477.5 41.0 %collective-permute-start.78 = (bf16[128,2048]{1,0:T(8,128)(2,1)S(1)}, bf16[128,2048]{1,0:T(8,128)(2,1)S(1)}, u32[]{:S(2)}, u32[]{:S(2)}) collective-permute-start(bf16[128,2048]{1,0:T(8,128)(2,1)S(1)} %get-tuple-element.469), channel_id=1, source_target_pairs={{0,1},{1,2},{2,3},{4,5},{5,6},{6,7},{8,9},{9,10},{10,11},{12,13},{... | collective-permute-start | bytes 1572872 | tf_op jit(solution)/shard_map/ppermute | solution.py:66
  534.9 28.9 %collective-permute-start.74 = (bf16[1,4,128,1024]{3,2,0,1:T(8,128)(2,1)}, bf16[1,4,128,1024]{3,2,0,1:T(8,128)(2,1)S(1)}, u32[]{:S(2)}, u32[]{:S(2)}) collective-permute-start(bf16[1,4,128,1024]{3,2,0,1:T(8,128)(2,1)} %fusion.45), channel_id=1, source_target_pairs={{0,8},{8,0},{16,24},{24,16},{1,9},{9,1},{17,25},{25,17},{2,10},{10... | collective-permute-start | bytes 3145736 | tf_op jit(solution)/shard_map/ppermute | solution.py:732
  536.5 27.4 %collective-permute-start.73 = (bf16[1,4,128,1024]{3,2,0,1:T(8,128)(2,1)}, bf16[1,4,128,1024]{3,2,0,1:T(8,128)(2,1)}, u32[]{:S(2)}, u32[]{:S(2)}) collective-permute-start(bf16[1,4,128,1024]{3,2,0,1:T(8,128)(2,1)} %fusion.46), channel_id=1, source_target_pairs={{0,16},{8,24},{16,0},{24,8},{1,17},{9,25},{17,1},{25,9},{2,18},{10... | collective-permute-start | bytes 3145736 | tf_op jit(solution)/shard_map/ppermute | solution.py:732
  573.6 202.2 %all-gather.14.cloned.1.call-start = ((), (), s32[]{:S(2)}) async-start(), calls=%async_computation.3 | async-start | bytes 10485760 | tf_op jit(solution)/shard_map/all_gather | solution.py:727
  586.9 30.7 %collective-permute-start.93 = (bf16[2,128,1024]{2,1,0:T(8,128)(2,1)S(1)}, bf16[2,128,1024]{2,1,0:T(8,128)(2,1)S(1)}, u32[]{:S(2)}, u32[]{:S(2)}) collective-permute-start(bf16[2,128,1024]{2,1,0:T(8,128)(2,1)S(1)} %get-tuple-element.454), channel_id=1, source_target_pairs={{0,1},{1,2},{2,3},{3,0},{4,5},{5,6},{6,7},{7,4},{8,9},{9,10},{10,1... | collective-permute-start | bytes 1572872 | tf_op jit(solution)/shard_map/ppermute | solution.py:63
  587.4 37.1 %collective-permute-start.92 = (bf16[2,128,1024]{2,1,0:T(8,128)(2,1)S(1)}, bf16[2,128,1024]{2,1,0:T(8,128)(2,1)S(1)}, u32[]{:S(2)}, u32[]{:S(2)}) collective-permute-start(bf16[2,128,1024]{2,1,0:T(8,128)(2,1)S(1)} %get-tuple-element.455), channel_id=1, source_target_pairs={{0,2},{1,3},{2,0},{3,1},{4,6},{5,7},{6,4},{7,5},{8,10},{9,11},{10,... | collective-permute-start | bytes 1572872 | tf_op jit(solution)/shard_map/ppermute | solution.py:63
  589.4 35.1 %collective-permute-start.91 = (bf16[2,128,1024]{2,1,0:T(8,128)(2,1)S(1)}, bf16[2,128,1024]{2,1,0:T(8,128)(2,1)S(1)}, u32[]{:S(2)}, u32[]{:S(2)}) collective-permute-start(bf16[2,128,1024]{2,1,0:T(8,128)(2,1)S(1)} %get-tuple-element.456), channel_id=1, source_target_pairs={{0,3},{1,0},{2,1},{3,2},{4,7},{5,4},{6,5},{7,6},{8,11},{9,8},{10,9... | collective-permute-start | bytes 1572872 | tf_op jit(solution)/shard_map/ppermute | solution.py:63
  605.9 40.1 %collective-permute-start.97 = (bf16[2,4,128,512]{3,2,1,0:T(8,128)(2,1)S(1)}, bf16[2,4,128,512]{3,2,1,0:T(8,128)(2,1)S(1)}, u32[]{:S(2)}, u32[]{:S(2)}) collective-permute-start(bf16[2,4,128,512]{3,2,1,0:T(8,128)(2,1)S(1)} %pad_maximum_fusion.21), channel_id=1, source_target_pairs={{0,8},{8,0},{16,24},{24,16},{1,9},{9,1},{17,25},{25,17},{2,10},{10... | collective-permute-start | bytes 3145736 | tf_op jit(solution)/shard_map/ppermute | solution.py:732
  606.7 39.6 %collective-permute-start.98 = (bf16[2,4,128,512]{3,2,1,0:T(8,128)(2,1)S(1)}, bf16[2,4,128,512]{3,2,1,0:T(8,128)(2,1)}, u32[]{:S(2)}, u32[]{:S(2)}) collective-permute-start(bf16[2,4,128,512]{3,2,1,0:T(8,128)(2,1)S(1)} %pad_maximum_fusion.22), channel_id=1, source_target_pairs={{0,16},{8,24},{16,0},{24,8},{1,17},{9,25},{17,1},{25,9},{2,18},{10... | collective-permute-start | bytes 3145736 | tf_op jit(solution)/shard_map/ppermute | solution.py:732
  656.5 24.9 %collective-permute-start.105 = (bf16[1,4,128,512]{3,2,1,0:T(8,128)(2,1)S(1)}, bf16[1,4,128,512]{3,2,1,0:T(8,128)(2,1)S(1)}, u32[]{:S(2)}, u32[]{:S(2)}) collective-permute-start(bf16[1,4,128,512]{3,2,1,0:T(8,128)(2,1)S(1)} %fusion.134), channel_id=1, source_target_pairs={{0,8},{8,0},{16,24},{24,16},{1,9},{9,1},{17,25},{25,17},{2,10},{10... | collective-permute-start | bytes 1572872 | tf_op jit(solution)/shard_map/ppermute | solution.py:732
  659.7 28.0 %collective-permute-start.103 = (bf16[512,512]{1,0:T(8,128)(2,1)S(1)}, bf16[512,512]{1,0:T(8,128)(2,1)S(1)}, u32[]{:S(2)}, u32[]{:S(2)}) collective-permute-start(bf16[512,512]{1,0:T(8,128)(2,1)S(1)} %get-tuple-element.399), channel_id=1, source_target_pairs={{3,2},{0,1},{7,6},{4,5},{11,10},{8,9},{15,14},{12,13},{19,18},{16,... | collective-permute-start | bytes 1572872 | tf_op jit(solution)/shard_map/ppermute | solution.py:66
  707.2 47.7 %collective-permute-start.110 = (bf16[4,128,1024]{2,1,0:T(8,128)(2,1)S(1)}, bf16[4,128,1024]{2,1,0:T(8,128)(2,1)S(1)}, u32[]{:S(2)}, u32[]{:S(2)}) collective-permute-start(bf16[4,128,1024]{2,1,0:T(8,128)(2,1)S(1)} %pad_maximum_fusion.23.refs_0_), channel_id=1, source_target_pairs={{0,16},{8,24},{16,0},{24,8},{1,17},{9,25},{17,1},{25,9},{2,18},{10... | collective-permute-start | bytes 3145736 | tf_op jit(solution)/shard_map/ppermute | solution.py:732
  707.4 48.4 %collective-permute-start.109 = (bf16[4,128,1024]{2,1,0:T(8,128)(2,1)S(1)}, bf16[4,128,1024]{2,1,0:T(8,128)(2,1)S(1)}, u32[]{:S(2)}, u32[]{:S(2)}) collective-permute-start(bf16[4,128,1024]{2,1,0:T(8,128)(2,1)S(1)} %pad_maximum_fusion.23.refs_0_), channel_id=1, source_target_pairs={{0,8},{8,0},{16,24},{24,16},{1,9},{9,1},{17,25},{25,17},{2,10},{10... | collective-permute-start | bytes 3145736 | tf_op jit(solution)/shard_map/ppermute | solution.py:732
  726.0 36.1 %collective-permute-start.117 = (bf16[512,512]{1,0:T(8,128)(2,1)S(1)}, bf16[512,512]{1,0:T(8,128)(2,1)S(1)}, u32[]{:S(2)}, u32[]{:S(2)}) collective-permute-start(bf16[512,512]{1,0:T(8,128)(2,1)S(1)} %copy-done.79), channel_id=1, source_target_pairs={{1,0},{2,1},{3,2},{5,4},{6,5},{7,6},{9,8},{10,9},{11,10},{13,12},{... | collective-permute-start | bytes 1572872 | tf_op jit(solution)/shard_map/ppermute | solution.py:66
  732.9 29.3 %collective-permute-start.118 = (bf16[512,512]{1,0:T(8,128)(2,1)S(1)}, bf16[512,512]{1,0:T(8,128)(2,1)S(1)}, u32[]{:S(2)}, u32[]{:S(2)}) collective-permute-start(bf16[512,512]{1,0:T(8,128)(2,1)S(1)} %copy-done.78), channel_id=1, source_target_pairs={{0,1},{1,2},{2,3},{4,5},{5,6},{6,7},{8,9},{9,10},{10,11},{12,13},{... | collective-permute-start | bytes 1572872 | tf_op jit(solution)/shard_map/ppermute | solution.py:66
  735.4 33.0 %collective-permute-start.119 = (bf16[512,512]{1,0:T(8,128)(2,1)S(1)}, bf16[512,512]{1,0:T(8,128)(2,1)S(1)}, u32[]{:S(2)}, u32[]{:S(2)}) collective-permute-start(bf16[512,512]{1,0:T(8,128)(2,1)S(1)} %copy-done.83), channel_id=1, source_target_pairs={{0,2},{1,3},{2,0},{3,1},{4,6},{5,7},{6,4},{7,5},{8,10},{9,11},{10,... | collective-permute-start | bytes 1572872 | tf_op jit(solution)/shard_map/ppermute | solution.py:66
  758.4 27.6 %collective-permute-start.121 = (bf16[2,128,1024]{2,1,0:T(8,128)(2,1)}, bf16[2,128,1024]{2,1,0:T(8,128)(2,1)}, u32[]{:S(2)}, u32[]{:S(2)}) collective-permute-start(bf16[2,128,1024]{2,1,0:T(8,128)(2,1)} %slice.389), channel_id=1, source_target_pairs={{0,8},{8,0},{16,24},{24,16},{1,9},{9,1},{17,25},{25,17},{2,10},{10... | collective-permute-start | bytes 1572872 | tf_op jit(solution)/shard_map/ppermute | solution.py:732
  760.4 25.7 %collective-permute-start.120 = (bf16[2,128,1024]{2,1,0:T(8,128)(2,1)}, bf16[2,128,1024]{2,1,0:T(8,128)(2,1)}, u32[]{:S(2)}, u32[]{:S(2)}) collective-permute-start(bf16[2,128,1024]{2,1,0:T(8,128)(2,1)} %slice.388), channel_id=1, source_target_pairs={{0,16},{8,24},{16,0},{24,8},{1,17},{9,25},{17,1},{25,9},{2,18},{10... | collective-permute-start | bytes 1572872 | tf_op jit(solution)/shard_map/ppermute | solution.py:732
  (184 other events, 1960.8 us)
Sparse Core Ops, SparseCore 0:
  115.9 55.6 all-gather.7
  178.7 87.8 all-gather.9
  573.7 67.0 all-gather.11
  648.2 127.5 all-gather.13

commit v5 on v4

--- a/solution.py
+++ b/solution.py
@@ -76,21 +76,20 @@
     return lax.optimization_barrier((values, earlier))[0]
 
 
-def gather_steps(col, values, early=(), beside=(), late=()):
+def gather_steps(col, values, early=(), beside=()):
     two = col.send(values, [(0, 2), (1, 3), (2, 0), (3, 1)])
     below = col.send(values, [(0, 1), (1, 2), (2, 3)])
     above = col.send(values, [(1, 0), (2, 1), (3, 2)])
     two, early = lax.optimization_barrier((two, early))
     two, below, above, beside = lax.optimization_barrier((two, below, above, beside))
     relayed = col.send(two, [(2, 3), (1, 0)])
-    relayed, late = lax.optimization_barrier((relayed, late))
-    return two, below, above, relayed, early, beside, late
+    return two, below, above, relayed, early, beside
 
 
 def gather_col(col, values, early, beside):
     if col.size != 4:
         return [col.fetch(values, k) for k in range(col.size)], early, beside
-    two, below, above, relayed, early, beside, _ = gather_steps(col, values, early, beside)
+    two, below, above, relayed, early, beside = gather_steps(col, values, early, beside)
     near = [
         values,
         jnp.where(col.here == 3, relayed, above),
@@ -115,7 +114,7 @@
 def gather_near(col, values, early=(), late=()):
     if col.size != 4:
         return [col.fetch(values, k) for k in range(col.size)], early, late
-    two, below, above, relayed, early, _, late = gather_steps(col, values, early, (), late)
+    two, below, above, relayed, early, late = gather_steps(col, values, early, late)
     inside = (col.here == 1) | (col.here == 2)
     near = [
         values,
@@ -883,14 +882,15 @@
         attn_scale = rms_scale(attended)
         hidden_state = own_input + attended * attn_scale * gain_attn_all
 
-        state_rows, _, w_gate_up = gather_tokens(
-            row, col, hidden_state.astype(BF), (), w_gate_up
-        )
-        w_gate, w_up = w_gate_up[0], w_gate_up[1]
-        grad_output = after(grad_output, state_rows)
+        state_low, grad_output = lax.optimization_barrier((hidden_state.astype(BF), grad_output))
         cotangent = exchange(
             col, lambda index: block_at(grad_output, index, own_tokens, 0)
         )
+        state_rows, _, (w_gate_up, cotangent) = gather_tokens(
+            row, col, state_low, (), (w_gate_up, cotangent)
+        )
+        cotangent = assemble(col, cotangent, 1).astype(F32)
+        w_gate, w_up = w_gate_up[0], w_gate_up[1]
         kept, activated = [], []
         for block in state_rows:
             pair = lax.optimization_barrier((dot(block, w_gate), dot(block, w_up)))
@@ -898,8 +898,6 @@
             kept.append(pair)
             activated.append((gate_values * jax.nn.sigmoid(gate_values) * up_values).astype(BF))
         lowered = [sum_rows(row, dot(block, w_down_all)) for block in activated]
-        lowered, cotangent = lax.optimization_barrier((lowered, cotangent))
-        cotangent = assemble(col, cotangent, 1).astype(F32)
         lowered, _, _ = reduce_near(col, lowered)
         ffn_scale = rms_scale(lowered)
         own_output = (hidden_state + lowered * ffn_scale * gain_ffn_all).astype(BF)
@@ -972,16 +970,22 @@
             grad_gain_query,
             grad_gain_key,
         ) = attend_backward(row, col, raw, lines, head_gains, tables, saved, grad_mixture)
-        gate_up_sum.came, down_parts, inner = lax.optimization_barrier(
-            (gate_up_sum.came, down_parts, inner)
-        )
-        gate_up_sum, _ = gate_up_sum.finish(())
+        gate_up_sum.came, down_parts, inner, mixture = lax.optimization_barrier(
+            (gate_up_sum.came, down_parts, inner, mixture)
+        )
+        out_grads = dot_tn(mixture, attended_rows).astype(BF)
+        out_grads = out_grads.reshape(n_dp, out_rows, n_col, n_out, -1)
+        out_grads = out_grads.transpose(2, 0, 3, 1, 4).reshape(n_col, n_dp, in_rows, -1)
+        out_grads = from_here(col, out_grads, 1, 0)
         down_back = assemble(col, [part[None] for part in down_parts], 0)
         down_all = gather_dp(down_back[None])
         small = jnp.stack([grad_gain_attn, grad_gain_ffn])
         inner, small = sum_all(row, col, inner[:2], lambda index: block_at(small, index, features, 1))
+        inner, out_grads = lax.optimization_barrier((inner, out_grads))
         inner = inner / width
-        gate_up_whole = after(jnp.stack(gate_up_sum), inner)
+        gate_up_sum.came, inner = lax.optimization_barrier((gate_up_sum.came, inner))
+        gate_up_sum, _ = gate_up_sum.finish(())
+        gate_up_whole = jnp.stack(gate_up_sum)
         gate_up_parts = exchange(
             col, lambda index: lax.dynamic_index_in_dim(gate_up_whole, index, 1, False)
         )
@@ -989,8 +993,6 @@
         head_gain_grads = [grad_gain_query.reshape(-1), grad_gain_key.reshape(-1)]
         small = sum((row.fetch(small, j) for j in range(1, n_row)), small)
         small = jnp.concatenate([small, jnp.stack(head_gain_grads)], axis=1)
-        for step in steps:
-            small = small + partner(small, step)
         grad_query = (
             query_scale * query_weighted
             - query_raw * (query_scale * query_scale * query_scale) * inner[0][:, None]
@@ -1002,13 +1004,15 @@
         grad_qkv = jnp.concatenate(
             [grad_query.astype(BF), grad_key.astype(BF), grad_value], axis=1
         )
-        grad_w_qkv = jnp.stack([dot_tn(rows, grad_qkv).astype(BF) for rows in input_rows])
+        small, grad_qkv = lax.optimization_barrier((small, grad_qkv))
+        grad_w_qkv = [dot_tn(rows, grad_qkv).astype(BF) for rows in input_rows]
+        for step in steps:
+            came = partner(small, step)
+            if step == steps[0]:
+                came, grad_w_qkv[0] = lax.optimization_barrier((came, grad_w_qkv[0]))
+            small = small + came
+        grad_w_qkv = jnp.stack(grad_w_qkv)
         qkv_grads = grad_w_qkv.reshape(n_col, n_dp, in_rows, 3 * head_cols)
-        out_grads = dot_tn(mixture, after(attended_rows, inner)).astype(BF)
-        out_grads = out_grads.reshape(n_dp, out_rows, n_col, n_out, -1)
-        out_grads = out_grads.transpose(2, 0, 3, 1, 4).reshape(n_col, n_dp, in_rows, -1)
-        out_grads = from_here(col, out_grads, 1, 0)
-
         def last_block(index):
             return halves_of(
                 jnp.concatenate(

time: 811 us -> 803 us (level)
    ppermute x68, waiting for transfers between devices: 83.3 us -> 115 us  [fetch(): return lax.ppermute(values, self.name, pairs)]
    ppermute x32, waiting for transfers between devices: 186 us -> 161 us  [send(): return lax.ppermute(values, self.name, pairs)]
    ppermute x22, waiting for transfers between devices: 85.2 us -> 70.2 us  [partner(): return lax.ppermute(values, 'dp', [(i, i ^ step) for i in range(n_dp)])]
    ppermute x32, starting transfers between devices: 70.3 us -> 84.9 us  [send(): return lax.ppermute(values, self.name, pairs)]
    unnamed x221 -> x193, local copies, waits for them, and re-layouts: 24.3 us -> 21.6 us
  transfers between devices with their start and end apart: 126 -> 126, of which waited for: 52 -> 49; matrix products, arithmetic and copies ran while one was open for 22% -> 21% of each run, Pallas kernels for 7% -> 7%
where the time goes in v5:
time: 803 us; the launch traced here: 791 us
  waiting for transfers between devices  353 us (44%)
  starting transfers between devices  166 us (21%)
  matrix products  89.4 us (11%)
  Pallas kernels  64.5 us (8%)
  other arithmetic  51.3 us (6%)
  local copies, waits for them, and re-layouts  49.3 us (6%)
  between operations  17.2 us (2%)
    ppermute x32, waiting for transfers between devices, send(): return lax.ppermute(values, self.name, pairs)  161 us
    ppermute x68, waiting for transfers between devices, fetch(): return lax.ppermute(values, self.name, pairs)  115 us
    ppermute x32, starting transfers between devices, send(): return lax.ppermute(values, self.name, pairs)  84.9 us
    ppermute x22, waiting for transfers between devices, partner(): return lax.ppermute(values, 'dp', [(i, i ^ step) for i in range(n_dp)])  70.2 us
    ppermute x68, starting transfers between devices, fetch(): return lax.ppermute(values, self.name, pairs)  55 us
    dot_general x20, matrix products, dot_nt(): lax.dot_general(a, b, (((1,), (1,)), ((), ())), preferred_element_type=F32)  37.9 us
    dot_general x24, matrix products, dot(): return jnp.dot(a, b, preferred_element_type=F32)  29.8 us
    ppermute x22, starting transfers between devices, partner(): return lax.ppermute(values, 'dp', [(i, i ^ step) for i in range(n_dp)])  26.3 us
  transfers between devices with their start and end apart: 126, of which 49 were waited for; matrix products, arithmetic and copies ran while one was open for 21% of the time, Pallas kernels for 7%

profile of v5, /device:TPU:0, one launch (start us, length us, event | category | flops | bytes accessed | tf_op | source)
XLA Modules:
  0.0 790.7 jit_solution(15343879142715604622)
XLA Ops:
  17.3 10.9 %collective-permute-done.1 = bf16[128,1024]{1,0:T(8,128)(2,1)S(1)} collective-permute-done((bf16[128,1024]{1,0:T(8,128)(2,1)S(1)}, bf16[128,1024]{1,0:T(8,128)(2,1)S(1)}, u32[]{:S(2)}, u32[]{:S(2)}) %collective-permute-start.1) | collective-permute-done | bytes 262176 | tf_op jit(solution)/shard_map/ppermute | solution.py:63
  28.2 5.1 collective-permute-done.2
  33.3 7.1 collective-permute-start.3
  42.3 5.3 collective-permute-start.4
  51.5 12.8 %collective-permute-done.3.refs_2_ = bf16[512,512]{1,0:T(8,128)(2,1)} collective-permute-done((bf16[512,512]{1,0:T(8,128)(2,1)}, bf16[512,512]{1,0:T(8,128)(2,1)}, u32[]{:S(2)}, u32[]{:S(2)}) %collective-permute-start.3) | collective-permute-done | bytes 524320 | tf_op jit(solution)/shard_map/ppermute | solution.py:66
  75.8 13.7 %collective-permute-done.6 = bf16[512,512]{1,0:T(8,128)(2,1)} collective-permute-done((bf16[512,512]{1,0:T(8,128)(2,1)}, bf16[512,512]{1,0:T(8,128)(2,1)}, u32[]{:S(2)}, u32[]{:S(2)}) %collective-permute-start.6) | collective-permute-done | bytes 524320 | tf_op jit(solution)/shard_map/ppermute | solution.py:66
  106.1 8.1 %collective-permute-done.16.refs_2_ = bf16[256,512]{1,0:T(8,128)(2,1)S(1)} collective-permute-done((bf16[256,512]{1,0:T(8,128)(2,1)S(1)}, bf16[256,512]{1,0:T(8,128)(2,1)S(1)}, u32[]{:S(2)}, u32[]{:S(2)}) %collective-permute-start.16) | collective-permute-done | bytes 262176 | tf_op jit(solution)/shard_map/ppermute | solution.py:63
  129.1 19.6 %collective-permute-done.21 = f32[2,1536]{1,0:T(2,128)S(1)} collective-permute-done((f32[2,1536]{1,0:T(2,128)S(1)}, f32[2,1536]{1,0:T(2,128)S(1)}, u32[]{:S(2)}, u32[]{:S(2)}) %collective-permute-start.21) | collective-permute-done | bytes 12320 | tf_op jit(solution)/shard_map/ppermute | solution.py:63
  151.5 11.3 %attend_forward.1 = (bf16[1024,256]{1,0:T(8,128)(2,1)}, bf16[1024,256]{1,0:T(8,128)(2,1)}, bf16[1024,256]{1,0:T(8,128)(2,1)}, bf16[1024,256]{1,0:T(8,128)(2,1)}) custom-call(s32[1]{0:T(128)} %bitcast.here_ref, f32[1024,768]{1,0:T(8,128)} %copy-done.13, f32[1024,768]{1,0:T(8,128)} %copy-done.13, f32[1024,768]{1,0:T(8,128)} %copy-done.13, ...), custom_call_target="tpu_custom_call" | custom-call | flops 1073741824 | bytes 5242880 | tf_op jit(solution)/shard_map/attend_forward/pallas_call | solution.py:635
  184.3 8.8 %collective-permute-done.31 = bf16[128,2048]{1,0:T(8,128)(2,1)S(1)} collective-permute-done((bf16[128,2048]{1,0:T(8,128)(2,1)}, bf16[128,2048]{1,0:T(8,128)(2,1)S(1)}, u32[]{:S(2)}, u32[]{:S(2)}) %collective-permute-start.31) | collective-permute-done | bytes 524320 | tf_op jit(solution)/shard_map/ppermute | solution.py:66
  198.3 6.1 collective-permute-done.30
  204.4 18.0 %collective-permute-done.32 = bf16[128,2048]{1,0:T(8,128)(2,1)S(1)} collective-permute-done((bf16[128,2048]{1,0:T(8,128)(2,1)S(1)}, bf16[128,2048]{1,0:T(8,128)(2,1)S(1)}, u32[]{:S(2)}, u32[]{:S(2)}) %collective-permute-start.32) | collective-permute-done | bytes 524320 | tf_op jit(solution)/shard_map/ppermute | solution.py:66
  226.1 4.6 collective-permute-start.35
  235.3 11.7 %collective-permute-done.34 = bf16[128,2048]{1,0:T(8,128)(2,1)S(1)} collective-permute-done((bf16[128,2048]{1,0:T(8,128)(2,1)}, bf16[128,2048]{1,0:T(8,128)(2,1)S(1)}, u32[]{:S(2)}, u32[]{:S(2)}) %collective-permute-start.34) | collective-permute-done | bytes 524320 | tf_op jit(solution)/shard_map/ppermute | solution.py:66
  252.4 12.7 %collective-permute-done.38.refs_2_ = bf16[128,512]{1,0:T(8,128)(2,1)S(1)} collective-permute-done((bf16[128,512]{1,0:T(8,128)(2,1)S(1)}, bf16[128,512]{1,0:T(8,128)(2,1)S(1)}, u32[]{:S(2)}, u32[]{:S(2)}) %collective-permute-start.38) | collective-permute-done | bytes 131104 | tf_op jit(solution)/shard_map/ppermute | solution.py:63
  304.1 4.6 collective-permute-start.47
  308.7 4.6 collective-permute-done.50
  318.1 9.8 %collective-permute-done.46 = bf16[128,2048]{1,0:T(8,128)(2,1)S(1)} collective-permute-done((bf16[128,2048]{1,0:T(8,128)(2,1)S(1)}, bf16[128,2048]{1,0:T(8,128)(2,1)S(1)}, u32[]{:S(2)}, u32[]{:S(2)}) %collective-permute-start.46) | collective-permute-done | bytes 524320 | tf_op jit(solution)/shard_map/ppermute | solution.py:66
  327.9 13.1 %collective-permute-done.51 = bf16[128,2048]{1,0:T(8,128)(2,1)S(1)} collective-permute-done((bf16[128,2048]{1,0:T(8,128)(2,1)S(1)}, bf16[128,2048]{1,0:T(8,128)(2,1)S(1)}, u32[]{:S(2)}, u32[]{:S(2)}) %collective-permute-start.51) | collective-permute-done | bytes 524320 | tf_op jit(solution)/shard_map/ppermute | solution.py:66
  345.1 7.9 %collective-permute-start.53 = (bf16[128,2048]{1,0:T(8,128)(2,1)}, bf16[128,2048]{1,0:T(8,128)(2,1)S(1)}, u32[]{:S(2)}, u32[]{:S(2)}) collective-permute-start(bf16[128,2048]{1,0:T(8,128)(2,1)} %get-tuple-element.425), channel_id=1, source_target_pairs={{0,1},{1,2},{2,3},{4,5},{5,6},{6,7},{8,9},{9,10},{10,11},{12,13},{... | collective-permute-start | bytes 1572872 | tf_op jit(solution)/shard_map/ppermute | solution.py:66
  357.2 13.9 %collective-permute-done.52 = bf16[128,2048]{1,0:T(8,128)(2,1)} collective-permute-done((bf16[128,2048]{1,0:T(8,128)(2,1)}, bf16[128,2048]{1,0:T(8,128)(2,1)}, u32[]{:S(2)}, u32[]{:S(2)}) %collective-permute-start.52) | collective-permute-done | bytes 524320 | tf_op jit(solution)/shard_map/ppermute | solution.py:66
  387.7 7.4 collective-permute-done.57
  413.4 4.4 collective-permute-start.68
  419.6 4.6 collective-permute-start.61
  424.2 5.9 collective-permute-done.68
  430.3 4.9 convolution_convert_fusion.2
  440.0 4.9 convolution_convert_fusion
  444.9 4.9 convolution_convert_fusion.1
  455.7 4.6 collective-permute-done.69
  469.7 5.0 collective-permute-start.78
  474.7 14.3 %collective-permute-done.70 = bf16[128,2048]{1,0:T(8,128)(2,1)S(1)} collective-permute-done((bf16[128,2048]{1,0:T(8,128)(2,1)S(1)}, bf16[128,2048]{1,0:T(8,128)(2,1)S(1)}, u32[]{:S(2)}, u32[]{:S(2)}) %collective-permute-start.70) | collective-permute-done | bytes 524320 | tf_op jit(solution)/shard_map/ppermute | solution.py:66
  491.0 16.9 %collective-permute-done.72 = bf16[2,4,128,1024]{3,2,0,1:T(8,128)(2,1)} collective-permute-done((bf16[2,4,128,1024]{3,2,0,1:T(8,128)(2,1)}, bf16[2,4,128,1024]{3,2,0,1:T(8,128)(2,1)}, u32[]{:S(2)}, u32[]{:S(2)}) %collective-permute-start.72) | collective-permute-done | bytes 2097184 | tf_op jit(solution)/shard_map/ppermute | solution.py:731
  514.5 8.1 %collective-permute-done.82 = bf16[128,2048]{1,0:T(8,128)(2,1)S(1)} collective-permute-done((bf16[128,2048]{1,0:T(8,128)(2,1)S(1)}, bf16[128,2048]{1,0:T(8,128)(2,1)S(1)}, u32[]{:S(2)}, u32[]{:S(2)}) %collective-permute-start.82) | collective-permute-done | bytes 524320 | tf_op jit(solution)/shard_map/ppermute | solution.py:66
  538.2 14.4 %attend_backward.1 = (f32[1024,256]{1,0:T(8,128)}, f32[1024,256]{1,0:T(8,128)}, bf16[1024,256]{1,0:T(8,128)(2,1)}, f32[8,1024]{1,0:T(8,128)}, f32[2,1,128]{2,1,0:T(1,128)}, /*index=5*/f32[2,1,128]{2,1,0:T(1,128)}) custom-call(s32[1]{0:T(128)} %bitcast.here_ref, f32[1024,768]{1,0:T(8,128)} %copy-done.13, f32[1024,768]{1,0:T(8,128)} %copy-done.13, ...), custom_call_target="tpu_custom_call" | custom-call | flops 2684354560 | bytes 7864320 | tf_op jit(solution)/shard_map/attend_backward/pallas_call | solution.py:667
  552.7 5.8 collective-permute-done.85
  605.5 21.7 %collective-permute-done.92 = bf16[2,128,1024]{2,1,0:T(8,128)(2,1)S(1)} collective-permute-done((bf16[2,128,1024]{2,1,0:T(8,128)(2,1)S(1)}, bf16[2,128,1024]{2,1,0:T(8,128)(2,1)S(1)}, u32[]{:S(2)}, u32[]{:S(2)}) %collective-permute-start.92) | collective-permute-done | bytes 524320 | tf_op jit(solution)/shard_map/ppermute | solution.py:63
  627.2 10.6 %collective-permute-done.97 = bf16[2,4,128,512]{3,2,1,0:T(8,128)(2,1)S(1)} collective-permute-done((bf16[2,4,128,512]{3,2,1,0:T(8,128)(2,1)S(1)}, bf16[2,4,128,512]{3,2,1,0:T(8,128)(2,1)S(1)}, u32[]{:S(2)}, u32[]{:S(2)}) %collective-permute-start.97) | collective-permute-done | bytes 1048608 | tf_op jit(solution)/shard_map/ppermute | solution.py:731
  655.0 12.3 %collective-permute-done.104 = bf16[1,4,128,512]{3,2,1,0:T(8,128)(2,1)S(1)} collective-permute-done((bf16[1,4,128,512]{3,2,1,0:T(8,128)(2,1)S(1)}, bf16[1,4,128,512]{3,2,1,0:T(8,128)(2,1)S(1)}, u32[]{:S(2)}, u32[]{:S(2)}) %collective-permute-start.104) | collective-permute-done | bytes 524320 | tf_op jit(solution)/shard_map/ppermute | solution.py:731
  667.3 5.9 collective-permute-done.105
  680.4 10.9 %down_gradients.1 = f32[4,4,256,512]{3,2,1,0:T(8,128)} custom-call(bf16[4,4,256,512]{3,2,1,0:T(8,128)(2,1)} %bitcast.355), custom_call_target="tpu_custom_call" | custom-call | bytes 12582912 | tf_op jit(solution)/shard_map/down_gradients/pallas_call | solution.py:287
  691.4 7.7 collective-permute-done.107
  710.1 8.0 %collective-permute-done.112.refs_2_ = bf16[128,512]{1,0:T(8,128)(2,1)S(1)} collective-permute-done((bf16[128,512]{1,0:T(8,128)(2,1)S(1)}, bf16[128,512]{1,0:T(8,128)(2,1)S(1)}, u32[]{:S(2)}, u32[]{:S(2)}) %collective-permute-start.112) | collective-permute-done | bytes 131104 | tf_op jit(solution)/shard_map/ppermute | solution.py:63
  721.0 5.1 collective-permute-done.115.refs_2_
  730.8 16.2 %collective-permute-done.110.refs_2_ = bf16[4,128,1024]{2,1,0:T(8,128)(2,1)S(1)} collective-permute-done((bf16[4,128,1024]{2,1,0:T(8,128)(2,1)S(1)}, bf16[4,128,1024]{2,1,0:T(8,128)(2,1)S(1)}, u32[]{:S(2)}, u32[]{:S(2)}) %collective-permute-start.110) | collective-permute-done | bytes 1048608 | tf_op jit(solution)/shard_map/ppermute | solution.py:731
  755.9 4.9 collective-permute-done.119
  762.1 4.8 all-gather.14.cloned.1.call-done
  766.9 10.2 %pair_gradients.1 = (f32[512,4096]{1,0:T(8,128)}, f32[512,4096]{1,0:T(8,128)}) custom-call(bf16[4,4,2,128,1024]{4,3,2,1,0:T(8,128)(2,1)} %bitcast.354), custom_call_target="tpu_custom_call" | custom-call | bytes 25165824 | tf_op jit(solution)/shard_map/pair_gradients/pallas_call | solution.py:264
  777.2 6.5 last_gradients.1
  (640 shorter events, 332.9 us)
Async XLA Ops:
  7.2 167.4 %all-gather.8.cloned.1.call-start = ((), (), s32[]{:S(2)}) async-start(), calls=%async_computation | async-start | bytes 5242880 | tf_op jit(solution)/shard_map/all_gather | solution.py:726
  33.3 31.0 %collective-permute-start.3 = (bf16[512,512]{1,0:T(8,128)(2,1)}, bf16[512,512]{1,0:T(8,128)(2,1)}, u32[]{:S(2)}, u32[]{:S(2)}) collective-permute-start(bf16[512,512]{1,0:T(8,128)(2,1)} %refs_0_), channel_id=1, source_target_pairs={{0,2},{1,3},{2,0},{3,1},{4,6},{5,7},{6,4},{7,5},{8,10},{9,11},{10,... | collective-permute-start | bytes 1572872 | tf_op jit(solution)/shard_map/ppermute | solution.py:66
  41.0 26.8 %collective-permute-start.5 = (bf16[512,512]{1,0:T(8,128)(2,1)}, bf16[512,512]{1,0:T(8,128)(2,1)}, u32[]{:S(2)}, u32[]{:S(2)}) collective-permute-start(bf16[512,512]{1,0:T(8,128)(2,1)} %refs_0_), channel_id=1, source_target_pairs={{1,0},{2,1},{3,2},{5,4},{6,5},{7,6},{9,8},{10,9},{11,10},{13,12},{... | collective-permute-start | bytes 1572872 | tf_op jit(solution)/shard_map/ppermute | solution.py:66
  42.3 25.5 %collective-permute-start.4 = (bf16[512,512]{1,0:T(8,128)(2,1)}, bf16[512,512]{1,0:T(8,128)(2,1)}, u32[]{:S(2)}, u32[]{:S(2)}) collective-permute-start(bf16[512,512]{1,0:T(8,128)(2,1)} %refs_0_), channel_id=1, source_target_pairs={{0,1},{1,2},{2,3},{4,5},{5,6},{6,7},{8,9},{9,10},{10,11},{12,13},{... | collective-permute-start | bytes 1572872 | tf_op jit(solution)/shard_map/ppermute | solution.py:66
  47.8 24.7 %collective-permute-start.9 = (bf16[4,128,1024]{2,1,0:T(8,128)(2,1)S(1)}, bf16[4,128,1024]{2,1,0:T(8,128)(2,1)S(1)}, u32[]{:S(2)}, u32[]{:S(2)}) collective-permute-start(bf16[4,128,1024]{2,1,0:T(8,128)(2,1)S(1)} %pad_maximum_fusion.7.refs_0_), channel_id=1, source_target_pairs={{0,16},{8,24},{16,0},{24,8},{1,17},{9,25},{17,1},{25,9},{2,18},{10... | collective-permute-start | bytes 3145736 | tf_op jit(solution)/shard_map/ppermute | solution.py:731
  49.4 24.0 %collective-permute-start.8 = (bf16[4,128,1024]{2,1,0:T(8,128)(2,1)S(1)}, bf16[4,128,1024]{2,1,0:T(8,128)(2,1)S(1)}, u32[]{:S(2)}, u32[]{:S(2)}) collective-permute-start(bf16[4,128,1024]{2,1,0:T(8,128)(2,1)S(1)} %pad_maximum_fusion.7.refs_0_), channel_id=1, source_target_pairs={{0,8},{8,0},{16,24},{24,16},{1,9},{9,1},{17,25},{25,17},{2,10},{10... | collective-permute-start | bytes 3145736 | tf_op jit(solution)/shard_map/ppermute | solution.py:731
  115.8 150.9 %all-gather.10.cloned.1.call-start = ((), (), s32[]{:S(2)}) async-start(), calls=%async_computation.1 | async-start | bytes 10485760 | tf_op jit(solution)/shard_map/all_gather | solution.py:880
  118.7 31.3 %collective-permute-start.22 = (bf16[2,128,1024]{2,1,0:T(8,128)(2,1)S(1)}, bf16[2,128,1024]{2,1,0:T(8,128)(2,1)S(1)}, u32[]{:S(2)}, u32[]{:S(2)}) collective-permute-start(bf16[2,128,1024]{2,1,0:T(8,128)(2,1)S(1)} %pad_maximum_fusion.34), channel_id=1, source_target_pairs={{0,3},{1,0},{2,1},{3,2},{4,7},{5,4},{6,5},{7,6},{8,11},{9,8},{10,9... | collective-permute-start | bytes 1572872 | tf_op jit(solution)/shard_map/ppermute | solution.py:63
  122.8 27.2 %collective-permute-start.23 = (bf16[2,128,1024]{2,1,0:T(8,128)(2,1)S(1)}, bf16[2,128,1024]{2,1,0:T(8,128)(2,1)S(1)}, u32[]{:S(2)}, u32[]{:S(2)}) collective-permute-start(bf16[2,128,1024]{2,1,0:T(8,128)(2,1)S(1)} %pad_maximum_fusion.35), channel_id=1, source_target_pairs={{0,1},{1,2},{2,3},{3,0},{4,5},{5,6},{6,7},{7,4},{8,9},{9,10},{10,1... | collective-permute-start | bytes 1572872 | tf_op jit(solution)/shard_map/ppermute | solution.py:63
  124.3 24.3 %collective-permute-start.21 = (f32[2,1536]{1,0:T(2,128)S(1)}, f32[2,1536]{1,0:T(2,128)S(1)}, u32[]{:S(2)}, u32[]{:S(2)}) collective-permute-start(f32[2,1536]{1,0:T(2,128)S(1)} %maximum_maximum_fusion.1), channel_id=1, source_target_pairs={{0,1},{1,2},{2,3},{3,0},{4,5},{5,6},{6,7},{7,4},{8,9},{9,10},{10,1... | collective-permute-start | bytes 36872 | tf_op jit(solution)/shard_map/ppermute | solution.py:63
  148.6 25.2 %collective-permute-start.24 = (bf16[2,128,1024]{2,1,0:T(8,128)(2,1)S(1)}, bf16[2,128,1024]{2,1,0:T(8,128)(2,1)S(1)}, u32[]{:S(2)}, u32[]{:S(2)}) collective-permute-start(bf16[2,128,1024]{2,1,0:T(8,128)(2,1)S(1)} %pad_maximum_fusion.36), channel_id=1, source_target_pairs={{0,2},{1,3},{2,0},{3,1},{4,6},{5,7},{6,4},{7,5},{8,10},{9,11},{10,... | collective-permute-start | bytes 1572872 | tf_op jit(solution)/shard_map/ppermute | solution.py:63
  178.6 501.9 %all-gather.12.cloned.1.call-start = ((), (), s32[]{:S(2)}) async-start(), calls=%async_computation.2 | async-start | bytes 5242880 | tf_op jit(solution)/shard_map/all_gather | solution.py:726
  193.3 29.1 %collective-permute-start.32 = (bf16[128,2048]{1,0:T(8,128)(2,1)S(1)}, bf16[128,2048]{1,0:T(8,128)(2,1)S(1)}, u32[]{:S(2)}, u32[]{:S(2)}) collective-permute-start(bf16[128,2048]{1,0:T(8,128)(2,1)S(1)} %add_convert_fusion.5), channel_id=1, source_target_pairs={{0,2},{1,3},{2,0},{3,1},{4,6},{5,7},{6,4},{7,5},{8,10},{9,11},{10,... | collective-permute-start | bytes 1572872 | tf_op jit(solution)/shard_map/ppermute | solution.py:66
  224.8 40.3 %collective-permute-start.36 = (bf16[128,2048]{1,0:T(8,128)(2,1)}, bf16[128,2048]{1,0:T(8,128)(2,1)}, u32[]{:S(2)}, u32[]{:S(2)}) collective-permute-start(bf16[128,2048]{1,0:T(8,128)(2,1)} %fusion.148), channel_id=1, source_target_pairs={{1,0},{2,1},{3,2},{5,4},{6,5},{7,6},{9,8},{10,9},{11,10},{13,12},{... | collective-permute-start | bytes 1572872 | tf_op jit(solution)/shard_map/ppermute | solution.py:66
  226.1 39.0 %collective-permute-start.35 = (bf16[128,2048]{1,0:T(8,128)(2,1)}, bf16[128,2048]{1,0:T(8,128)(2,1)S(1)}, u32[]{:S(2)}, u32[]{:S(2)}) collective-permute-start(bf16[128,2048]{1,0:T(8,128)(2,1)} %fusion.148), channel_id=1, source_target_pairs={{0,1},{1,2},{2,3},{4,5},{5,6},{6,7},{8,9},{9,10},{10,11},{12,13},{... | collective-permute-start | bytes 1572872 | tf_op jit(solution)/shard_map/ppermute | solution.py:66
  302.7 25.2 %collective-permute-start.40 = (bf16[128,2048]{1,0:T(8,128)(2,1)S(1)}, bf16[128,2048]{1,0:T(8,128)(2,1)S(1)}, u32[]{:S(2)}, u32[]{:S(2)}) collective-permute-start(bf16[128,2048]{1,0:T(8,128)(2,1)S(1)} %slice.671), channel_id=1, source_target_pairs={{0,4},{4,0},{1,5},{5,1},{2,6},{6,2},{3,7},{7,3},{8,12},{12,8},{9,1... | collective-permute-start | bytes 1572872 | tf_op jit(solution)/shard_map/ppermute | solution.py:63
  302.8 25.1 %collective-permute-start.46 = (bf16[128,2048]{1,0:T(8,128)(2,1)S(1)}, bf16[128,2048]{1,0:T(8,128)(2,1)S(1)}, u32[]{:S(2)}, u32[]{:S(2)}) collective-permute-start(bf16[128,2048]{1,0:T(8,128)(2,1)S(1)} %get-tuple-element.428), channel_id=1, source_target_pairs={{1,0},{2,1},{3,2},{5,4},{6,5},{7,6},{9,8},{10,9},{11,10},{13,12},{... | collective-permute-start | bytes 1572872 | tf_op jit(solution)/shard_map/ppermute | solution.py:66
  313.5 27.6 %collective-permute-start.51 = (bf16[128,2048]{1,0:T(8,128)(2,1)S(1)}, bf16[128,2048]{1,0:T(8,128)(2,1)S(1)}, u32[]{:S(2)}, u32[]{:S(2)}) collective-permute-start(bf16[128,2048]{1,0:T(8,128)(2,1)S(1)} %fusion.68), channel_id=1, source_target_pairs={{0,2},{1,3},{2,0},{3,1},{4,6},{5,7},{6,4},{7,5},{8,10},{9,11},{10,... | collective-permute-start | bytes 1572872 | tf_op jit(solution)/shard_map/ppermute | solution.py:66
  343.8 27.4 %collective-permute-start.52 = (bf16[128,2048]{1,0:T(8,128)(2,1)}, bf16[128,2048]{1,0:T(8,128)(2,1)}, u32[]{:S(2)}, u32[]{:S(2)}) collective-permute-start(bf16[128,2048]{1,0:T(8,128)(2,1)} %get-tuple-element.425), channel_id=1, source_target_pairs={{0,2},{1,3},{2,0},{3,1},{4,6},{5,7},{6,4},{7,5},{8,10},{9,11},{10,... | collective-permute-start | bytes 1572872 | tf_op jit(solution)/shard_map/ppermute | solution.py:66
  343.8 27.5 %collective-permute-start.54 = (bf16[128,2048]{1,0:T(8,128)(2,1)}, bf16[128,2048]{1,0:T(8,128)(2,1)}, u32[]{:S(2)}, u32[]{:S(2)}) collective-permute-start(bf16[128,2048]{1,0:T(8,128)(2,1)} %get-tuple-element.425), channel_id=1, source_target_pairs={{1,0},{2,1},{3,2},{5,4},{6,5},{7,6},{9,8},{10,9},{11,10},{13,12},{... | collective-permute-start | bytes 1572872 | tf_op jit(solution)/shard_map/ppermute | solution.py:66
  345.1 26.2 %collective-permute-start.53 = (bf16[128,2048]{1,0:T(8,128)(2,1)}, bf16[128,2048]{1,0:T(8,128)(2,1)S(1)}, u32[]{:S(2)}, u32[]{:S(2)}) collective-permute-start(bf16[128,2048]{1,0:T(8,128)(2,1)} %get-tuple-element.425), channel_id=1, source_target_pairs={{0,1},{1,2},{2,3},{4,5},{5,6},{6,7},{8,9},{9,10},{10,11},{12,13},{... | collective-permute-start | bytes 1572872 | tf_op jit(solution)/shard_map/ppermute | solution.py:66
  382.6 30.3 %collective-permute-start.64 = (bf16[128,2048]{1,0:T(8,128)(2,1)S(1)}, bf16[128,2048]{1,0:T(8,128)(2,1)S(1)}, u32[]{:S(2)}, u32[]{:S(2)}) collective-permute-start(bf16[128,2048]{1,0:T(8,128)(2,1)S(1)} %slice.665), channel_id=1, source_target_pairs={{0,4},{4,0},{1,5},{5,1},{2,6},{6,2},{3,7},{7,3},{8,12},{12,8},{9,1... | collective-permute-start | bytes 1572872 | tf_op jit(solution)/shard_map/ppermute | solution.py:63
  418.3 31.6 %collective-permute-start.60 = (bf16[128,2048]{1,0:T(8,128)(2,1)S(1)}, bf16[128,2048]{1,0:T(8,128)(2,1)S(1)}, u32[]{:S(2)}, u32[]{:S(2)}) collective-permute-start(bf16[128,2048]{1,0:T(8,128)(2,1)S(1)} %get-tuple-element.411), channel_id=1, source_target_pairs={{1,0},{2,1},{3,2},{5,4},{6,5},{7,6},{9,8},{10,9},{11,10},{13,12},{... | collective-permute-start | bytes 1572872 | tf_op jit(solution)/shard_map/ppermute | solution.py:66
  419.6 30.3 %collective-permute-start.61 = (bf16[128,2048]{1,0:T(8,128)(2,1)S(1)}, bf16[128,2048]{1,0:T(8,128)(2,1)S(1)}, u32[]{:S(2)}, u32[]{:S(2)}) collective-permute-start(bf16[128,2048]{1,0:T(8,128)(2,1)S(1)} %get-tuple-element.413), channel_id=1, source_target_pairs={{0,1},{1,2},{2,3},{4,5},{5,6},{6,7},{8,9},{9,10},{10,11},{12,13},{... | collective-permute-start | bytes 1572872 | tf_op jit(solution)/shard_map/ppermute | solution.py:66
  435.2 25.0 %collective-permute-start.69 = (bf16[128,2048]{1,0:T(8,128)(2,1)S(1)}, bf16[128,2048]{1,0:T(8,128)(2,1)S(1)}, u32[]{:S(2)}, u32[]{:S(2)}) collective-permute-start(bf16[128,2048]{1,0:T(8,128)(2,1)S(1)} %add_convert_fusion.4), channel_id=1, source_target_pairs={{0,2},{1,3},{2,0},{3,1},{4,6},{5,7},{6,4},{7,5},{8,10},{9,11},{10,... | collective-permute-start | bytes 1572872 | tf_op jit(solution)/shard_map/ppermute | solution.py:66
  437.7 26.2 %collective-permute-start.66 = (bf16[2,256,1024]{2,1,0:T(8,128)(2,1)S(1)}, bf16[2,256,1024]{2,1,0:T(8,128)(2,1)S(1)}, u32[]{:S(2)}, u32[]{:S(2)}) collective-permute-start(bf16[2,256,1024]{2,1,0:T(8,128)(2,1)S(1)} %pad_maximum_fusion.12), channel_id=1, source_target_pairs={{0,8},{8,0},{16,24},{24,16},{1,9},{9,1},{17,25},{25,17},{2,10},{10... | collective-permute-start | bytes 3145736 | tf_op jit(solution)/shard_map/ppermute | solution.py:731
  439.3 26.2 %collective-permute-start.67 = (bf16[2,256,1024]{2,1,0:T(8,128)(2,1)S(1)}, bf16[2,256,1024]{2,1,0:T(8,128)(2,1)S(1)}, u32[]{:S(2)}, u32[]{:S(2)}) collective-permute-start(bf16[2,256,1024]{2,1,0:T(8,128)(2,1)S(1)} %pad_maximum_fusion.13), channel_id=1, source_target_pairs={{0,16},{8,24},{16,0},{24,8},{1,17},{9,25},{17,1},{25,9},{2,18},{10... | collective-permute-start | bytes 3145736 | tf_op jit(solution)/shard_map/ppermute | solution.py:731
  451.9 56.0 %collective-permute-start.72 = (bf16[2,4,128,1024]{3,2,0,1:T(8,128)(2,1)}, bf16[2,4,128,1024]{3,2,0,1:T(8,128)(2,1)}, u32[]{:S(2)}, u32[]{:S(2)}) collective-permute-start(bf16[2,4,128,1024]{3,2,0,1:T(8,128)(2,1)} %pad_maximum_fusion.5), channel_id=1, source_target_pairs={{0,16},{8,24},{16,0},{24,8},{1,17},{9,25},{17,1},{25,9},{2,18},{10... | collective-permute-start | bytes 6291464 | tf_op jit(solution)/shard_map/ppermute | solution.py:731
  455.1 53.4 %collective-permute-start.71 = (bf16[2,4,128,1024]{3,2,0,1:T(8,128)(2,1)}, bf16[2,4,128,1024]{3,2,0,1:T(8,128)(2,1)}, u32[]{:S(2)}, u32[]{:S(2)}) collective-permute-start(bf16[2,4,128,1024]{3,2,0,1:T(8,128)(2,1)} %pad_maximum_fusion.4), channel_id=1, source_target_pairs={{0,8},{8,0},{16,24},{24,16},{1,9},{9,1},{17,25},{25,17},{2,10},{10... | collective-permute-start | bytes 6291464 | tf_op jit(solution)/shard_map/ppermute | solution.py:731
  468.4 41.6 %collective-permute-start.79 = (bf16[128,2048]{1,0:T(8,128)(2,1)S(1)}, bf16[128,2048]{1,0:T(8,128)(2,1)S(1)}, u32[]{:S(2)}, u32[]{:S(2)}) collective-permute-start(bf16[128,2048]{1,0:T(8,128)(2,1)S(1)} %get-tuple-element.478), channel_id=1, source_target_pairs={{1,0},{2,1},{3,2},{5,4},{6,5},{7,6},{9,8},{10,9},{11,10},{13,12},{... | collective-permute-start | bytes 1572872 | tf_op jit(solution)/shard_map/ppermute | solution.py:66
  469.7 40.3 %collective-permute-start.78 = (bf16[128,2048]{1,0:T(8,128)(2,1)S(1)}, bf16[128,2048]{1,0:T(8,128)(2,1)S(1)}, u32[]{:S(2)}, u32[]{:S(2)}) collective-permute-start(bf16[128,2048]{1,0:T(8,128)(2,1)S(1)} %get-tuple-element.478), channel_id=1, source_target_pairs={{0,1},{1,2},{2,3},{4,5},{5,6},{6,7},{8,9},{9,10},{10,11},{12,13},{... | collective-permute-start | bytes 1572872 | tf_op jit(solution)/shard_map/ppermute | solution.py:66
  526.3 26.4 %collective-permute-start.74 = (bf16[1,4,128,1024]{3,2,0,1:T(8,128)(2,1)}, bf16[1,4,128,1024]{3,2,0,1:T(8,128)(2,1)}, u32[]{:S(2)}, u32[]{:S(2)}) collective-permute-start(bf16[1,4,128,1024]{3,2,0,1:T(8,128)(2,1)} %fusion.56), channel_id=1, source_target_pairs={{0,8},{8,0},{16,24},{24,16},{1,9},{9,1},{17,25},{25,17},{2,10},{10... | collective-permute-start | bytes 3145736 | tf_op jit(solution)/shard_map/ppermute | solution.py:731
  526.9 25.7 %collective-permute-start.73 = (bf16[1,4,128,1024]{3,2,0,1:T(8,128)(2,1)}, bf16[1,4,128,1024]{3,2,0,1:T(8,128)(2,1)}, u32[]{:S(2)}, u32[]{:S(2)}) collective-permute-start(bf16[1,4,128,1024]{3,2,0,1:T(8,128)(2,1)} %fusion.57), channel_id=1, source_target_pairs={{0,16},{8,24},{16,0},{24,8},{1,17},{9,25},{17,1},{25,9},{2,18},{10... | collective-permute-start | bytes 3145736 | tf_op jit(solution)/shard_map/ppermute | solution.py:731
  565.4 201.5 %all-gather.14.cloned.1.call-start = ((), (), s32[]{:S(2)}) async-start(), calls=%async_computation.3 | async-start | bytes 10485760 | tf_op jit(solution)/shard_map/all_gather | solution.py:726
  578.2 27.4 %collective-permute-start.93 = (bf16[2,128,1024]{2,1,0:T(8,128)(2,1)S(1)}, bf16[2,128,1024]{2,1,0:T(8,128)(2,1)S(1)}, u32[]{:S(2)}, u32[]{:S(2)}) collective-permute-start(bf16[2,128,1024]{2,1,0:T(8,128)(2,1)S(1)} %get-tuple-element.463), channel_id=1, source_target_pairs={{0,1},{1,2},{2,3},{3,0},{4,5},{5,6},{6,7},{7,4},{8,9},{9,10},{10,1... | collective-permute-start | bytes 1572872 | tf_op jit(solution)/shard_map/ppermute | solution.py:63
  578.8 26.7 %collective-permute-start.91 = (bf16[2,128,1024]{2,1,0:T(8,128)(2,1)S(1)}, bf16[2,128,1024]{2,1,0:T(8,128)(2,1)S(1)}, u32[]{:S(2)}, u32[]{:S(2)}) collective-permute-start(bf16[2,128,1024]{2,1,0:T(8,128)(2,1)S(1)} %get-tuple-element.465), channel_id=1, source_target_pairs={{0,3},{1,0},{2,1},{3,2},{4,7},{5,4},{6,5},{7,6},{8,11},{9,8},{10,9... | collective-permute-start | bytes 1572872 | tf_op jit(solution)/shard_map/ppermute | solution.py:63
  582.0 45.2 %collective-permute-start.92 = (bf16[2,128,1024]{2,1,0:T(8,128)(2,1)S(1)}, bf16[2,128,1024]{2,1,0:T(8,128)(2,1)S(1)}, u32[]{:S(2)}, u32[]{:S(2)}) collective-permute-start(bf16[2,128,1024]{2,1,0:T(8,128)(2,1)S(1)} %get-tuple-element.466), channel_id=1, source_target_pairs={{0,2},{1,3},{2,0},{3,1},{4,6},{5,7},{6,4},{7,5},{8,10},{9,11},{10,... | collective-permute-start | bytes 1572872 | tf_op jit(solution)/shard_map/ppermute | solution.py:63
  593.9 43.9 %collective-permute-start.97 = (bf16[2,4,128,512]{3,2,1,0:T(8,128)(2,1)S(1)}, bf16[2,4,128,512]{3,2,1,0:T(8,128)(2,1)S(1)}, u32[]{:S(2)}, u32[]{:S(2)}) collective-permute-start(bf16[2,4,128,512]{3,2,1,0:T(8,128)(2,1)S(1)} %pad_maximum_fusion.18), channel_id=1, source_target_pairs={{0,8},{8,0},{16,24},{24,16},{1,9},{9,1},{17,25},{25,17},{2,10},{10... | collective-permute-start | bytes 3145736 | tf_op jit(solution)/shard_map/ppermute | solution.py:731
  595.3 42.6 %collective-permute-start.98 = (bf16[2,4,128,512]{3,2,1,0:T(8,128)(2,1)S(1)}, bf16[2,4,128,512]{3,2,1,0:T(8,128)(2,1)}, u32[]{:S(2)}, u32[]{:S(2)}) collective-permute-start(bf16[2,4,128,512]{3,2,1,0:T(8,128)(2,1)S(1)} %pad_maximum_fusion.19), channel_id=1, source_target_pairs={{0,16},{8,24},{16,0},{24,8},{1,17},{9,25},{17,1},{25,9},{2,18},{10... | collective-permute-start | bytes 3145736 | tf_op jit(solution)/shard_map/ppermute | solution.py:731
  648.2 24.9 %collective-permute-start.105 = (bf16[1,4,128,512]{3,2,1,0:T(8,128)(2,1)S(1)}, bf16[1,4,128,512]{3,2,1,0:T(8,128)(2,1)S(1)}, u32[]{:S(2)}, u32[]{:S(2)}) collective-permute-start(bf16[1,4,128,512]{3,2,1,0:T(8,128)(2,1)S(1)} %fusion.152), channel_id=1, source_target_pairs={{0,8},{8,0},{16,24},{24,16},{1,9},{9,1},{17,25},{25,17},{2,10},{10... | collective-permute-start | bytes 1572872 | tf_op jit(solution)/shard_map/ppermute | solution.py:731
  651.5 28.0 %collective-permute-start.103 = (bf16[512,512]{1,0:T(8,128)(2,1)S(1)}, bf16[512,512]{1,0:T(8,128)(2,1)S(1)}, u32[]{:S(2)}, u32[]{:S(2)}) collective-permute-start(bf16[512,512]{1,0:T(8,128)(2,1)S(1)} %get-tuple-element.407), channel_id=1, source_target_pairs={{3,2},{0,1},{7,6},{4,5},{11,10},{8,9},{15,14},{12,13},{19,18},{16,... | collective-permute-start | bytes 1572872 | tf_op jit(solution)/shard_map/ppermute | solution.py:66
  699.2 47.8 %collective-permute-start.110 = (bf16[4,128,1024]{2,1,0:T(8,128)(2,1)S(1)}, bf16[4,128,1024]{2,1,0:T(8,128)(2,1)S(1)}, u32[]{:S(2)}, u32[]{:S(2)}) collective-permute-start(bf16[4,128,1024]{2,1,0:T(8,128)(2,1)S(1)} %pad_maximum_fusion.20.refs_0_), channel_id=1, source_target_pairs={{0,16},{8,24},{16,0},{24,8},{1,17},{9,25},{17,1},{25,9},{2,18},{10... | collective-permute-start | bytes 3145736 | tf_op jit(solution)/shard_map/ppermute | solution.py:731
  699.3 48.4 %collective-permute-start.109 = (bf16[4,128,1024]{2,1,0:T(8,128)(2,1)S(1)}, bf16[4,128,1024]{2,1,0:T(8,128)(2,1)S(1)}, u32[]{:S(2)}, u32[]{:S(2)}) collective-permute-start(bf16[4,128,1024]{2,1,0:T(8,128)(2,1)S(1)} %pad_maximum_fusion.20.refs_0_), channel_id=1, source_target_pairs={{0,8},{8,0},{16,24},{24,16},{1,9},{9,1},{17,25},{25,17},{2,10},{10... | collective-permute-start | bytes 3145736 | tf_op jit(solution)/shard_map/ppermute | solution.py:731
  719.7 34.6 %collective-permute-start.117 = (bf16[512,512]{1,0:T(8,128)(2,1)S(1)}, bf16[512,512]{1,0:T(8,128)(2,1)S(1)}, u32[]{:S(2)}, u32[]{:S(2)}) collective-permute-start(bf16[512,512]{1,0:T(8,128)(2,1)S(1)} %copy-done.74), channel_id=1, source_target_pairs={{1,0},{2,1},{3,2},{5,4},{6,5},{7,6},{9,8},{10,9},{11,10},{13,12},{... | collective-permute-start | bytes 1572872 | tf_op jit(solution)/shard_map/ppermute | solution.py:66
  726.0 28.3 %collective-permute-start.118 = (bf16[512,512]{1,0:T(8,128)(2,1)S(1)}, bf16[512,512]{1,0:T(8,128)(2,1)S(1)}, u32[]{:S(2)}, u32[]{:S(2)}) collective-permute-start(bf16[512,512]{1,0:T(8,128)(2,1)S(1)} %copy-done.73), channel_id=1, source_target_pairs={{0,1},{1,2},{2,3},{4,5},{5,6},{6,7},{8,9},{9,10},{10,11},{12,13},{... | collective-permute-start | bytes 1572872 | tf_op jit(solution)/shard_map/ppermute | solution.py:66
  727.4 33.4 %collective-permute-start.119 = (bf16[512,512]{1,0:T(8,128)(2,1)S(1)}, bf16[512,512]{1,0:T(8,128)(2,1)S(1)}, u32[]{:S(2)}, u32[]{:S(2)}) collective-permute-start(bf16[512,512]{1,0:T(8,128)(2,1)S(1)} %copy-done.76), channel_id=1, source_target_pairs={{0,2},{1,3},{2,0},{3,1},{4,6},{5,7},{6,4},{7,5},{8,10},{9,11},{10,... | collective-permute-start | bytes 1572872 | tf_op jit(solution)/shard_map/ppermute | solution.py:66
  750.3 26.9 %collective-permute-start.121 = (bf16[2,128,1024]{2,1,0:T(8,128)(2,1)}, bf16[2,128,1024]{2,1,0:T(8,128)(2,1)}, u32[]{:S(2)}, u32[]{:S(2)}) collective-permute-start(bf16[2,128,1024]{2,1,0:T(8,128)(2,1)} %slice.389), channel_id=1, source_target_pairs={{0,8},{8,0},{16,24},{24,16},{1,9},{9,1},{17,25},{25,17},{2,10},{10... | collective-permute-start | bytes 1572872 | tf_op jit(solution)/shard_map/ppermute | solution.py:731
  752.3 24.9 %collective-permute-start.120 = (bf16[2,128,1024]{2,1,0:T(8,128)(2,1)}, bf16[2,128,1024]{2,1,0:T(8,128)(2,1)}, u32[]{:S(2)}, u32[]{:S(2)}) collective-permute-start(bf16[2,128,1024]{2,1,0:T(8,128)(2,1)} %slice.388), channel_id=1, source_target_pairs={{0,16},{8,24},{16,0},{24,8},{1,17},{9,25},{17,1},{25,9},{2,18},{10... | collective-permute-start | bytes 1572872 | tf_op jit(solution)/shard_map/ppermute | solution.py:731
  (170 other events, 1933.1 us)
Sparse Core Ops, SparseCore 0:
  115.9 55.6 all-gather.7
  178.7 87.8 all-gather.9
  565.6 69.6 all-gather.11
  639.9 127.0 all-gather.13
